TPU v7x, 32 devices: a whole 2x2x4 slice. The times are simulated.
32 devices in a mesh: gx: 8 (over z, x), gz: 4 (over y, core).
Axes of the slice: x: 2, y: 2, z: 4, core: 2. Of those that a mesh axis runs over, the one named last changes fastest.
Arguments:
- right_side: float32 [128, 128, 512], P('gx', None, 'gz'), may hold values from -6 to 6
- reaction: float32 [128, 128, 512], P('gx', None, 'gz'), may hold values from 0.25 to 2
- initial: float32 [128, 128, 512], P('gx', None, 'gz'), may hold values from -3 to 3
- coarse_inverse: float32 [4096, 4096], P(('gx', 'gz')), may hold values from -0.04 to 0.32
Outputs:
- pressure: float32 [128, 128, 512], P('gx', None, 'gz')
- residual: float32 [128, 128, 512], P('gx', None, 'gz')
All inputs are finite; a program needn't handle non-finite values.
Results may differ from a plain program's by a relative error of at most 0.0003.
Values sent between devices are 32-bit elements; how exact they have to be, the bound alone decides.
No kernel may reach another device: no remote copies, remote signals or barrier semaphores. Data moves between devices by JAX's collectives and lax.ppermute only.
A program may use at most 192 MiB of HBM per device.

v0:
```python
import jax
import jax.numpy as jnp
from jax import lax
from jax.sharding import PartitionSpec as P

LEVELS = 4
COARSE = 16


RELAX_WEIGHT = 0.8


def extended(block, sides, width):
    for axis, dim in sides:
        count = lax.axis_size(axis)
        forward = [(i, i + 1) for i in range(count - 1)]
        backward = [(target, source) for source, target in forward]
        low = lax.ppermute(
            lax.slice_in_dim(block, block.shape[dim] - width, None, axis=dim), axis, forward
        )
        high = lax.ppermute(lax.slice_in_dim(block, 0, width, axis=dim), axis, backward)
        block = jnp.concatenate([low, block, high], axis=dim)
    return block


def neighbours(padded):
    center = padded[1:-1, :, 1:-1]
    sides = jnp.pad(center, ((0, 0), (1, 1), (0, 0)))
    beside_all = padded[2:, :, 1:-1] + padded[:-2, :, 1:-1]
    beside_all = beside_all + sides[:, 2:, :] + sides[:, :-2, :]
    beside_all = beside_all + padded[1:-1, :, 2:] + padded[1:-1, :, :-2]
    return (center, beside_all)


def operate(field, coefficient):
    padded = extended(field, (("gx", 0), ("gz", 2)), 1)
    center, beside_all = neighbours(padded)
    return (6.0 + coefficient) * center - beside_all


def relax(field, source, coefficient):
    return field + RELAX_WEIGHT * (source - operate(field, coefficient)) / (6.0 + coefficient)


def block_sum(values, step_x, step_y, step_z):
    size_x, size_y, size_z = values.shape
    shaped = values.reshape(
        size_x // step_x, step_x, size_y // step_y, step_y, size_z // step_z, step_z
    )
    return shaped.sum(axis=(1, 3, 5))


def assemble(flat, count_x, count_z, grid_x, grid_y, grid_z):
    whole = flat.reshape(count_x, count_z, grid_x, grid_y, grid_z).transpose(0, 2, 3, 1, 4)
    return whole.reshape(count_x * grid_x, grid_y, count_z * grid_z)


def local(right_side, reaction, initial, coarse_inverse):
    stored = []
    field, source, coefficient = (initial, right_side, reaction)
    remainder = right_side
    spread_levels = LEVELS
    for level_no in range(spread_levels):
        margins = None
        inside = None
        field = relax(relax(field, source, coefficient), source, coefficient)
        remainder = source - operate(field, coefficient)
        stored.append((field, source, coefficient, margins, inside))
        if level_no < LEVELS - 1:
            source = 0.5 * block_sum(remainder, 2, 2, 2)
            coefficient = block_sum(coefficient, 2, 2, 2) / 8.0
            field = jnp.zeros_like(source)
    grid_x, grid_y, grid_z = source.shape
    count_x = lax.axis_size("gx")
    count_z = lax.axis_size("gz")
    step_x = grid_x * count_x // COARSE
    step_y = grid_y // COARSE
    step_z = grid_z * count_z // COARSE
    everything = lax.all_gather(remainder.reshape(-1), ("gx", "gz"), axis=0, tiled=True)
    full_grid = assemble(everything, count_x, count_z, grid_x, grid_y, grid_z)
    coarse_side = 0.25 * block_sum(full_grid, step_x, step_y, step_z)
    flat_side = coarse_side.transpose(2, 1, 0).reshape(-1)
    row_part = jnp.dot(coarse_inverse, flat_side, precision=lax.Precision.HIGHEST)
    gathered = lax.all_gather(row_part, ("gx", "gz"), axis=0, tiled=True)
    coarse_field = gathered.reshape(COARSE, COARSE, COARSE).transpose(2, 1, 0)
    index_x = (lax.axis_index("gx") * grid_x + jnp.arange(grid_x)) // step_x
    index_z = (lax.axis_index("gz") * grid_z + jnp.arange(grid_z)) // step_z
    picked = jnp.take(jnp.take(coarse_field, index_x, axis=0), index_z, axis=2)
    lifted = jnp.repeat(picked, step_y, axis=1)
    for level_no in reversed(range(spread_levels)):
        field, source, coefficient, margins, inside = stored[level_no]
        field = field + lifted
        field = relax(relax(field, source, coefficient), source, coefficient)
        if level_no > 0:
            lifted = jnp.repeat(jnp.repeat(jnp.repeat(field, 2, 0), 2, 1), 2, 2)
    return (field, source - operate(field, coefficient))


def solution(mesh):
    return jax.shard_map(
        local,
        mesh=mesh,
        in_specs=(
            P("gx", None, "gz"),
            P("gx", None, "gz"),
            P("gx", None, "gz"),
            P(("gx", "gz"), None),
        ),
        out_specs=(P("gx", None, "gz"), P("gx", None, "gz")),
        check_vma=False,
    )
```

profile of v0, /device:TPU:0, one launch (start us, length us, event | category | flops | bytes accessed | tf_op | source)
XLA Modules:
  0.0 722.2 jit_solution(18204280692965042512)
XLA Ops:
  3.2 5.5 collective-permute-start.1
  12.0 3.0 collective-permute-start.3
  16.8 2.6 copy.96
  19.4 5.4 fusion.8
  26.2 5.3 collective-permute-start.5
  32.2 2.6 collective-permute-done.5
  36.6 3.6 collective-permute-start.7
  42.1 5.6 collective-permute-start.13
  47.8 69.2 %reshape.152 = f32[8,2,64,2,64,2]{5,4,3,2,1,0:T(8,128)} reshape(f32[16,128,128]{2,1,0:T(8,128)} %param.5) | data formatting | bytes 2097152 | tf_op jit(solution)/shard_map/reshape | solution.py:47
  117.0 20.8 %reduce_sum.64 = f32[8,64,64]{2,1,0:T(8,128)S(1)} reduce(f32[8,2,64,2,64,2]{5,4,3,2,1,0:T(8,128)} %reshape.152, f32[]{:T(128)} %constant.42.clone.1), dimensions={1,3,5}, to_apply=%region_1.2 | reduce | flops 229376 | bytes 1179652 | tf_op jit(solution)/shard_map/reduce_sum | solution.py:50
  137.8 5.4 fusion.17
  144.8 5.2 collective-permute-start.9
  153.7 3.0 collective-permute-start.11
  158.9 4.5 collective-permute-start.15
  165.2 2.6 copy.108
  167.8 69.2 %reshape.151 = f32[8,2,64,2,64,2]{5,4,3,2,1,0:T(8,128)} reshape(f32[16,128,128]{2,1,0:T(8,128)} %copy.108) | data formatting | bytes 2097152 | tf_op jit(solution)/shard_map/reshape | solution.py:47
  237.0 21.5 %reduce_sum.63 = f32[8,64,64]{2,1,0:T(8,128)} reduce(f32[8,2,64,2,64,2]{5,4,3,2,1,0:T(8,128)} %reshape.151, f32[]{:T(128)} %constant.42.clone.1), dimensions={1,3,5}, to_apply=%region_0.1 | reduce | flops 229376 | bytes 1179652 | tf_op jit(solution)/shard_map/reduce_sum | solution.py:50
  261.8 5.0 collective-permute-start.17
  270.1 3.1 collective-permute-start.19
  274.4 5.3 collective-permute-start.25
  281.5 5.9 collective-permute-start.21
  290.5 3.1 collective-permute-start.23
  295.6 4.3 collective-permute-start.27
  300.9 10.9 %reshape.153 = f32[4,2,32,2,32,2]{5,4,3,2,1,0:T(8,128)} reshape(f32[8,64,64]{2,1,0:T(8,128)} %get-tuple-element.49) | data formatting | bytes 262144 | tf_op jit(solution)/shard_map/reshape | solution.py:47
  311.8 4.1 reduce_sum.65
  315.9 10.9 %div.100 = f32[4,2,32,2,32,2]{5,4,3,2,1,0:T(8,128)} reshape(f32[8,64,64]{2,1,0:T(8,128)} %get-tuple-element.48) | data formatting | bytes 262144 | tf_op jit(solution)/shard_map/div | solution.py:71
  326.8 4.1 reduce_sum.66
  334.6 5.8 collective-permute-start.29
  342.3 5.5 collective-permute-start.37
  350.0 3.3 collective-permute-start.31
  358.0 5.2 collective-permute-start.33
  366.5 4.2 collective-permute-start.35
  374.0 6.3 collective-permute-start.39
  382.1 2.4 reshape.154
  387.3 2.4 div.105
  395.4 5.4 collective-permute-start.41
  403.5 3.0 collective-permute-start.43
  409.5 5.8 collective-permute-start.45
  418.0 3.1 collective-permute-start.47
  426.2 52.9 %all-gather = f32[32,1,512]{2,1,0:T(1,128)} all-gather(f32[1,1,512]{2,1,0:T(1,128)} %reshape.184), channel_id=1, replica_groups=mesh['gx'=8,'gz'=4] {'gx','gz'}, dimensions={0}, use_global_device_ids=true | all-gather | bytes 67584 | tf_op jit(solution)/shard_map/all_gather | solution.py:79
  491.5 2.4 convolution_bitcast_fusion
  493.9 37.7 %all-gather.1 = f32[32,1,128]{2,1,0:T(1,128)} all-gather(f32[1,1,128]{2,1,0:T(1,128)S(1)} %convolution_bitcast_fusion), channel_id=1, replica_groups=mesh['gx'=8,'gz'=4] {'gx','gz'}, dimensions={0}, use_global_device_ids=true | all-gather | bytes 16896 | tf_op jit(solution)/shard_map/all_gather | solution.py:84
  546.4 4.5 collective-permute-start.49
  553.6 3.0 collective-permute-start.51
  559.6 4.8 collective-permute-start.53
  567.1 3.3 collective-permute-start.55
  580.5 5.4 collective-permute-start.57
  588.8 4.3 collective-permute-start.59
  595.5 5.7 collective-permute-start.61
  604.0 5.5 collective-permute-start.63
  617.4 5.7 collective-permute-start.65
  626.2 5.7 collective-permute-start.67
  634.8 5.7 collective-permute-start.69
  643.6 7.7 %collective-permute-start.71 = (f32[10,64,1]{2,1,0:T(8,128)S(1)}, f32[10,64,1]{2,1,0:T(8,128)S(1)}, u32[]{:S(2)}, u32[]{:S(2)}) collective-permute-start(f32[10,64,1]{2,1,0:T(8,128)S(1)} %get-tuple-element.35), channel_id=1, source_target_pairs={{0,1},{1,2},{2,3},{4,5},{5,6},{6,7},{8,9},{9,10},{10,11},{12,13},{... | collective-permute-start | bytes 7688 | tf_op jit(solution)/shard_map/ppermute | solution.py:18
  654.3 2.5 copy.123
  659.8 5.8 collective-permute-start.73
  668.8 7.9 %collective-permute-start.75 = (f32[18,128,1]{1,0,2:T(8,128)S(1)}, f32[18,128,1]{1,0,2:T(8,128)S(1)}, u32[]{:S(2)}, u32[]{:S(2)}) collective-permute-start(f32[18,128,1]{1,0,2:T(8,128)S(1)} %get-tuple-element.15), channel_id=1, source_target_pairs={{0,1},{1,2},{2,3},{4,5},{5,6},{6,7},{8,9},{9,10},{10,11},{12,13},{... | collective-permute-start | bytes 27656 | tf_op jit(solution)/shard_map/ppermute | solution.py:18
  679.8 5.6 collective-permute-start.77
  688.6 5.2 collective-permute-start.79
  696.9 5.6 collective-permute-start.81
  705.8 5.0 collective-permute-start.83
  710.8 2.6 copy.127
  713.3 6.3 fusion.47
  719.6 2.5 copy.128
  (282 shorter events, 172.4 us)
Async XLA Ops:
  1.8 8.6 %collective-permute-start = (f32[1,128,128]{1,0,2:T(1,128)S(1)}, f32[1,128,128]{1,0,2:T(1,128)S(1)}, u32[]{:S(2)}, u32[]{:S(2)}) collective-permute-start(f32[1,128,128]{1,0,2:T(1,128)S(1)} %copy.98), channel_id=1, source_target_pairs={{4,0},{8,4},{12,8},{16,12},{20,16},{24,20},{28,24},{5,1},{9,5},{13... | collective-permute-start | bytes 196616 | tf_op jit(solution)/shard_map/ppermute | solution.py:21
  3.2 7.5 %collective-permute-start.1 = (f32[1,128,128]{1,0,2:T(1,128)S(1)}, f32[1,128,128]{1,0,2:T(1,128)S(1)}, u32[]{:S(2)}, u32[]{:S(2)}) collective-permute-start(f32[1,128,128]{1,0,2:T(1,128)S(1)} %copy.100), channel_id=1, source_target_pairs={{0,4},{4,8},{8,12},{12,16},{16,20},{20,24},{24,28},{1,5},{5,9},{9,... | collective-permute-start | bytes 196616 | tf_op jit(solution)/shard_map/ppermute | solution.py:18
  10.7 8.7 %collective-permute-start.2 = (f32[18,128,1]{1,0,2:T(8,128)S(1)}, f32[18,128,1]{1,0,2:T(8,128)S(1)}, u32[]{:S(2)}, u32[]{:S(2)}) collective-permute-start(f32[18,128,1]{1,0,2:T(8,128)S(1)} %get-tuple-element.20), channel_id=1, source_target_pairs={{1,0},{2,1},{3,2},{5,4},{6,5},{7,6},{9,8},{10,9},{11,10},{13,12},{... | collective-permute-start | bytes 27656 | tf_op jit(solution)/shard_map/ppermute | solution.py:21
  12.0 7.4 %collective-permute-start.3 = (f32[18,128,1]{1,0,2:T(8,128)S(1)}, f32[18,128,1]{1,0,2:T(8,128)S(1)}, u32[]{:S(2)}, u32[]{:S(2)}) collective-permute-start(f32[18,128,1]{1,0,2:T(8,128)S(1)} %get-tuple-element.21), channel_id=1, source_target_pairs={{0,1},{1,2},{2,3},{4,5},{5,6},{6,7},{8,9},{9,10},{10,11},{12,13},{... | collective-permute-start | bytes 27656 | tf_op jit(solution)/shard_map/ppermute | solution.py:18
  24.9 7.2 %collective-permute-start.4 = (f32[1,128,128]{1,0,2:T(1,128)S(1)}, f32[1,128,128]{1,0,2:T(1,128)S(1)}, u32[]{:S(2)}, u32[]{:S(2)}) collective-permute-start(f32[1,128,128]{1,0,2:T(1,128)S(1)} %get-tuple-element.31), channel_id=1, source_target_pairs={{4,0},{8,4},{12,8},{16,12},{20,16},{24,20},{28,24},{5,1},{9,5},{13... | collective-permute-start | bytes 196616 | tf_op jit(solution)/shard_map/ppermute | solution.py:21
  26.2 8.5 %collective-permute-start.5 = (f32[1,128,128]{1,0,2:T(1,128)S(1)}, f32[1,128,128]{1,0,2:T(1,128)S(1)}, u32[]{:S(2)}, u32[]{:S(2)}) collective-permute-start(f32[1,128,128]{1,0,2:T(1,128)S(1)} %get-tuple-element.30), channel_id=1, source_target_pairs={{0,4},{4,8},{8,12},{12,16},{16,20},{20,24},{24,28},{1,5},{5,9},{9,... | collective-permute-start | bytes 196616 | tf_op jit(solution)/shard_map/ppermute | solution.py:18
  35.3 102.4 %collective-permute-start.6 = (f32[18,128,1]{1,0,2:T(8,128)}, f32[18,128,1]{1,0,2:T(8,128)}, u32[]{:S(2)}, u32[]{:S(2)}) collective-permute-start(f32[18,128,1]{1,0,2:T(8,128)} %get-tuple-element.18), channel_id=1, source_target_pairs={{1,0},{2,1},{3,2},{5,4},{6,5},{7,6},{9,8},{10,9},{11,10},{13,12},{... | collective-permute-start | bytes 27656 | tf_op jit(solution)/shard_map/ppermute | solution.py:21
  36.6 101.2 %collective-permute-start.7 = (f32[18,128,1]{1,0,2:T(8,128)S(1)}, f32[18,128,1]{1,0,2:T(8,128)}, u32[]{:S(2)}, u32[]{:S(2)}) collective-permute-start(f32[18,128,1]{1,0,2:T(8,128)S(1)} %get-tuple-element.19), channel_id=1, source_target_pairs={{0,1},{1,2},{2,3},{4,5},{5,6},{6,7},{8,9},{9,10},{10,11},{12,13},{... | collective-permute-start | bytes 27656 | tf_op jit(solution)/shard_map/ppermute | solution.py:18
  40.9 109.1 %collective-permute-start.12 = (f32[1,64,64]{2,1,0:T(8,128)}, f32[1,64,64]{2,1,0:T(8,128)}, u32[]{:S(2)}, u32[]{:S(2)}) collective-permute-start(f32[1,64,64]{2,1,0:T(8,128)} %broadcast.286), channel_id=1, source_target_pairs={{4,0},{8,4},{12,8},{16,12},{20,16},{24,20},{28,24},{5,1},{9,5},{13... | collective-permute-start | bytes 49160 | tf_op jit(solution)/shard_map/ppermute | solution.py:21
  42.1 107.9 %collective-permute-start.13 = (f32[1,64,64]{2,1,0:T(8,128)}, f32[1,64,64]{2,1,0:T(8,128)}, u32[]{:S(2)}, u32[]{:S(2)}) collective-permute-start(f32[1,64,64]{2,1,0:T(8,128)} %broadcast.286), channel_id=1, source_target_pairs={{0,4},{4,8},{8,12},{12,16},{16,20},{20,24},{24,28},{1,5},{5,9},{9,... | collective-permute-start | bytes 49160 | tf_op jit(solution)/shard_map/ppermute | solution.py:18
  143.3 8.2 %collective-permute-start.8 = (f32[1,128,128]{1,0,2:T(1,128)S(1)}, f32[1,128,128]{1,0,2:T(1,128)S(1)}, u32[]{:S(2)}, u32[]{:S(2)}) collective-permute-start(f32[1,128,128]{1,0,2:T(1,128)S(1)} %get-tuple-element.29), channel_id=1, source_target_pairs={{4,0},{8,4},{12,8},{16,12},{20,16},{24,20},{28,24},{5,1},{9,5},{13... | collective-permute-start | bytes 196616 | tf_op jit(solution)/shard_map/ppermute | solution.py:21
  144.8 7.6 %collective-permute-start.9 = (f32[1,128,128]{1,0,2:T(1,128)S(1)}, f32[1,128,128]{1,0,2:T(1,128)S(1)}, u32[]{:S(2)}, u32[]{:S(2)}) collective-permute-start(f32[1,128,128]{1,0,2:T(1,128)S(1)} %get-tuple-element.28), channel_id=1, source_target_pairs={{0,4},{4,8},{8,12},{12,16},{16,20},{20,24},{24,28},{1,5},{5,9},{9,... | collective-permute-start | bytes 196616 | tf_op jit(solution)/shard_map/ppermute | solution.py:18
  152.4 11.1 %collective-permute-start.10 = (f32[18,128,1]{1,0,2:T(8,128)S(1)}, f32[18,128,1]{1,0,2:T(8,128)S(1)}, u32[]{:S(2)}, u32[]{:S(2)}) collective-permute-start(f32[18,128,1]{1,0,2:T(8,128)S(1)} %get-tuple-element.16), channel_id=1, source_target_pairs={{1,0},{2,1},{3,2},{5,4},{6,5},{7,6},{9,8},{10,9},{11,10},{13,12},{... | collective-permute-start | bytes 27656 | tf_op jit(solution)/shard_map/ppermute | solution.py:21
  153.7 9.8 %collective-permute-start.11 = (f32[18,128,1]{1,0,2:T(8,128)S(1)}, f32[18,128,1]{1,0,2:T(8,128)S(1)}, u32[]{:S(2)}, u32[]{:S(2)}) collective-permute-start(f32[18,128,1]{1,0,2:T(8,128)S(1)} %get-tuple-element.17), channel_id=1, source_target_pairs={{0,1},{1,2},{2,3},{4,5},{5,6},{6,7},{8,9},{9,10},{10,11},{12,13},{... | collective-permute-start | bytes 27656 | tf_op jit(solution)/shard_map/ppermute | solution.py:18
  157.6 100.8 %collective-permute-start.14 = (f32[10,64,1]{2,1,0:T(8,128)}, f32[10,64,1]{2,1,0:T(8,128)}, u32[]{:S(2)}, u32[]{:S(2)}) collective-permute-start(f32[10,64,1]{2,1,0:T(8,128)} %get-tuple-element.42), channel_id=1, source_target_pairs={{1,0},{2,1},{3,2},{5,4},{6,5},{7,6},{9,8},{10,9},{11,10},{13,12},{... | collective-permute-start | bytes 7688 | tf_op jit(solution)/shard_map/ppermute | solution.py:21
  158.9 99.6 %collective-permute-start.15 = (f32[10,64,1]{2,1,0:T(8,128)}, f32[10,64,1]{2,1,0:T(8,128)}, u32[]{:S(2)}, u32[]{:S(2)}) collective-permute-start(f32[10,64,1]{2,1,0:T(8,128)} %get-tuple-element.43), channel_id=1, source_target_pairs={{0,1},{1,2},{2,3},{4,5},{5,6},{6,7},{8,9},{9,10},{10,11},{12,13},{... | collective-permute-start | bytes 7688 | tf_op jit(solution)/shard_map/ppermute | solution.py:18
  261.8 6.7 collective-permute-start.17
  268.8 11.0 %collective-permute-start.18 = (f32[10,64,1]{2,1,0:T(8,128)S(1)}, f32[10,64,1]{2,1,0:T(8,128)S(1)}, u32[]{:S(2)}, u32[]{:S(2)}) collective-permute-start(f32[10,64,1]{2,1,0:T(8,128)S(1)} %get-tuple-element.40), channel_id=1, source_target_pairs={{1,0},{2,1},{3,2},{5,4},{6,5},{7,6},{9,8},{10,9},{11,10},{13,12},{... | collective-permute-start | bytes 7688 | tf_op jit(solution)/shard_map/ppermute | solution.py:21
  270.1 9.7 %collective-permute-start.19 = (f32[10,64,1]{2,1,0:T(8,128)S(1)}, f32[10,64,1]{2,1,0:T(8,128)S(1)}, u32[]{:S(2)}, u32[]{:S(2)}) collective-permute-start(f32[10,64,1]{2,1,0:T(8,128)S(1)} %get-tuple-element.41), channel_id=1, source_target_pairs={{0,1},{1,2},{2,3},{4,5},{5,6},{6,7},{8,9},{9,10},{10,11},{12,13},{... | collective-permute-start | bytes 7688 | tf_op jit(solution)/shard_map/ppermute | solution.py:18
  273.1 14.2 %collective-permute-start.24 = (f32[1,32,32]{2,1,0:T(8,128)S(1)}, f32[1,32,32]{2,1,0:T(8,128)S(1)}, u32[]{:S(2)}, u32[]{:S(2)}) collective-permute-start(f32[1,32,32]{2,1,0:T(8,128)S(1)} %broadcast.289), channel_id=1, source_target_pairs={{4,0},{8,4},{12,8},{16,12},{20,16},{24,20},{28,24},{5,1},{9,5},{13... | collective-permute-start | bytes 12296 | tf_op jit(solution)/shard_map/ppermute | solution.py:21
  274.4 13.0 %collective-permute-start.25 = (f32[1,32,32]{2,1,0:T(8,128)S(1)}, f32[1,32,32]{2,1,0:T(8,128)S(1)}, u32[]{:S(2)}, u32[]{:S(2)}) collective-permute-start(f32[1,32,32]{2,1,0:T(8,128)S(1)} %broadcast.289), channel_id=1, source_target_pairs={{0,4},{4,8},{8,12},{12,16},{16,20},{20,24},{24,28},{1,5},{5,9},{9,... | collective-permute-start | bytes 12296 | tf_op jit(solution)/shard_map/ppermute | solution.py:18
  280.2 7.4 %collective-permute-start.20 = (f32[1,64,64]{2,1,0:T(8,128)S(1)}, f32[1,64,64]{2,1,0:T(8,128)S(1)}, u32[]{:S(2)}, u32[]{:S(2)}) collective-permute-start(f32[1,64,64]{2,1,0:T(8,128)S(1)} %get-tuple-element.51), channel_id=1, source_target_pairs={{4,0},{8,4},{12,8},{16,12},{20,16},{24,20},{28,24},{5,1},{9,5},{13... | collective-permute-start | bytes 49160 | tf_op jit(solution)/shard_map/ppermute | solution.py:21
  281.5 7.5 %collective-permute-start.21 = (f32[1,64,64]{2,1,0:T(8,128)S(1)}, f32[1,64,64]{2,1,0:T(8,128)S(1)}, u32[]{:S(2)}, u32[]{:S(2)}) collective-permute-start(f32[1,64,64]{2,1,0:T(8,128)S(1)} %get-tuple-element.50), channel_id=1, source_target_pairs={{0,4},{4,8},{8,12},{12,16},{16,20},{20,24},{24,28},{1,5},{5,9},{9,... | collective-permute-start | bytes 49160 | tf_op jit(solution)/shard_map/ppermute | solution.py:18
  289.2 10.7 %collective-permute-start.22 = (f32[10,64,1]{2,1,0:T(8,128)S(1)}, f32[10,64,1]{2,1,0:T(8,128)S(1)}, u32[]{:S(2)}, u32[]{:S(2)}) collective-permute-start(f32[10,64,1]{2,1,0:T(8,128)S(1)} %get-tuple-element.38), channel_id=1, source_target_pairs={{1,0},{2,1},{3,2},{5,4},{6,5},{7,6},{9,8},{10,9},{11,10},{13,12},{... | collective-permute-start | bytes 7688 | tf_op jit(solution)/shard_map/ppermute | solution.py:21
  290.5 9.4 %collective-permute-start.23 = (f32[10,64,1]{2,1,0:T(8,128)S(1)}, f32[10,64,1]{2,1,0:T(8,128)S(1)}, u32[]{:S(2)}, u32[]{:S(2)}) collective-permute-start(f32[10,64,1]{2,1,0:T(8,128)S(1)} %get-tuple-element.39), channel_id=1, source_target_pairs={{0,1},{1,2},{2,3},{4,5},{5,6},{6,7},{8,9},{9,10},{10,11},{12,13},{... | collective-permute-start | bytes 7688 | tf_op jit(solution)/shard_map/ppermute | solution.py:18
  294.3 36.6 %collective-permute-start.26 = (f32[6,32,1]{2,1,0:T(8,128)}, f32[6,32,1]{2,1,0:T(8,128)}, u32[]{:S(2)}, u32[]{:S(2)}) collective-permute-start(f32[6,32,1]{2,1,0:T(8,128)} %get-tuple-element.62), channel_id=1, source_target_pairs={{1,0},{2,1},{3,2},{5,4},{6,5},{7,6},{9,8},{10,9},{11,10},{13,12},{... | collective-permute-start | bytes 2312 | tf_op jit(solution)/shard_map/ppermute | solution.py:21
  295.6 35.3 %collective-permute-start.27 = (f32[6,32,1]{2,1,0:T(8,128)}, f32[6,32,1]{2,1,0:T(8,128)}, u32[]{:S(2)}, u32[]{:S(2)}) collective-permute-start(f32[6,32,1]{2,1,0:T(8,128)} %get-tuple-element.63), channel_id=1, source_target_pairs={{0,1},{1,2},{2,3},{4,5},{5,6},{6,7},{8,9},{9,10},{10,11},{12,13},{... | collective-permute-start | bytes 2312 | tf_op jit(solution)/shard_map/ppermute | solution.py:18
  333.3 14.4 %collective-permute-start.28 = (f32[1,32,32]{2,1,0:T(8,128)}, f32[1,32,32]{2,1,0:T(8,128)S(1)}, u32[]{:S(2)}, u32[]{:S(2)}) collective-permute-start(f32[1,32,32]{2,1,0:T(8,128)} %get-tuple-element.73), channel_id=1, source_target_pairs={{4,0},{8,4},{12,8},{16,12},{20,16},{24,20},{28,24},{5,1},{9,5},{13... | collective-permute-start | bytes 12296 | tf_op jit(solution)/shard_map/ppermute | solution.py:21
  334.6 13.1 %collective-permute-start.29 = (f32[1,32,32]{2,1,0:T(8,128)}, f32[1,32,32]{2,1,0:T(8,128)}, u32[]{:S(2)}, u32[]{:S(2)}) collective-permute-start(f32[1,32,32]{2,1,0:T(8,128)} %get-tuple-element.72), channel_id=1, source_target_pairs={{0,4},{4,8},{8,12},{12,16},{16,20},{20,24},{24,28},{1,5},{5,9},{9,... | collective-permute-start | bytes 12296 | tf_op jit(solution)/shard_map/ppermute | solution.py:18
  341.0 29.7 %collective-permute-start.36 = (f32[1,16,16]{1,0,2:T(1,128)}, f32[1,16,16]{1,0,2:T(1,128)}, u32[]{:S(2)}, u32[]{:S(2)}) collective-permute-start(f32[1,16,16]{1,0,2:T(1,128)} %broadcast.292), channel_id=1, source_target_pairs={{4,0},{8,4},{12,8},{16,12},{20,16},{24,20},{28,24},{5,1},{9,5},{13... | collective-permute-start | bytes 3080 | tf_op jit(solution)/shard_map/ppermute | solution.py:21
  342.3 28.5 %collective-permute-start.37 = (f32[1,16,16]{1,0,2:T(1,128)}, f32[1,16,16]{1,0,2:T(1,128)}, u32[]{:S(2)}, u32[]{:S(2)}) collective-permute-start(f32[1,16,16]{1,0,2:T(1,128)} %broadcast.292), channel_id=1, source_target_pairs={{0,4},{4,8},{8,12},{12,16},{16,20},{20,24},{24,28},{1,5},{5,9},{9,... | collective-permute-start | bytes 3080 | tf_op jit(solution)/shard_map/ppermute | solution.py:18
  356.7 7.1 collective-permute-start.32
  365.2 15.0 %collective-permute-start.34 = (f32[6,32,1]{2,1,0:T(8,128)S(1)}, f32[6,32,1]{2,1,0:T(8,128)S(1)}, u32[]{:S(2)}, u32[]{:S(2)}) collective-permute-start(f32[6,32,1]{2,1,0:T(8,128)S(1)} %get-tuple-element.58), channel_id=1, source_target_pairs={{1,0},{2,1},{3,2},{5,4},{6,5},{7,6},{9,8},{10,9},{11,10},{13,12},{... | collective-permute-start | bytes 2312 | tf_op jit(solution)/shard_map/ppermute | solution.py:21
  366.5 13.7 %collective-permute-start.35 = (f32[6,32,1]{2,1,0:T(8,128)S(1)}, f32[6,32,1]{2,1,0:T(8,128)S(1)}, u32[]{:S(2)}, u32[]{:S(2)}) collective-permute-start(f32[6,32,1]{2,1,0:T(8,128)S(1)} %get-tuple-element.59), channel_id=1, source_target_pairs={{0,1},{1,2},{2,3},{4,5},{5,6},{6,7},{8,9},{9,10},{10,11},{12,13},{... | collective-permute-start | bytes 2312 | tf_op jit(solution)/shard_map/ppermute | solution.py:18
  372.7 20.4 %collective-permute-start.38 = (f32[4,16,1]{1,0,2:T(4,128)}, f32[4,16,1]{1,0,2:T(4,128)}, u32[]{:S(2)}, u32[]{:S(2)}) collective-permute-start(f32[4,16,1]{1,0,2:T(4,128)} %get-tuple-element.82), channel_id=1, source_target_pairs={{1,0},{2,1},{3,2},{5,4},{6,5},{7,6},{9,8},{10,9},{11,10},{13,12},{... | collective-permute-start | bytes 776 | tf_op jit(solution)/shard_map/ppermute | solution.py:21
  374.0 19.1 %collective-permute-start.39 = (f32[4,16,1]{1,0,2:T(4,128)}, f32[4,16,1]{1,0,2:T(4,128)}, u32[]{:S(2)}, u32[]{:S(2)}) collective-permute-start(f32[4,16,1]{1,0,2:T(4,128)} %get-tuple-element.83), channel_id=1, source_target_pairs={{0,1},{1,2},{2,3},{4,5},{5,6},{6,7},{8,9},{9,10},{10,11},{12,13},{... | collective-permute-start | bytes 776 | tf_op jit(solution)/shard_map/ppermute | solution.py:18
  394.1 6.8 collective-permute-start.40
  395.4 6.8 collective-permute-start.41
  408.2 7.7 %collective-permute-start.44 = (f32[1,16,16]{1,0,2:T(1,128)S(1)}, f32[1,16,16]{1,0,2:T(1,128)S(1)}, u32[]{:S(2)}, u32[]{:S(2)}) collective-permute-start(f32[1,16,16]{1,0,2:T(1,128)S(1)} %get-tuple-element.89), channel_id=1, source_target_pairs={{4,0},{8,4},{12,8},{16,12},{20,16},{24,20},{28,24},{5,1},{9,5},{13... | collective-permute-start | bytes 3080 | tf_op jit(solution)/shard_map/ppermute | solution.py:21
  409.5 7.2 collective-permute-start.45
  579.2 6.8 collective-permute-start.56
  580.5 6.9 collective-permute-start.57
  594.2 7.0 collective-permute-start.60
  595.5 7.2 collective-permute-start.61
  602.7 6.8 collective-permute-start.62
  616.1 7.0 collective-permute-start.64
  617.4 7.3 %collective-permute-start.65 = (f32[1,64,64]{2,1,0:T(8,128)S(1)}, f32[1,64,64]{2,1,0:T(8,128)S(1)}, u32[]{:S(2)}, u32[]{:S(2)}) collective-permute-start(f32[1,64,64]{2,1,0:T(8,128)S(1)} %get-tuple-element.46), channel_id=1, source_target_pairs={{0,4},{4,8},{8,12},{12,16},{16,20},{20,24},{24,28},{1,5},{5,9},{9,... | collective-permute-start | bytes 49160 | tf_op jit(solution)/shard_map/ppermute | solution.py:18
  625.0 7.0 collective-permute-start.66
  626.2 6.9 collective-permute-start.67
  633.5 7.0 collective-permute-start.68
  634.8 7.3 %collective-permute-start.69 = (f32[1,64,64]{2,1,0:T(8,128)S(1)}, f32[1,64,64]{2,1,0:T(8,128)S(1)}, u32[]{:S(2)}, u32[]{:S(2)}) collective-permute-start(f32[1,64,64]{2,1,0:T(8,128)S(1)} %get-tuple-element.44), channel_id=1, source_target_pairs={{0,4},{4,8},{8,12},{12,16},{16,20},{20,24},{24,28},{1,5},{5,9},{9,... | collective-permute-start | bytes 49160 | tf_op jit(solution)/shard_map/ppermute | solution.py:18
  642.3 9.0 %collective-permute-start.70 = (f32[10,64,1]{2,1,0:T(8,128)S(1)}, f32[10,64,1]{2,1,0:T(8,128)S(1)}, u32[]{:S(2)}, u32[]{:S(2)}) collective-permute-start(f32[10,64,1]{2,1,0:T(8,128)S(1)} %get-tuple-element.34), channel_id=1, source_target_pairs={{1,0},{2,1},{3,2},{5,4},{6,5},{7,6},{9,8},{10,9},{11,10},{13,12},{... | collective-permute-start | bytes 7688 | tf_op jit(solution)/shard_map/ppermute | solution.py:21
  643.6 8.9 %collective-permute-start.71 = (f32[10,64,1]{2,1,0:T(8,128)S(1)}, f32[10,64,1]{2,1,0:T(8,128)S(1)}, u32[]{:S(2)}, u32[]{:S(2)}) collective-permute-start(f32[10,64,1]{2,1,0:T(8,128)S(1)} %get-tuple-element.35), channel_id=1, source_target_pairs={{0,1},{1,2},{2,3},{4,5},{5,6},{6,7},{8,9},{9,10},{10,11},{12,13},{... | collective-permute-start | bytes 7688 | tf_op jit(solution)/shard_map/ppermute | solution.py:18
  658.5 7.4 %collective-permute-start.72 = (f32[1,128,128]{1,0,2:T(1,128)S(1)}, f32[1,128,128]{1,0,2:T(1,128)S(1)}, u32[]{:S(2)}, u32[]{:S(2)}) collective-permute-start(f32[1,128,128]{1,0,2:T(1,128)S(1)} %get-tuple-element.27), channel_id=1, source_target_pairs={{4,0},{8,4},{12,8},{16,12},{20,16},{24,20},{28,24},{5,1},{9,5},{13... | collective-permute-start | bytes 196616 | tf_op jit(solution)/shard_map/ppermute | solution.py:21
  659.8 7.6 %collective-permute-start.73 = (f32[1,128,128]{1,0,2:T(1,128)S(1)}, f32[1,128,128]{1,0,2:T(1,128)S(1)}, u32[]{:S(2)}, u32[]{:S(2)}) collective-permute-start(f32[1,128,128]{1,0,2:T(1,128)S(1)} %get-tuple-element.26), channel_id=1, source_target_pairs={{0,4},{4,8},{8,12},{12,16},{16,20},{20,24},{24,28},{1,5},{5,9},{9,... | collective-permute-start | bytes 196616 | tf_op jit(solution)/shard_map/ppermute | solution.py:18
  667.5 9.2 %collective-permute-start.74 = (f32[18,128,1]{1,0,2:T(8,128)S(1)}, f32[18,128,1]{1,0,2:T(8,128)S(1)}, u32[]{:S(2)}, u32[]{:S(2)}) collective-permute-start(f32[18,128,1]{1,0,2:T(8,128)S(1)} %get-tuple-element.14), channel_id=1, source_target_pairs={{1,0},{2,1},{3,2},{5,4},{6,5},{7,6},{9,8},{10,9},{11,10},{13,12},{... | collective-permute-start | bytes 27656 | tf_op jit(solution)/shard_map/ppermute | solution.py:21
  668.8 8.7 %collective-permute-start.75 = (f32[18,128,1]{1,0,2:T(8,128)S(1)}, f32[18,128,1]{1,0,2:T(8,128)S(1)}, u32[]{:S(2)}, u32[]{:S(2)}) collective-permute-start(f32[18,128,1]{1,0,2:T(8,128)S(1)} %get-tuple-element.15), channel_id=1, source_target_pairs={{0,1},{1,2},{2,3},{4,5},{5,6},{6,7},{8,9},{9,10},{10,11},{12,13},{... | collective-permute-start | bytes 27656 | tf_op jit(solution)/shard_map/ppermute | solution.py:18
  678.5 7.2 %collective-permute-start.76 = (f32[1,128,128]{1,0,2:T(1,128)S(1)}, f32[1,128,128]{1,0,2:T(1,128)S(1)}, u32[]{:S(2)}, u32[]{:S(2)}) collective-permute-start(f32[1,128,128]{1,0,2:T(1,128)S(1)} %get-tuple-element.25), channel_id=1, source_target_pairs={{4,0},{8,4},{12,8},{16,12},{20,16},{24,20},{28,24},{5,1},{9,5},{13... | collective-permute-start | bytes 196616 | tf_op jit(solution)/shard_map/ppermute | solution.py:21
  679.8 7.5 %collective-permute-start.77 = (f32[1,128,128]{1,0,2:T(1,128)S(1)}, f32[1,128,128]{1,0,2:T(1,128)S(1)}, u32[]{:S(2)}, u32[]{:S(2)}) collective-permute-start(f32[1,128,128]{1,0,2:T(1,128)S(1)} %get-tuple-element.24), channel_id=1, source_target_pairs={{0,4},{4,8},{8,12},{12,16},{16,20},{20,24},{24,28},{1,5},{5,9},{9,... | collective-permute-start | bytes 196616 | tf_op jit(solution)/shard_map/ppermute | solution.py:18
  687.3 6.5 collective-permute-start.78
  695.6 7.2 %collective-permute-start.80 = (f32[1,128,128]{1,0,2:T(1,128)S(1)}, f32[1,128,128]{1,0,2:T(1,128)S(1)}, u32[]{:S(2)}, u32[]{:S(2)}) collective-permute-start(f32[1,128,128]{1,0,2:T(1,128)S(1)} %get-tuple-element.23), channel_id=1, source_target_pairs={{4,0},{8,4},{12,8},{16,12},{20,16},{24,20},{28,24},{5,1},{9,5},{13... | collective-permute-start | bytes 196616 | tf_op jit(solution)/shard_map/ppermute | solution.py:21
  696.9 7.5 %collective-permute-start.81 = (f32[1,128,128]{1,0,2:T(1,128)S(1)}, f32[1,128,128]{1,0,2:T(1,128)S(1)}, u32[]{:S(2)}, u32[]{:S(2)}) collective-permute-start(f32[1,128,128]{1,0,2:T(1,128)S(1)} %get-tuple-element.22), channel_id=1, source_target_pairs={{0,4},{4,8},{8,12},{12,16},{16,20},{20,24},{24,28},{1,5},{5,9},{9,... | collective-permute-start | bytes 196616 | tf_op jit(solution)/shard_map/ppermute | solution.py:18
  704.5 8.9 %collective-permute-start.82 = (f32[18,128,1]{1,0,2:T(8,128)S(1)}, f32[18,128,1]{1,0,2:T(8,128)S(1)}, u32[]{:S(2)}, u32[]{:S(2)}) collective-permute-start(f32[18,128,1]{1,0,2:T(8,128)S(1)} %get-tuple-element.10), channel_id=1, source_target_pairs={{1,0},{2,1},{3,2},{5,4},{6,5},{7,6},{9,8},{10,9},{11,10},{13,12},{... | collective-permute-start | bytes 27656 | tf_op jit(solution)/shard_map/ppermute | solution.py:21
  705.8 7.6 %collective-permute-start.83 = (f32[18,128,1]{1,0,2:T(8,128)S(1)}, f32[18,128,1]{1,0,2:T(8,128)S(1)}, u32[]{:S(2)}, u32[]{:S(2)}) collective-permute-start(f32[18,128,1]{1,0,2:T(8,128)S(1)} %get-tuple-element.11), channel_id=1, source_target_pairs={{0,1},{1,2},{2,3},{4,5},{5,6},{6,7},{8,9},{9,10},{10,11},{12,13},{... | collective-permute-start | bytes 27656 | tf_op jit(solution)/shard_map/ppermute | solution.py:18
  (37 other events, 766.2 us)
where the time goes:
time: 734 us; the launch traced here: 722 us
  starting transfers between devices  261 us (36%)
  local copies, waits for them, and re-layouts  224 us (31%)
  other arithmetic  109 us (15%)
  blocking collectives  90.6 us (12%)
  waiting for transfers between devices  32.6 us (4%)
    ppermute x42, starting transfers between devices, extended(): lax.ppermute(lax.slice_in_dim(block, block.shape[dim] - width, None, axis...  207 us
    reshape x4, local copies, waits for them, and re-layouts, block_sum(): values.reshape(size_x // step_x, step_x, size_y // step_y, step_y, size_z...  152 us
    reduce_sum x7, other arithmetic, block_sum(): return shaped.sum(axis=(1, 3, 5))  56.4 us
    ppermute x42, starting transfers between devices, extended(): lax.ppermute(lax.slice_in_dim(block, 0, width, axis=dim), axis, backward)  54.2 us
    all_gather x1, blocking collectives, local(): lax.all_gather(remainder.reshape(-1), ('gx', 'gz'), axis=0, tiled=True)  52.9 us
    all_gather x1, blocking collectives, local(): gathered = lax.all_gather(row_part, ('gx', 'gz'), axis=0, tiled=True)  37.7 us
    ppermute x42, waiting for transfers between devices, extended(): lax.ppermute(lax.slice_in_dim(block, block.shape[dim] - width, None, axis...  30.8 us
    add x13, other arithmetic, relax(): field + RELAX_WEIGHT * (source - operate(field, coefficient)) / (6.0 + co...  18.3 us
  transfers between devices with their start and end apart: 84, of which 33 were waited for; matrix products, arithmetic and copies ran while one was open for 35% of the time, Pallas kernels for 0%

commit v1 on v0

v1 whole, which is shorter than its diff:
```python
import functools
import math

import jax
import jax.numpy as jnp
from jax import lax
from jax.experimental import pallas as pl
from jax.experimental.pallas import tpu as pltpu
from jax.sharding import Mesh
from jax.sharding import PartitionSpec as P

COARSE = 16
RELAX_WEIGHT = 0.8
F32 = jnp.float32
LANES = 128
DEEP = 16
KEEP = 8
GUARD = 8
MIB = 1 << 20


def lanes_of(rows):
    return lax.broadcasted_iota(jnp.int32, (rows, LANES), 1)


def subs_of(rows):
    return lax.broadcasted_iota(jnp.int32, (rows, LANES), 0)


def take_lanes(values, index):
    return jnp.take_along_axis(values, index, axis=1, mode="promise_in_bounds")


def beside_lanes(values, lane, width, step):
    place = lane & (width - 1)
    low = jnp.where(place >= step, pltpu.roll(values, step, 1), 0.0)
    high = jnp.where(place < width - step, pltpu.roll(values, LANES - step, 1), 0.0)
    return low + high


def weight_of(c):
    return jnp.where(c > 0.0, RELAX_WEIGHT / (6.0 + c), 0.0)


def around(ref, at, start, rows, lane, width, lower=True, upper=True):
    center = ref[at, pl.ds(start, rows)]
    total = ref[at, pl.ds(start - 1, rows)] + ref[at, pl.ds(start + 1, rows)]
    total = total + beside_lanes(center, lane, width, 1)
    if lower:
        total = total + ref[at - 1, pl.ds(start, rows)]
    if upper:
        total = total + ref[at + 1, pl.ds(start, rows)]
    return center, total


def halve_two(ref, planes, lane, first, rows):
    index = 2 * (lane & 63)

    def part(start):
        total = None
        for at in planes:
            for odd in (0, 1):
                piece = ref[at, pl.ds(start + odd, rows, stride=2), :]
                total = piece if total is None else total + piece
        total = total + pltpu.roll(total, LANES - 1, 1)
        return take_lanes(total, index)

    return jnp.where(lane < 64, part(first), part(first + 64))


def halve_four(ref, planes, lane8, first):
    total = None
    for at in planes:
        for odd in (0, 1):
            piece = ref[at, pl.ds(first + odd, 16, stride=2), :]
            total = piece if total is None else total + piece
    total = total + pltpu.roll(total, LANES - 1, 1)
    index = (lane8 & 64) + 2 * (lane8 & 31)
    return jnp.where((lane8 & 32) == 0, take_lanes(total[:8], index), take_lanes(total[8:], index))


def call(kernel, name, outs, args, scratch=(), results=None):
    limit = sum(4 * math.prod(s) for s in scratch) + 6 * MIB
    args = [pltpu.with_memory_space_constraint(a, pltpu.VMEM) for a in args]
    shapes = [
        jax.ShapeDtypeStruct(s, F32) if results else pltpu.VMEM(s, F32) for s in outs
    ]
    return pl.pallas_call(
        kernel,
        out_shape=shapes,
        in_specs=[pl.BlockSpec(memory_space=pltpu.VMEM)] * len(args),
        out_specs=[pl.BlockSpec(memory_space=pltpu.VMEM)] * len(outs),
        scratch_shapes=[pltpu.VMEM(s, F32) for s in scratch],
        compiler_params=pltpu.CompilerParams(vmem_limit_bytes=limit),
        name=name,
    )(*args)


def turn_kernel(f_in, c_in, v_in, f_out, c_out, v_out, to_a, to_b):
    odd = lax.axis_index("gc")
    size_x, _, size_z = f_in.shape
    far = size_z - DEEP
    start_a = pl.multiple_of((1 - odd) * far, DEEP)
    start_b = pl.multiple_of(odd * far, DEEP)
    for which, (source, target) in enumerate(((f_in, f_out), (c_in, c_out), (v_in, v_out))):
        for x in range(size_x):
            target[x] = source[x].T
        to_a[which] = target[:, pl.ds(start_a, DEEP), :]
        to_b[which] = target[:, pl.ds(start_b, DEEP), :]


def fill_rows(target, at, own, low, high):
    rows = own.shape[0]
    target[at, pl.ds(GUARD, DEEP)] = low
    target[at, pl.ds(GUARD + DEEP, rows)] = own
    target[at, pl.ds(GUARD + DEEP + rows, DEEP)] = high


def coefficient_kernel(c_in, za, zb, to_a, to_b, padded):
    odd_z = lax.axis_index("gc") == 1
    even_x = lax.axis_index("gx") % 2 == 0
    size_x, size_z, _ = c_in.shape
    wide = size_z + 2 * DEEP
    coarse_rows = size_z // 4 + 2 * GUARD
    lane = lanes_of(coarse_rows)
    for x in (*range(6), *range(size_x - 6, size_x)):
        low = jnp.where(odd_z, za[1, x], zb[1, x])
        high = jnp.where(odd_z, zb[1, x], za[1, x])
        fill_rows(padded, x, c_in[x], low, high)
    sides = []
    for order in (range(size_x), range(size_x - 1, -1, -1)):
        sides.append(
            (
                padded[order[0], pl.ds(GUARD, wide)],
                padded[order[1], pl.ds(GUARD, wide)],
                0.125 * halve_two(padded, order[2:4], lane, GUARD, coarse_rows),
                0.125 * halve_two(padded, order[4:6], lane, GUARD, coarse_rows),
            )
        )
    start = 0
    for left, right in zip(*sides, strict=True):
        rows = pl.ds(start, left.shape[0])
        to_a[rows] = jnp.where(even_x, right, left)
        to_b[rows] = jnp.where(even_x, left, right)
        start += left.shape[0]


def down_kernel(
    f_in, c_in, v_in, za, zb, xa, xb,
    chunk, v_out, f_out, c_out, f1_out, c1_out, to_a, to_b,
    va, vb, c, g, f, f1, c1, u1, w1,
):
    odd_z = lax.axis_index("gc") == 1
    even_x = lax.axis_index("gx") % 2 == 0
    size_x, size_z, _ = f_in.shape
    wide = size_z + 2 * DEEP
    half = wide // 2
    parts = [(GUARD, half), (GUARD + half, half)]
    off = 4
    last = size_x + off - 1
    lane = lanes_of(half)
    zeros8 = jnp.zeros((GUARD, LANES), F32)

    for which, (source, target, shift) in enumerate(((f_in, f, 0), (c_in, c, off), (v_in, va, off))):
        for x in range(size_x):
            low = jnp.where(odd_z, za[which, x], zb[which, x])
            high = jnp.where(odd_z, zb[which, x], za[which, x])
            fill_rows(target, x + shift, source[x], low, high)
    for ref in (va, vb):
        for at in range(2, size_x + 6):
            ref[at, pl.ds(0, GUARD)] = zeros8
            ref[at, pl.ds(GUARD + wide, GUARD)] = zeros8
    for k in range(2):
        rows = pl.ds(k * wide, wide)
        c[off - 1 - k, pl.ds(GUARD, wide)] = jnp.where(even_x, xb[rows], xa[rows])
        c[last + 1 + k, pl.ds(GUARD, wide)] = jnp.where(even_x, xa[rows], xb[rows])
    for at in range(off - 2, last + 3):
        for start, rows in parts:
            g[at, pl.ds(start, rows)] = weight_of(c[at, pl.ds(start, rows)])

    for at in range(off - 1, last + 2):
        for start, rows in parts:
            here = pl.ds(start, rows)
            if at < off:
                vb[at, here] = g[at, here] * va[off, here]
            elif at > last:
                vb[at, here] = g[at, here] * va[last, here]
            else:
                center, total = around(va, at, start, rows, lane, LANES, at > off, at < last)
                vb[at, here] = 0.2 * center + g[at, here] * (total + f[at - off, here])
    for at in range(off - 2, last + 3):
        for start, rows in parts:
            here = pl.ds(start, rows)
            if at == off - 2:
                va[at, here] = g[at, here] * vb[at + 1, here]
            elif at == last + 2:
                va[at, here] = g[at, here] * vb[at - 1, here]
            else:
                center, total = around(vb, at, start, rows, lane, LANES, at > off - 1, at < last + 1)
                if off <= at <= last:
                    total = total + f[at - off, here]
                va[at, here] = 0.2 * center + g[at, here] * total
    for at in range(off - 3, last + 4):
        for start, rows in parts:
            here = pl.ds(start, rows)
            if at == off - 3:
                vb[at, here] = va[at + 1, here]
            elif at == last + 3:
                vb[at, here] = va[at - 1, here]
            else:
                center, total = around(va, at, start, rows, lane, LANES, at > off - 2, at < last + 2)
                if off <= at <= last:
                    total = total + f[at - off, here]
                vb[at, here] = total - (6.0 + c[at, here]) * center

    rows1 = size_z // 4 + 2 * GUARD
    size1 = size_x // 2
    off1 = 5
    here1 = pl.ds(GUARD, rows1)
    lane1 = lanes_of(rows1)
    for x in range(-2, size1 + 2):
        planes = [at for at in (2 * x + off, 2 * x + off + 1) if off - 3 <= at <= last + 3]
        f1[x + off1, here1] = 0.5 * halve_two(vb, planes, lane1, GUARD, rows1)
    for x in range(-1, size1 + 1):
        c1[x + off1, here1] = 0.125 * halve_two(c, (2 * x + off, 2 * x + off + 1), lane1, GUARD, rows1)
    for k in range(2):
        rows = pl.ds(2 * wide + k * rows1, rows1)
        c1[off1 - 2 - k, here1] = jnp.where(even_x, xb[rows], xa[rows])
        c1[off1 + size1 + 1 + k, here1] = jnp.where(even_x, xa[rows], xb[rows])
    low1, high1 = off1 - 2, off1 + size1 + 1
    for at in range(low1 - 1, high1 + 2):
        for ref in (u1, w1):
            ref[at, pl.ds(0, GUARD)] = zeros8
            ref[at, pl.ds(GUARD + rows1, GUARD)] = zeros8
    for at in range(low1, high1 + 1):
        u1[at, here1] = weight_of(c1[at, here1]) * f1[at, here1]
    for at in range(low1 - 1, high1 + 2):
        weight = weight_of(c1[at, here1])
        if at == low1 - 1:
            w1[at, here1] = weight * u1[at + 1, here1]
        elif at == high1 + 1:
            w1[at, here1] = weight * u1[at - 1, here1]
        else:
            center, total = around(u1, at, GUARD, rows1, lane1, 64, at > low1, at < high1)
            w1[at, here1] = 0.2 * center + weight * (total + f1[at, here1])
    for at in range(low1 - 2, high1 + 3):
        if at == low1 - 2:
            u1[at, here1] = w1[at + 1, here1]
        elif at == high1 + 2:
            u1[at, here1] = w1[at - 1, here1]
        else:
            center, total = around(w1, at, GUARD, rows1, lane1, 64, at > low1 - 1, at < high1 + 1)
            if low1 <= at <= high1:
                total = total + f1[at, here1]
            u1[at, here1] = total - (6.0 + c1[at, here1]) * center

    size2 = size_x // 4
    lane8 = lanes_of(8)
    for x in range(-2, size2 + 2):
        chunk[x + 2] = 0.5 * halve_four(u1, (2 * x + off1, 2 * x + off1 + 1), lane8, 2 * GUARD)
    for x in range(size2):
        chunk[size2 + 4 + x] = 0.125 * halve_four(c1, (2 * x + off1, 2 * x + off1 + 1), lane8, 2 * GUARD)

    inner = pl.ds(GUARD + DEEP - KEEP, size_z + 2 * KEEP)
    v_out[...] = va[pl.ds(off - 2, size_x + 4), inner]
    c_out[...] = c[pl.ds(off - 2, size_x + 4), inner]
    f_out[...] = f[:, inner]
    f1_out[...] = f1[pl.ds(off1 - 2, size1 + 4), here1]
    c1_out[...] = c1[pl.ds(off1 - 3, size1 + 6), here1]
    kept = size_z + 2 * KEEP
    start = 0
    for k in range(5):
        rows = pl.ds(start, kept)
        left, right = va[off - 2 + k, inner], va[last + 2 - k, inner]
        to_a[rows] = jnp.where(even_x, right, left)
        to_b[rows] = jnp.where(even_x, left, right)
        start += kept
    for k in range(2):
        rows = pl.ds(start, kept)
        left, right = f[k, inner], f[size_x - 1 - k, inner]
        to_a[rows] = jnp.where(even_x, right, left)
        to_b[rows] = jnp.where(even_x, left, right)
        start += kept
    pairs = [(f1, off1 - 2 + k, off1 + size1 + 1 - k) for k in range(7)]
    pairs += [(c1, off1 + 3 + k, off1 + size1 - 4 - k) for k in range(2)]
    for ref, at_left, at_right in pairs:
        rows = pl.ds(start, rows1)
        left, right = ref[at_left, here1], ref[at_right, here1]
        to_a[rows] = jnp.where(even_x, right, left)
        to_b[rows] = jnp.where(even_x, left, right)
        start += rows1


def around_tile(ref, x, t, step, lane, sub):
    center = ref[x, t]
    total = ref[x - 1, t] + ref[x + 1, t] + beside_lanes(center, lane, 32, step)
    after = pltpu.roll(jnp.where(lane < 32, ref[x, t + 1], center), LANES - 32, 1)
    total = total + pltpu.roll(jnp.where(sub < step, after, center), 8 - step, 0)
    before = pltpu.roll(jnp.where(lane >= 96, ref[x, t - 1], center), 32, 1)
    total = total + pltpu.roll(jnp.where(sub >= 8 - step, before, center), step, 0)
    return center, total


def pair_sums(values, lane, sub):
    partner = jnp.where((lane & 1) == 0, pltpu.roll(values, LANES - 1, 1), pltpu.roll(values, 1, 1))
    values = values + partner
    partner = jnp.where((sub & 1) == 0, pltpu.roll(values, 7, 0), pltpu.roll(values, 1, 0))
    return values + partner


def loop(count, body):
    if count <= 16:
        for i in range(count):
            body(i)
    else:
        lax.fori_loop(0, count, lambda i, _: (body(i), None)[1], None)


def coarse_kernel(
    nx, nz, own, other, inverse,
    window2, window3, e_out,
    v2, f2, g2, c2, u2, v3, f3, g3, c3, u3, turned, flat,
):
    core = lax.axis_index("gc")
    ny = nz // 2
    size2 = (own.shape[1] - 4) // 2
    lane, sub = lanes_of(8), subs_of(8)
    for ref in (v2, f2, g2, c2, u2, v3, f3, g3, u3):
        ref[...] = jnp.zeros(ref.shape, F32)

    def collect(at):
        for y in range(ny):
            for source, t in ((own, 1 + 2 * y + core), (other, 2 + 2 * y - core)):
                for x in range(size2 + 4):
                    f2[size2 * at + x + 2, t] += source[at * ny + y, x]
                for x in range(size2):
                    c2[size2 * at + x + 4, t] = source[at * ny + y, size2 + 4 + x]

    loop(nx, collect)

    def first(at):
        for x in range(4 + 4 * at, 8 + 4 * at) if isinstance(at, int) else [4 + 4 * at + k for k in range(4)]:
            for t in range(1, nz + 1):
                g2[x, t] = RELAX_WEIGHT / (6.0 + c2[x, t])
                u2[x, t] = g2[x, t] * f2[x, t]

    loop(nx, first)

    def second(at):
        for k in range(4):
            x = 4 + 4 * at + k
            for t in range(1, nz + 1):
                center, total = around_tile(u2, x, t, 1, lane, sub)
                v2[x, t] = 0.2 * center + g2[x, t] * (total + f2[x, t])

    loop(nx, second)

    def third(at):
        for k in range(2):
            x3 = 4 + 2 * at + k
            for t in range(1, nz + 1):
                total_r, total_c = 0.0, 0.0
                for x in (4 + 4 * at + 2 * k, 5 + 4 * at + 2 * k):
                    center, total = around_tile(v2, x, t, 1, lane, sub)
                    total_r += f2[x, t] + total - (6.0 + c2[x, t]) * center
                    total_c += c2[x, t]
                f3[x3, t] = 0.5 * pair_sums(total_r, lane, sub)
                c3[x3, t] = 0.125 * pair_sums(total_c, lane, sub)
                g3[x3, t] = RELAX_WEIGHT / (6.0 + c3[x3, t])
                u3[x3, t] = g3[x3, t] * f3[x3, t]

    loop(nx, third)

    def fourth(at):
        for k in range(2):
            x = 4 + 2 * at + k
            for t in range(1, nz + 1):
                center, total = around_tile(u3, x, t, 2, lane, sub)
                v3[x, t] = 0.2 * center + g3[x, t] * (total + f3[x, t])

    loop(nx, fourth)

    step_x = 2 * nx // COARSE
    group = nz // 4

    for t in range(1, nz + 1):
        rows = []
        for xc in range(COARSE):
            total = 0.0
            for k in range(step_x):
                x = 4 + xc * step_x + k
                center, beside = around_tile(v3, x, t, 2, lane, sub)
                total += f3[x, t] + beside - (6.0 + c3[x, t]) * center
            rows.append(jnp.sum(total, axis=0, keepdims=True))
        block = 0.125 * jnp.concatenate(rows, axis=0)
        spread = block
        for k in range(1, group):
            spread = spread + pltpu.roll(block, LANES - 32 * k, 1)
        tall = jnp.concatenate([spread, jnp.zeros((LANES - COARSE, LANES), F32)], axis=0)
        turned[...] = tall.T
        line = jnp.zeros((8, LANES), F32)
        for k in range(8):
            piece = pltpu.roll(turned[pl.ds(2 * k, 8, stride=16), :], 16 * k, 1) if k else turned[pl.ds(0, 8, stride=16), :]
            line = jnp.where((lane >= 16 * k) & (lane < 16 * k + 16), piece, line)
        count = 4 // group
        for q in range(count):
            at = 2 * ((t - 1) * count + q)
            flat[at : at + 2] = line[2 * group * q : 2 * group * q + 2]

    at_x = lax.axis_index("gx")
    at_z = 2 * lax.axis_index("gy") + core
    for k, (fields2, fields3) in enumerate(((v2, v3), (f2, f3), (g2, g3))):
        for t in range(3):
            window2[k, :, t] = fields2[pl.ds(size2 * at_x, size2 + 8), at_z + t]
            window3[k, :, t] = fields3[pl.ds(2 * at_x, 10), at_z + t]

    total = None
    for t in range(inverse.shape[1] // LANES):
        piece = inverse[:, t * LANES : (t + 1) * LANES] * flat[t : t + 1]
        total = piece if total is None else total + piece
    column = jnp.sum(total, axis=1, keepdims=True)
    copies = e_out.shape[0]
    width = -(-copies // LANES) * LANES
    e_out[...] = jnp.broadcast_to(column, (inverse.shape[0], width)).T[:copies]


def up_kernel(
    nx, nz, e, window2, window3, v_in, f_in, c_in, f1_in, c1_in, xa, xb,
    pressure, residual,
    lifted3, u3, w3, turned, u2, w2, f1, c1, u1, w1, lift1, ua, ub, g, lift0,
):
    even_x = lax.axis_index("gx") % 2 == 0
    at_x = lax.axis_index("gx")
    at_z = 2 * lax.axis_index("gy") + lax.axis_index("gc")
    lane, sub = lanes_of(8), subs_of(8)
    zeros8 = jnp.zeros((GUARD, LANES), F32)
    step_x = 2 * nx // COARSE
    group = nz // 4

    for ref in (lifted3, u3, w3, u2, w2):
        ref[...] = jnp.zeros(ref.shape, F32)
    for t in range(1, nz + 1):
        pieces = []
        for q in range(4):
            at = 2 * (((t - 1) * 4 + q) // group)
            pieces.append(e[at : at + 2])
        rows = jnp.concatenate(pieces, axis=0)
        for k in range(8):
            piece = pltpu.roll(rows, LANES - 16 * k, 1) if k else rows
            turned[pl.ds(2 * k, 8, stride=16), :] = piece
            turned[pl.ds(2 * k + 1, 8, stride=16), :] = piece
        lifted = turned[...].T
        for xc in range(COARSE):
            tile = jnp.broadcast_to(lifted[xc : xc + 1], (8, LANES))
            for k in range(step_x):
                lifted3[4 + xc * step_x + k, t] = tile
    for x in range(10):
        for t in range(3):
            u3[x, t + 1] = window3[0, x, t] + lifted3[2 * at_x + x, at_z + t]
    for source, target, margin in ((u3, w3, 1), (w3, u3, 2)):
        for x in range(margin, 10 - margin):
            for t in range(3):
                center, total = around_tile(source, x, t + 1, 2, lane, sub)
                target[x, t + 1] = 0.2 * center + window3[2, x, t] * (total + window3[1, x, t])

    size2 = 4
    planes2 = size2 + 8
    for x in range(planes2):
        for t in range(3):
            u2[x, t + 1] = window2[0, x, t] + u3[2 + x // 2, t + 1]
    for source, target, margin in ((u2, w2, 1), (w2, u2, 2)):
        for x in range(margin, planes2 - margin):
            for t in range(3):
                center, total = around_tile(source, x, t + 1, 1, lane, sub)
                target[x, t + 1] = 0.2 * center + window2[2, x, t] * (total + window2[1, x, t])

    rows1 = f1_in.shape[1]
    size1 = 2 * size2
    off1 = 5
    here1 = pl.ds(GUARD, rows1)
    lane1 = lanes_of(rows1)
    side = lane >> 6
    fine = (lane & 63) >> 1
    for x in range(2, planes2 - 2):
        below, middle, above = u2[x, 1], u2[x, 2], u2[x, 3]
        index = [(((2 * side + q) & 3) << 5) + fine for q in (-1, 0, 1, 2)]
        tiles = [
            jnp.where(side == 0, take_lanes(below, index[0]), take_lanes(middle, index[0]))[4:],
            take_lanes(middle, index[1]),
            take_lanes(middle, index[2]),
            jnp.where(side == 0, take_lanes(middle, index[3]), take_lanes(above, index[3]))[:4],
        ]
        start = 0
        for tile in tiles:
            count = tile.shape[0]
            lift1[x - 2, pl.ds(start, count, stride=2), :] = tile
            lift1[x - 2, pl.ds(start + 1, count, stride=2), :] = tile
            start += 2 * count

    kept = v_in.shape[1]
    base1 = 7 * kept

    def arrived(start, rows):
        a, b = xa[pl.ds(start, rows)], xb[pl.ds(start, rows)]
        return jnp.where(even_x, b, a), jnp.where(even_x, a, b)

    for x in range(-2, size1 + 2):
        f1[x + off1, here1] = f1_in[x + 2]
    for x in range(-3, size1 + 3):
        c1[x + off1, here1] = c1_in[x + 3]
    for k in range(7):
        left, right = arrived(base1 + k * rows1, rows1)
        if k < 4:
            f1[off1 + 1 - k, here1] += left
            f1[off1 + size1 - 2 + k, here1] += right
        else:
            f1[off1 + 1 - k, here1] = left
            f1[off1 + size1 - 2 + k, here1] = right
    for k in range(2):
        left, right = arrived(base1 + (7 + k) * rows1, rows1)
        c1[off1 - 5 + (1 - k), here1] = left
        c1[off1 + size1 + 3 + k, here1] = right
    planes1 = size1 + 10
    for ref in (u1, w1):
        for at in range(planes1):
            ref[at, pl.ds(0, GUARD)] = zeros8
            ref[at, pl.ds(GUARD + rows1, GUARD)] = zeros8
    for at in range(planes1):
        c1[at, here1] = weight_of(c1[at, here1])
        u1[at, here1] = c1[at, here1] * f1[at, here1]
    for source, target, margin in ((u1, w1, 1), (w1, u1, 2), (u1, w1, 3)):
        for at in range(margin, planes1 - margin):
            center, total = around(source, at, GUARD, rows1, lane1, 64)
            value = 0.2 * center + c1[at, here1] * (total + f1[at, here1])
            if margin == 1:
                value = value + lift1[(at - 1) // 2]
            target[at, here1] = value

    size_x = f_in.shape[0]
    size_z = kept - 2 * KEEP
    short = kept // 4
    index = lanes_of(short) >> 1
    for x in range(-2, size1 + 2):
        for part in range(2):
            source = w1[x + off1, pl.ds(GUARD + (4 if part == 0 else 8), short)]
            tile = take_lanes(source, index + 64 * part)
            lift0[x + 2, pl.ds(part * 2 * short, short, stride=2), :] = tile
            lift0[x + 2, pl.ds(part * 2 * short + 1, short, stride=2), :] = tile

    off = 3
    last = size_x + off - 1
    here = pl.ds(GUARD, kept)
    for ref in (ua, ub):
        for at in range(size_x + 6):
            ref[at, pl.ds(0, GUARD)] = zeros8
            ref[at, pl.ds(GUARD + kept, GUARD)] = zeros8
    reach = {}
    for k in range(5):
        left, right = arrived(k * kept, kept)
        reach[1 - k] = left
        reach[size_x - 2 + k] = right
    for x in range(-3, size_x + 3):
        value = lift0[(x + 4) // 2]
        if -2 <= x <= size_x + 1:
            value = value + v_in[x + 2]
        if x in reach:
            value = value + reach[x]
        ua[x + off, here] = value
    half = kept // 2
    parts = [(GUARD, half), (GUARD + half, half)]
    laneh = lanes_of(half)
    for x in range(-2, size_x + 2):
        for start, rows in parts:
            g[x + 2, pl.ds(start, rows)] = weight_of(c_in[x + 2, pl.ds(start - GUARD, rows)])

    def source_of(x, start, rows):
        at = pl.ds(start - GUARD, rows)
        if 0 <= x < size_x:
            return f_in[x, at]
        k = -1 - x if x < 0 else x - size_x
        left, right = arrived((5 + k) * kept + start - GUARD, rows)
        return left if x < 0 else right

    for source, target, margin in ((ua, ub, 1), (ub, ua, 2)):
        for at in range(margin, size_x + 6 - margin):
            for start, rows in parts:
                center, total = around(source, at, start, rows, laneh, LANES)
                total = total + source_of(at - off, start, rows)
                target[at, pl.ds(start, rows)] = 0.2 * center + g[at - 1, pl.ds(start, rows)] * total
    lane_z = lanes_of(size_z)
    own = GUARD + KEEP
    for x in range(size_x):
        center, total = around(ua, x + off, own, size_z, lane_z, LANES)
        total = total + f_in[x, pl.ds(KEEP, size_z)]
        pressure[x] = center.T
        residual[x] = (total - (6.0 + c_in[x + 2, pl.ds(KEEP, size_z)]) * center).T


def pairs_of(count):
    even = [(i, i ^ 1) for i in range(count)]
    odd = [(i, ((i - 1) ^ 1) + 1) for i in range(1, count - 1)]
    return even, odd


def local(nx, nz, right_side, reaction, initial, coarse_inverse):
    size_x, _, size_z = right_side.shape
    brick = (size_x, size_z, LANES)
    slab = (3, size_x, DEEP, LANES)
    f, c, v, mza, mzb = call(
        turn_kernel, "turn", (brick, brick, brick, slab, slab), (right_side, reaction, initial)
    )
    even_z, odd_z = pairs_of(nz)
    za = lax.ppermute(mza, ("gy", "gc"), even_z)
    zb = lax.ppermute(mzb, ("gy", "gc"), odd_z)

    wide = size_z + 2 * DEEP
    deep = wide + 2 * GUARD
    rows1 = size_z // 4 + 2 * GUARD
    size1, size2 = size_x // 2, size_x // 4
    message = (2 * wide + 2 * rows1, LANES)
    mxa, mxb = call(
        coefficient_kernel, "coefficients", (message, message), (c, za, zb), [(size_x, deep, LANES)]
    )
    even_x, odd_x = pairs_of(nx)
    xa = lax.ppermute(mxa, "gx", even_x)
    xb = lax.ppermute(mxb, "gx", odd_x)

    kept = size_z + 2 * KEEP
    margin = (7 * kept + 9 * rows1, LANES)
    field = (size_x + 8, deep, LANES)
    field1 = (size1 + 10, rows1 + 2 * GUARD, LANES)
    chunk, v, f, c, f1, c1, mua, mub = call(
        down_kernel, "down",
        (
            (2 * size2 + 4, 8, LANES),
            (size_x + 4, kept, LANES),
            (size_x, kept, LANES),
            (size_x + 4, kept, LANES),
            (size1 + 4, rows1, LANES),
            (size1 + 6, rows1, LANES),
            margin,
            margin,
        ),
        (f, c, v, za, zb, xa, xb),
        [field, field, field, field, (size_x, deep, LANES), field1, field1, field1, field1],
    )
    ua = lax.ppermute(mua, "gx", even_x)
    ub = lax.ppermute(mub, "gx", odd_x)

    copies = jnp.broadcast_to(chunk, (nx * nz // 2, *chunk.shape))
    own = lax.all_to_all(copies, ("gx", "gy"), 0, 0, tiled=True)
    other = lax.ppermute(own, "gc", [(0, 1), (1, 0)])

    grid2 = (size2 * nx + 8, nz + 2, 8, LANES)
    grid3 = (2 * nx + 8, nz + 2, 8, LANES)
    rows = coarse_inverse.shape[0]
    window2, window3, e = call(
        functools.partial(coarse_kernel, nx, nz), "coarse",
        ((3, size2 + 8, 3, 8, LANES), (3, 10, 3, 8, LANES), (nx * nz, rows)),
        (own, other, coarse_inverse),
        [*[grid2] * 5, *[grid3] * 5, (LANES, LANES), (COARSE**3 // LANES, LANES)],
    )
    e = lax.all_to_all(e, ("gx", "gy", "gc"), 0, 0, tiled=True).reshape(COARSE**3 // LANES, LANES)

    box2 = (size2 + 8, 5, 8, LANES)
    box3 = (10, 5, 8, LANES)
    box = (size_x + 6, kept + 2 * GUARD, LANES)
    return call(
        functools.partial(up_kernel, nx, nz), "up",
        ((size_x, LANES, size_z), (size_x, LANES, size_z)),
        (e, window2, window3, v, f, c, f1, c1, ua, ub),
        [
            grid3, box3, box3, (LANES, LANES), box2, box2,
            field1, field1, field1, field1, (size2 + 4, rows1, LANES),
            box, box, box, (size1 + 4, kept, LANES),
        ],
        results=True,
    )


def solution(mesh):
    nx, nz = mesh.shape["gx"], mesh.shape["gz"]
    fine = Mesh(mesh.devices.reshape(nx, nz // 2, 2), ("gx", "gy", "gc"))
    brick = P("gx", None, ("gy", "gc"))
    return jax.shard_map(
        lambda *args: tuple(local(nx, nz, *args)),
        mesh=fine,
        in_specs=(brick, brick, brick, P(("gx", "gy", "gc"), None)),
        out_specs=(brick, brick),
        check_vma=False,
    )
```

time: 734 us -> 104 us (0.14); the launches traced: 722 us -> 104 us
  starting transfers between devices: 261 us -> 11.3 us
  local copies, waits for them, and re-layouts: 224 us -> 8.71 us
  other arithmetic: 109 us -> 0 us
  blocking collectives: 90.6 us -> 37.8 us
  Pallas kernels: 0 us -> 23.7 us
  waiting for transfers between devices: 32.6 us -> 21.7 us
    ppermute x84 -> x7, starting transfers between devices: 261 us -> 7.22 us  [the longest x1 2.93 us: local(): xa = lax.ppermute(mxa, 'gx', even_x)]
    reshape x13 -> x0, local copies, waits for them, and re-layouts: 167 us -> none  [the longest x4 152 us: block_sum(): values.reshape(size_x // step_x, step_x, size_y // step_y, step_y, size_z...]
    all_gather x2 -> x0, blocking collectives: 90.6 us -> none  [the longest x1 52.9 us: local(): lax.all_gather(remainder.reshape(-1), ('gx', 'gz'), axis=0, tiled=True)]
    reduce_sum x7 -> x0, other arithmetic: 56.4 us -> none  [block_sum(): return shaped.sum(axis=(1, 3, 5))]
    all_to_all x0 -> x1, blocking collectives: none -> 37.8 us  [local(): own = lax.all_to_all(copies, ('gx', 'gy'), 0, 0, tiled=True)]
    pallas_call x0 -> x5, Pallas kernels: none -> 23.7 us  [call(): pl.pallas_call(kernel, out_shape=shapes, in_specs=[pl.BlockSpec(memory_sp...]
    add x17 -> x0, other arithmetic: 22.7 us -> none  [the longest x13 18.3 us: relax(): field + RELAX_WEIGHT * (source - operate(field, coefficient)) / (6.0 + co...]
    div x2 -> x0, local copies, waits for them, and re-layouts: 13.3 us -> none  [local(): coefficient = block_sum(coefficient, 2, 2, 2) / 8.0]
  transfers between devices with their start and end apart: 84 -> 8, of which waited for: 33 -> 3; matrix products, arithmetic and copies ran while one was open for 35% -> 0% of each run, Pallas kernels for 0% -> 8%
where the time goes in v1:
time: 104 us
  blocking collectives  37.8 us (36%)
  Pallas kernels  23.7 us (23%)
  waiting for transfers between devices  21.7 us (21%)
  starting transfers between devices  11.3 us (11%)
  local copies, waits for them, and re-layouts  8.71 us (8%)
    all_to_all x1, blocking collectives, local(): own = lax.all_to_all(copies, ('gx', 'gy'), 0, 0, tiled=True)  37.8 us
    pallas_call x5, Pallas kernels, call(): pl.pallas_call(kernel, out_shape=shapes, in_specs=[pl.BlockSpec(memory_sp...  23.7 us
    ppermute x1, waiting for transfers between devices, local(): ua = lax.ppermute(mua, 'gx', even_x)  17.8 us
    unnamed x24, local copies, waits for them, and re-layouts  8.64 us
    all_to_all x1, starting transfers between devices, local(): lax.all_to_all(e, ('gx', 'gy', 'gc'), 0, 0, tiled=True)  4.04 us
    ppermute x1, waiting for transfers between devices, local(): xa = lax.ppermute(mxa, 'gx', even_x)  3.16 us
    ppermute x1, starting transfers between devices, local(): xa = lax.ppermute(mxa, 'gx', even_x)  2.93 us
  transfers between devices with their start and end apart: 8, of which 3 were waited for; matrix products, arithmetic and copies ran while one was open for 0% of the time, Pallas kernels for 8%

profile of v1, /device:TPU:0, one launch (start us, length us, event | category | flops | bytes accessed | tf_op | source)
XLA Modules:
  0.0 103.9 jit_solution(17674336381420105283)
XLA Ops:
  0.6 0.0 copy-start.3
  0.6 1.2 %copy-done.3 = f32[16,128,128]{2,1,0:T(8,128)S(1)} copy-done((f32[16,128,128]{2,1,0:T(8,128)S(1)}, f32[16,128,128]{2,1,0:T(8,128)}, u32[]{:S(2)}) %copy-start.3) | copy-done | bytes 1048600
  1.9 0.0 copy-start.4
  1.9 1.2 %copy-done.4 = f32[16,128,128]{2,1,0:T(8,128)S(1)} copy-done((f32[16,128,128]{2,1,0:T(8,128)S(1)}, f32[16,128,128]{2,1,0:T(8,128)}, u32[]{:S(2)}) %copy-start.4) | copy-done | bytes 1048600
  3.1 0.0 copy-start.5
  3.1 1.2 %copy-done.5 = f32[16,128,128]{2,1,0:T(8,128)S(1)} copy-done((f32[16,128,128]{2,1,0:T(8,128)S(1)}, f32[16,128,128]{2,1,0:T(8,128)}, u32[]{:S(2)}) %copy-start.5) | copy-done | bytes 1048600
  4.3 0.9 turn.1
  5.2 0.5 collective-permute-start
  5.7 0.7 collective-permute-start.1
  6.4 0.7 collective-permute-done.za
  7.1 0.0 collective-permute-done.1.zb
  7.1 0.3 coefficients.1
  7.3 2.9 %collective-permute-start.2 = (f32[416,128]{1,0:T(8,128)S(1)}, f32[416,128]{1,0:T(8,128)S(1)}, u32[]{:S(2)}, u32[]{:S(2)}) collective-permute-start(f32[416,128]{1,0:T(8,128)S(1)} %get-tuple-element.25), channel_id=1, source_target_pairs={{0,4},{4,0},{8,12},{12,8},{16,20},{20,16},{24,28},{28,24},{1,5},{5... | collective-permute-start | bytes 638984 | tf_op jit(solution)/shard_map/ppermute | solution.py:625
  10.3 0.7 collective-permute-start.3
  10.9 3.2 %collective-permute-done.2.xa = f32[416,128]{1,0:T(8,128)S(1)} collective-permute-done((f32[416,128]{1,0:T(8,128)S(1)}, f32[416,128]{1,0:T(8,128)S(1)}, u32[]{:S(2)}, u32[]{:S(2)}) %collective-permute-start.2) | collective-permute-done | bytes 213024 | tf_op jit(solution)/shard_map/ppermute | solution.py:625
  14.1 0.0 collective-permute-done.3.xb
  14.1 7.1 %down.1 = (f32[12,8,128]{2,1,0:T(8,128)S(1)}, f32[20,144,128]{2,1,0:T(8,128)S(1)}, f32[16,144,128]{2,1,0:T(8,128)S(1)}, f32[20,144,128]{2,1,0:T(8,128)S(1)}, f32...) custom-call(f32[16,128,128]{2,1,0:T(8,128)S(1)} %get-tuple-element.20.f_in, ...), custom_call_target="tpu_custom_call" | custom-call | tf_op jit(solution)/shard_map/down/pallas_call | solution.py:88
  21.2 0.0 copy-start.1
  21.2 0.0 copy-start.8
  21.2 0.0 copy-start.10
  21.2 0.0 copy-start
  21.2 0.1 broadcast_in_dim.3
  21.3 37.8 %all_to_all.16.own = f32[16,12,8,128]{3,2,1,0:T(8,128)S(1)} all-to-all(f32[16,12,8,128]{3,2,1,0:T(8,128)S(1)} %broadcast_in_dim.3), channel_id=1, replica_groups=mesh['gx'=8,'gy'=2,'gc'=2] {'gx','gy'}, dimensions={0} | all-to-all | bytes 1572864 | tf_op jit(solution)/shard_map/all_to_all | solution.py:651
  59.1 0.0 collective-permute-start.4
  59.1 0.9 collective-permute-start.5
  60.0 1.5 %collective-permute-start.6 = (f32[1440,128]{1,0:T(8,128)}, f32[1440,128]{1,0:T(8,128)}, u32[]{:S(2)}, u32[]{:S(2)}) collective-permute-start(f32[1440,128]{1,0:T(8,128)} %get-tuple-element.37), channel_id=1, source_target_pairs={{4,8},{8,4},{12,16},{16,12},{20,24},{24,20},{5,9},{9,5},{13,17},{1... | collective-permute-start | bytes 2211848 | tf_op jit(solution)/shard_map/ppermute | solution.py:648
  61.5 0.0 collective-permute-done.4.other
  61.5 0.0 copy-done
  61.5 8.5 %coarse.1 = (f32[3,12,3,8,128]{4,3,2,1,0:T(8,128)S(1)}, f32[3,10,3,8,128]{4,3,2,1,0:T(8,128)S(1)}, f32[32,128]{1,0:T(8,128)}) custom-call(f32[16,12,8,128]{3,2,1,0:T(8,128)S(1)} %all_to_all.16.own, f32[16,12,8,128]{3,2,1,0:T(8,128)S(1)} %collective-permute-done.4.other, f32[128,4096]{1,0:T(8,128)S(1)} %copy-done), custom_call_target="tpu_custom_call" | custom-call | tf_op jit(solution)/shard_map/coarse/pallas_call | solution.py:88
  70.0 0.0 copy-done.1
  70.0 0.0 copy-done.8
  70.1 0.0 copy-done.10
  70.1 0.0 copy-start.6
  70.1 0.8 copy-done.6
  70.8 4.0 %all-to-all-start.1 = ((f32[32,1,128]{2,1,0:T(1,128)}), f32[32,1,128]{2,1,0:T(1,128)S(1)}, u32[]{:S(2)}, u32[]{:S(2)}) async-start(f32[32,1,128]{2,1,0:T(1,128)} %bitcast.1), calls=%async_computation.1 | async-start | bytes 32768 | tf_op jit(solution)/shard_map/all_to_all | solution.py:663
  74.9 17.8 %collective-permute-done.5.xa = f32[1440,128]{1,0:T(8,128)} collective-permute-done((f32[1440,128]{1,0:T(8,128)}, f32[1440,128]{1,0:T(8,128)}, u32[]{:S(2)}, u32[]{:S(2)}) %collective-permute-start.5) | collective-permute-done | bytes 737312 | tf_op jit(solution)/shard_map/ppermute | solution.py:647
  92.7 0.0 collective-permute-done.6.xb
  92.7 0.0 all-to-all-done.1
  92.7 0.0 copy-start.2
  92.7 1.3 %copy-done.2 = f32[16,144,128]{2,1,0:T(8,128)S(1)} copy-done((f32[16,144,128]{2,1,0:T(8,128)S(1)}, f32[16,144,128]{2,1,0:T(8,128)}, u32[]{:S(2)}) %copy-start.2) | copy-done | bytes 1179672
  94.0 0.0 copy-start.7
  94.0 1.0 copy-done.7
  95.0 0.0 copy-start.9
  95.0 1.0 copy-done.9
  95.9 0.0 copy-start.11
  95.9 1.0 copy-done.11
  96.9 7.0 %up.1 = (f32[16,128,128]{2,1,0:T(8,128)}, f32[16,128,128]{2,1,0:T(8,128)}) custom-call(f32[32,128]{1,0:T(8,128)S(1)} %bitcast.4, f32[3,12,3,8,128]{4,3,2,1,0:T(8,128)S(1)} %get-tuple-element.29.window2, f32[3,10,3,8,128]{4,3,2,1,0:T(8,128)S(1)} %copy-done.7, f32[20,144,128]{2,1,0:T(8,128)S(1)} %get-tuple-element.31.v_in, f32[16,144,128]{2,1,0:T(8,128)S(1)} %copy-done.2, ...), custom_call_target="tpu_custom_call" | custom-call | tf_op jit(solution)/shard_map/up/pallas_call | solution.py:88
Async XLA Ops:
  0.6 1.2 %copy-start.3 = (f32[16,128,128]{2,1,0:T(8,128)S(1)}, f32[16,128,128]{2,1,0:T(8,128)}, u32[]{:S(2)}) copy-start(f32[16,128,128]{2,1,0:T(8,128)} %f_in.1) | copy-start | bytes 3145732
  1.9 1.2 %copy-start.4 = (f32[16,128,128]{2,1,0:T(8,128)S(1)}, f32[16,128,128]{2,1,0:T(8,128)}, u32[]{:S(2)}) copy-start(f32[16,128,128]{2,1,0:T(8,128)} %c_in.1) | copy-start | bytes 3145732
  3.1 1.2 %copy-start.5 = (f32[16,128,128]{2,1,0:T(8,128)S(1)}, f32[16,128,128]{2,1,0:T(8,128)}, u32[]{:S(2)}) copy-start(f32[16,128,128]{2,1,0:T(8,128)} %v_in.1) | copy-start | bytes 3145732
  5.2 1.9 %collective-permute-start = (f32[3,16,16,128]{3,2,1,0:T(8,128)S(1)}, f32[3,16,16,128]{3,2,1,0:T(8,128)S(1)}, u32[]{:S(2)}, u32[]{:S(2)}) collective-permute-start(f32[3,16,16,128]{3,2,1,0:T(8,128)S(1)} %get-tuple-element.23), channel_id=1, source_target_pairs={{0,1},{1,0},{2,3},{3,2},{4,5},{5,4},{6,7},{7,6},{8,9},{9,8},{10,11... | collective-permute-start | bytes 1179656 | tf_op jit(solution)/shard_map/ppermute | solution.py:613
  5.7 1.4 %collective-permute-start.1 = (f32[3,16,16,128]{3,2,1,0:T(8,128)S(1)}, f32[3,16,16,128]{3,2,1,0:T(8,128)S(1)}, u32[]{:S(2)}, u32[]{:S(2)}) collective-permute-start(f32[3,16,16,128]{3,2,1,0:T(8,128)S(1)} %get-tuple-element.24), channel_id=1, source_target_pairs={{1,2},{2,1},{5,6},{6,5},{9,10},{10,9},{13,14},{14,13},{17,18},{18,... | collective-permute-start | bytes 1179656 | tf_op jit(solution)/shard_map/ppermute | solution.py:614
  7.3 6.8 %collective-permute-start.2 = (f32[416,128]{1,0:T(8,128)S(1)}, f32[416,128]{1,0:T(8,128)S(1)}, u32[]{:S(2)}, u32[]{:S(2)}) collective-permute-start(f32[416,128]{1,0:T(8,128)S(1)} %get-tuple-element.25), channel_id=1, source_target_pairs={{0,4},{4,0},{8,12},{12,8},{16,20},{20,16},{24,28},{28,24},{1,5},{5... | collective-permute-start | bytes 638984 | tf_op jit(solution)/shard_map/ppermute | solution.py:625
  10.3 3.8 %collective-permute-start.3 = (f32[416,128]{1,0:T(8,128)S(1)}, f32[416,128]{1,0:T(8,128)S(1)}, u32[]{:S(2)}, u32[]{:S(2)}) collective-permute-start(f32[416,128]{1,0:T(8,128)S(1)} %get-tuple-element.26), channel_id=1, source_target_pairs={{4,8},{8,4},{12,16},{16,12},{20,24},{24,20},{5,9},{9,5},{13,17},{1... | collective-permute-start | bytes 638984 | tf_op jit(solution)/shard_map/ppermute | solution.py:626
  21.2 48.8 %copy-start.1 = (f32[16,144,128]{2,1,0:T(8,128)}, f32[16,144,128]{2,1,0:T(8,128)S(1)}, u32[]{:S(2)}) copy-start(f32[16,144,128]{2,1,0:T(8,128)S(1)} %get-tuple-element.32.f_in) | copy-start | bytes 3538948
  21.2 48.8 %copy-start.8 = (f32[14,48,128]{2,1,0:T(8,128)}, f32[14,48,128]{2,1,0:T(8,128)S(1)}, u32[]{:S(2)}) copy-start(f32[14,48,128]{2,1,0:T(8,128)S(1)} %get-tuple-element.35.c1_in) | copy-start | bytes 1032196
  21.2 48.8 %copy-start.10 = (f32[12,48,128]{2,1,0:T(8,128)}, f32[12,48,128]{2,1,0:T(8,128)S(1)}, u32[]{:S(2)}) copy-start(f32[12,48,128]{2,1,0:T(8,128)S(1)} %get-tuple-element.34.f1_in) | copy-start | bytes 884740
  21.2 40.3 %copy-start = (f32[128,4096]{1,0:T(8,128)S(1)}, f32[128,4096]{1,0:T(8,128)}, u32[]{:S(2)}) copy-start(f32[128,4096]{1,0:T(8,128)} %inverse.1) | copy-start | bytes 6291460
  59.1 2.4 %collective-permute-start.4 = (f32[16,12,8,128]{3,2,1,0:T(8,128)S(1)}, f32[16,12,8,128]{3,2,1,0:T(8,128)S(1)}, u32[]{:S(2)}, u32[]{:S(2)}) collective-permute-start(f32[16,12,8,128]{3,2,1,0:T(8,128)S(1)} %all_to_all.16.own), channel_id=1, source_target_pairs={{0,1},{1,0},{2,3},{3,2},{4,5},{5,4},{6,7},{7,6},{8,9},{9,8},{10,11... | collective-permute-start | bytes 2359304 | tf_op jit(solution)/shard_map/ppermute | solution.py:652
  59.1 33.6 %collective-permute-start.5 = (f32[1440,128]{1,0:T(8,128)}, f32[1440,128]{1,0:T(8,128)}, u32[]{:S(2)}, u32[]{:S(2)}) collective-permute-start(f32[1440,128]{1,0:T(8,128)} %get-tuple-element.36), channel_id=1, source_target_pairs={{0,4},{4,0},{8,12},{12,8},{16,20},{20,16},{24,28},{28,24},{1,5},{5... | collective-permute-start | bytes 2211848 | tf_op jit(solution)/shard_map/ppermute | solution.py:647
  60.0 32.7 %collective-permute-start.6 = (f32[1440,128]{1,0:T(8,128)}, f32[1440,128]{1,0:T(8,128)}, u32[]{:S(2)}, u32[]{:S(2)}) collective-permute-start(f32[1440,128]{1,0:T(8,128)} %get-tuple-element.37), channel_id=1, source_target_pairs={{4,8},{8,4},{12,16},{16,12},{20,24},{24,20},{5,9},{9,5},{13,17},{1... | collective-permute-start | bytes 2211848 | tf_op jit(solution)/shard_map/ppermute | solution.py:648
  70.1 0.8 copy-start.6
  70.8 21.9 %all-to-all-start.1 = ((f32[32,1,128]{2,1,0:T(1,128)}), f32[32,1,128]{2,1,0:T(1,128)S(1)}, u32[]{:S(2)}, u32[]{:S(2)}) async-start(f32[32,1,128]{2,1,0:T(1,128)} %bitcast.1), calls=%async_computation.1 | async-start | bytes 32768 | tf_op jit(solution)/shard_map/all_to_all | solution.py:663
  92.7 1.3 %copy-start.2 = (f32[16,144,128]{2,1,0:T(8,128)S(1)}, f32[16,144,128]{2,1,0:T(8,128)}, u32[]{:S(2)}) copy-start(f32[16,144,128]{2,1,0:T(8,128)} %copy-done.1) | copy-start | bytes 3538948
  94.0 1.0 copy-start.7
  95.0 1.0 copy-start.9
  95.9 1.0 copy-start.11

commit v2 on v1

--- a/solution.py
+++ b/solution.py
@@ -77,6 +77,45 @@
     total = total + pltpu.roll(total, LANES - 1, 1)
     index = (lane8 & 64) + 2 * (lane8 & 31)
     return jnp.where((lane8 & 32) == 0, take_lanes(total[:8], index), take_lanes(total[8:], index))
+
+
+def around_tile(ref, x, t, step, lane, sub):
+    center = ref[x, t]
+    total = ref[x - 1, t] + ref[x + 1, t] + beside_lanes(center, lane, 32, step)
+    after = pltpu.roll(jnp.where(lane < 32, ref[x, t + 1], center), LANES - 32, 1)
+    total = total + pltpu.roll(jnp.where(sub < step, after, center), 8 - step, 0)
+    before = pltpu.roll(jnp.where(lane >= 96, ref[x, t - 1], center), 32, 1)
+    total = total + pltpu.roll(jnp.where(sub >= 8 - step, before, center), step, 0)
+    return center, total
+
+
+def pair_sums(values, lane, sub):
+    partner = jnp.where((lane & 1) == 0, pltpu.roll(values, LANES - 1, 1), pltpu.roll(values, 1, 1))
+    values = values + partner
+    partner = jnp.where((sub & 1) == 0, pltpu.roll(values, 7, 0), pltpu.roll(values, 1, 0))
+    return values + partner
+
+
+def halve_tiles(ref, planes, lane, sub, beyond):
+    def edge(start):
+        total = None
+        for at in planes:
+            for odd in (0, 1):
+                piece = ref[at, pl.ds(start + odd, 4, stride=2), :]
+                total = piece if total is None else total + piece
+        return total
+
+    past = jnp.concatenate([edge(beyond), edge(GUARD)], axis=0)
+    past = past + pltpu.roll(past, LANES - 1, 1)
+    past = take_lanes(past, jnp.where(sub < 4, 64, 0) + 2 * (lane & 31))
+    kept = ((sub < 4) & (lane < 32)) | ((sub >= 4) & (lane >= 96))
+    return halve_four(ref, planes, lane, 2 * GUARD), jnp.where(kept, past, 0.0)
+
+
+def put_tiles(target, at, own, past, lane):
+    target[at, 2] = own
+    target[at, 1] = jnp.where(lane >= 96, past, 0.0)
+    target[at, 3] = jnp.where(lane < 32, past, 0.0)
 
 
 def call(kernel, name, outs, args, scratch=(), results=None):
@@ -116,26 +155,27 @@
     target[at, pl.ds(GUARD + DEEP + rows, DEEP)] = high
 
 
-def coefficient_kernel(c_in, za, zb, to_a, to_b, padded):
+def coefficient_kernel(c_in, za, zb, to_a, to_b, padded, c1):
     odd_z = lax.axis_index("gc") == 1
     even_x = lax.axis_index("gx") % 2 == 0
     size_x, size_z, _ = c_in.shape
-    wide = size_z + 2 * DEEP
-    coarse_rows = size_z // 4 + 2 * GUARD
-    lane = lanes_of(coarse_rows)
-    for x in (*range(6), *range(size_x - 6, size_x)):
+    wide = pl.ds(GUARD, size_z + 2 * DEEP)
+    rows1 = size_z // 4 + 2 * GUARD
+    here1 = pl.ds(GUARD, rows1)
+    lane, lane8, sub8 = lanes_of(rows1), lanes_of(8), subs_of(8)
+    for x in range(size_x):
         low = jnp.where(odd_z, za[1, x], zb[1, x])
         high = jnp.where(odd_z, zb[1, x], za[1, x])
         fill_rows(padded, x, c_in[x], low, high)
+    for x in range(1, 7):
+        c1[x, here1] = 0.125 * halve_two(padded, (2 * x, 2 * x + 1), lane, GUARD, rows1)
     sides = []
-    for order in (range(size_x), range(size_x - 1, -1, -1)):
+    for order, order1 in ((range(size_x), range(8)), (range(size_x - 1, -1, -1), range(7, -1, -1))):
+        tiles = []
+        for k in (2, 4):
+            tiles += [0.125 * tile for tile in halve_tiles(c1, order1[k : k + 2], lane8, sub8, rows1)]
         sides.append(
-            (
-                padded[order[0], pl.ds(GUARD, wide)],
-                padded[order[1], pl.ds(GUARD, wide)],
-                0.125 * halve_two(padded, order[2:4], lane, GUARD, coarse_rows),
-                0.125 * halve_two(padded, order[4:6], lane, GUARD, coarse_rows),
-            )
+            [padded[order[0], wide], padded[order[1], wide], c1[order1[1], here1], c1[order1[2], here1], *tiles]
         )
     start = 0
     for left, right in zip(*sides, strict=True):
@@ -147,8 +187,8 @@
 
 def down_kernel(
     f_in, c_in, v_in, za, zb, xa, xb,
-    chunk, v_out, f_out, c_out, f1_out, c1_out, to_a, to_b,
-    va, vb, c, g, f, f1, c1, u1, w1,
+    chunk, near_a, near_b, to_a, to_b, v_out, f_out, c_out, f1_out, c1_out, v1_out, v2, f2, c2,
+    va, vb, c, g, f, f1, c1, u1, w1, u2, r2,
 ):
     odd_z = lax.axis_index("gc") == 1
     even_x = lax.axis_index("gx") % 2 == 0
@@ -255,11 +295,60 @@
             u1[at, here1] = total - (6.0 + c1[at, here1]) * center
 
     size2 = size_x // 4
-    lane8 = lanes_of(8)
+    off2 = 5
+    low2, high2 = off2 - 2, off2 + size2 + 1
+    lane8, sub8 = lanes_of(8), subs_of(8)
+    for ref in (v2, f2, c2, u2):
+        ref[...] = jnp.zeros(ref.shape, F32)
     for x in range(-2, size2 + 2):
-        chunk[x + 2] = 0.5 * halve_four(u1, (2 * x + off1, 2 * x + off1 + 1), lane8, 2 * GUARD)
-    for x in range(size2):
-        chunk[size2 + 4 + x] = 0.125 * halve_four(c1, (2 * x + off1, 2 * x + off1 + 1), lane8, 2 * GUARD)
+        own, past = halve_tiles(u1, (2 * x + off1, 2 * x + off1 + 1), lane8, sub8, rows1)
+        put_tiles(f2, x + off2, 0.5 * own, 0.5 * past, lane8)
+    for x in range(-1, size2 + 1):
+        own, past = halve_tiles(c1, (2 * x + off1, 2 * x + off1 + 1), lane8, sub8, rows1)
+        put_tiles(c2, x + off2, 0.125 * own, 0.125 * past, lane8)
+    for k in range(2):
+        own, past = (pl.ds(2 * wide + 2 * rows1 + 8 * (2 * k + j), 8) for j in (0, 1))
+        put_tiles(
+            c2, low2 - k, jnp.where(even_x, xb[own], xa[own]), jnp.where(even_x, xb[past], xa[past]), lane8
+        )
+        put_tiles(
+            c2, high2 + k, jnp.where(even_x, xa[own], xb[own]), jnp.where(even_x, xa[past], xb[past]), lane8
+        )
+    for at in range(low2, high2 + 1):
+        for t in (1, 2, 3):
+            u2[at, t] = weight_of(c2[at, t]) * f2[at, t]
+    for at in range(low2 - 1, high2 + 2):
+        for t in (1, 2, 3):
+            center, total = around_tile(u2, at, t, 1, lane8, sub8)
+            v2[at, t] = 0.2 * center + weight_of(c2[at, t]) * (total + f2[at, t])
+    for at in range(low2 - 2, high2 + 3):
+        center, total = around_tile(v2, at, 2, 1, lane8, sub8)
+        r2[at] = f2[at, 2] + total - (6.0 + c2[at, 2]) * center
+
+    planes = [0.5 * pair_sums(r2[2 * k + 1] + r2[2 * k + 2], lane8, sub8) for k in range(size2 // 2 + 4)]
+    planes += [
+        0.125 * pair_sums(c2[off2 + 2 * k, 2] + c2[off2 + 2 * k + 1, 2], lane8, sub8) for k in range(size2 // 2)
+    ]
+    planes = [take_lanes(plane, 2 * (lane8 & 63)) for plane in planes]
+    for k in range(2):
+        even, odd = (
+            jnp.where(lane8 < 64, planes[4 * k + j], planes[4 * k + j + 1]) for j in (0, 2)
+        )
+        tile = jnp.where((sub8 & 1) == 0, even, odd)
+        for at in range(chunk.shape[0]):
+            chunk[at, k] = tile
+
+    pairs = [(v2, 2, off2 - k, off2 + size2 - 1 + k) for k in (1, 2, 3)]
+    pairs += [(f2, 2, off2 - k, off2 + size2 - 1 + k) for k in (1, 2)]
+    pairs += [(f1, here1, off1 + k, off1 + size1 - 1 - k) for k in (-2, -1, 0, 1, 2)]
+    pairs += [(w1, here1, off1 + k, off1 + size1 - 1 - k) for k in (2, 3)]
+    start = 0
+    for ref, rows, at_left, at_right in pairs:
+        left, right = ref[at_left, rows], ref[at_right, rows]
+        target = pl.ds(start, left.shape[0])
+        near_a[target] = jnp.where(even_x, right, left)
+        near_b[target] = jnp.where(even_x, left, right)
+        start += left.shape[0]
 
     inner = pl.ds(GUARD + DEEP - KEEP, size_z + 2 * KEEP)
     v_out[...] = va[pl.ds(off - 2, size_x + 4), inner]
@@ -267,45 +356,67 @@
     f_out[...] = f[:, inner]
     f1_out[...] = f1[pl.ds(off1 - 2, size1 + 4), here1]
     c1_out[...] = c1[pl.ds(off1 - 3, size1 + 6), here1]
+    v1_out[0] = w1[off1 - 3, here1]
+    v1_out[1] = w1[off1 + size1 + 2, here1]
+
     kept = size_z + 2 * KEEP
-    start = 0
-    for k in range(5):
-        rows = pl.ds(start, kept)
-        left, right = va[off - 2 + k, inner], va[last + 2 - k, inner]
+    lane = lanes_of(kept)
+    first = GUARD + DEEP - KEEP
+    sides = []
+    for edge, inward in ((off, 1), (last, -1)):
+        second = edge + inward
+        center, total = around(va, second, first, kept, lane, LANES)
+        swept = 0.2 * center + g[second, inner] * (total + f[second - off, inner])
+        source = f[edge - off, inner]
+        sides.append(
+            (va[edge - 2 * inward, inner], va[edge - inward, inner], va[edge, inner], source + center, source + swept)
+        )
+    for k, (left, right) in enumerate(zip(*sides, strict=True)):
+        rows = pl.ds(k * kept, kept)
         to_a[rows] = jnp.where(even_x, right, left)
         to_b[rows] = jnp.where(even_x, left, right)
-        start += kept
-    for k in range(2):
-        rows = pl.ds(start, kept)
-        left, right = f[k, inner], f[size_x - 1 - k, inner]
-        to_a[rows] = jnp.where(even_x, right, left)
-        to_b[rows] = jnp.where(even_x, left, right)
-        start += kept
-    pairs = [(f1, off1 - 2 + k, off1 + size1 + 1 - k) for k in range(7)]
-    pairs += [(c1, off1 + 3 + k, off1 + size1 - 4 - k) for k in range(2)]
-    for ref, at_left, at_right in pairs:
-        rows = pl.ds(start, rows1)
-        left, right = ref[at_left, here1], ref[at_right, here1]
-        to_a[rows] = jnp.where(even_x, right, left)
-        to_b[rows] = jnp.where(even_x, left, right)
-        start += rows1
-
-
-def around_tile(ref, x, t, step, lane, sub):
-    center = ref[x, t]
-    total = ref[x - 1, t] + ref[x + 1, t] + beside_lanes(center, lane, 32, step)
-    after = pltpu.roll(jnp.where(lane < 32, ref[x, t + 1], center), LANES - 32, 1)
-    total = total + pltpu.roll(jnp.where(sub < step, after, center), 8 - step, 0)
-    before = pltpu.roll(jnp.where(lane >= 96, ref[x, t - 1], center), 32, 1)
-    total = total + pltpu.roll(jnp.where(sub >= 8 - step, before, center), step, 0)
-    return center, total
-
-
-def pair_sums(values, lane, sub):
-    partner = jnp.where((lane & 1) == 0, pltpu.roll(values, LANES - 1, 1), pltpu.roll(values, 1, 1))
-    values = values + partner
-    partner = jnp.where((sub & 1) == 0, pltpu.roll(values, 7, 0), pltpu.roll(values, 1, 0))
-    return values + partner
+
+
+def hold_kernel(a, b, _, out_a, out_b):
+    out_a[...] = a[...]
+    out_b[...] = b[...]
+
+
+def complete_kernel(v2, f2, near_a, near_b, to_a, to_b, own, out_a, out_b):
+    even_x = lax.axis_index("gx") % 2 == 0
+    size2 = own.shape[0] // 2
+    planes = [ref[5 + x, 2] for ref in (v2, f2) for x in range(size2)]
+    for k, (base, step) in enumerate(((0, 0), (0, 1), (0, 2), (size2, 0), (size2, 1))):
+        rows = pl.ds(8 * k, 8)
+        left = jnp.where(even_x, near_b[rows], near_a[rows])
+        right = jnp.where(even_x, near_a[rows], near_b[rows])
+        planes[base + step] = planes[base + step] + left
+        planes[base + size2 - 1 - step] = planes[base + size2 - 1 - step] + right
+    for k, plane in enumerate(planes):
+        own[k] = plane
+    out_a[...] = to_a[...]
+    out_b[...] = to_b[...]
+
+
+def past_tiles(za, zb, k, odd_z, lane):
+    below = jnp.where(odd_z, za[k], zb[k])
+    above = jnp.where(odd_z, zb[k], za[k])
+    return jnp.where(lane >= 96, below, jnp.where(lane < 32, above, 0.0))
+
+
+def side_kernel(own, za, zb, to_a, to_b):
+    odd_z = lax.axis_index("gc") == 1
+    even_x = lax.axis_index("gx") % 2 == 0
+    size2 = own.shape[0] // 2
+    lane = lanes_of(8)
+    tiles = [(own[k], past_tiles(za, zb, k, odd_z, lane)) for k in range(2 * size2)]
+    at = 0
+    for base, count in ((0, size2), (size2, size2 - 1)):
+        for k in range(count):
+            for left, right in zip(tiles[base + k], tiles[base + size2 - 1 - k], strict=True):
+                to_a[at] = jnp.where(even_x, right, left)
+                to_b[at] = jnp.where(even_x, left, right)
+                at += 1
 
 
 def loop(count, body):
@@ -317,57 +428,38 @@
 
 
 def coarse_kernel(
-    nx, nz, own, other, inverse,
-    window2, window3, e_out,
-    v2, f2, g2, c2, u2, v3, f3, g3, c3, u3, turned, flat,
+    nx, nz, own, other, inverse, _,
+    window3, e_out,
+    v3, f3, g3, c3, u3, turned, flat,
 ):
     core = lax.axis_index("gc")
     ny = nz // 2
-    size2 = (own.shape[1] - 4) // 2
     lane, sub = lanes_of(8), subs_of(8)
-    for ref in (v2, f2, g2, c2, u2, v3, f3, g3, u3):
+    for ref in (v3, f3, g3, u3):
         ref[...] = jnp.zeros(ref.shape, F32)
 
     def collect(at):
         for y in range(ny):
             for source, t in ((own, 1 + 2 * y + core), (other, 2 + 2 * y - core)):
-                for x in range(size2 + 4):
-                    f2[size2 * at + x + 2, t] += source[at * ny + y, x]
-                for x in range(size2):
-                    c2[size2 * at + x + 4, t] = source[at * ny + y, size2 + 4 + x]
+                planes = []
+                for k in range(2):
+                    tile = source[at * ny + y, k]
+                    even = jnp.where((sub & 1) == 0, tile, pltpu.roll(tile, 1, 0))
+                    odd = jnp.where((sub & 1) == 1, tile, pltpu.roll(tile, 7, 0))
+                    planes += [take_lanes(part, (lane >> 1) + 64 * j) for part in (even, odd) for j in (0, 1)]
+                for k in range(6):
+                    f3[2 * at + 2 + k, t] += planes[k]
+                for k in range(2):
+                    c3[2 * at + 4 + k, t] = planes[6 + k]
 
     loop(nx, collect)
-
-    def first(at):
-        for x in range(4 + 4 * at, 8 + 4 * at) if isinstance(at, int) else [4 + 4 * at + k for k in range(4)]:
-            for t in range(1, nz + 1):
-                g2[x, t] = RELAX_WEIGHT / (6.0 + c2[x, t])
-                u2[x, t] = g2[x, t] * f2[x, t]
-
-    loop(nx, first)
-
-    def second(at):
-        for k in range(4):
-            x = 4 + 4 * at + k
-            for t in range(1, nz + 1):
-                center, total = around_tile(u2, x, t, 1, lane, sub)
-                v2[x, t] = 0.2 * center + g2[x, t] * (total + f2[x, t])
-
-    loop(nx, second)
 
     def third(at):
         for k in range(2):
-            x3 = 4 + 2 * at + k
+            x = 4 + 2 * at + k
             for t in range(1, nz + 1):
-                total_r, total_c = 0.0, 0.0
-                for x in (4 + 4 * at + 2 * k, 5 + 4 * at + 2 * k):
-                    center, total = around_tile(v2, x, t, 1, lane, sub)
-                    total_r += f2[x, t] + total - (6.0 + c2[x, t]) * center
-                    total_c += c2[x, t]
-                f3[x3, t] = 0.5 * pair_sums(total_r, lane, sub)
-                c3[x3, t] = 0.125 * pair_sums(total_c, lane, sub)
-                g3[x3, t] = RELAX_WEIGHT / (6.0 + c3[x3, t])
-                u3[x3, t] = g3[x3, t] * f3[x3, t]
+                g3[x, t] = RELAX_WEIGHT / (6.0 + c3[x, t])
+                u3[x, t] = g3[x, t] * f3[x, t]
 
     loop(nx, third)
 
@@ -409,10 +501,9 @@
 
     at_x = lax.axis_index("gx")
     at_z = 2 * lax.axis_index("gy") + core
-    for k, (fields2, fields3) in enumerate(((v2, v3), (f2, f3), (g2, g3))):
+    for k, ref in enumerate((v3, f3, g3)):
         for t in range(3):
-            window2[k, :, t] = fields2[pl.ds(size2 * at_x, size2 + 8), at_z + t]
-            window3[k, :, t] = fields3[pl.ds(2 * at_x, 10), at_z + t]
+            window3[k, :, t] = ref[pl.ds(2 * at_x, 10), at_z + t]
 
     total = None
     for t in range(inverse.shape[1] // LANES):
@@ -424,20 +515,14 @@
     e_out[...] = jnp.broadcast_to(column, (inverse.shape[0], width)).T[:copies]
 
 
-def up_kernel(
-    nx, nz, e, window2, window3, v_in, f_in, c_in, f1_in, c1_in, xa, xb,
-    pressure, residual,
-    lifted3, u3, w3, turned, u2, w2, f1, c1, u1, w1, lift1, ua, ub, g, lift0,
-):
-    even_x = lax.axis_index("gx") % 2 == 0
+def top_kernel(nx, nz, e, window3, u3, lifted3, w3, turned):
     at_x = lax.axis_index("gx")
     at_z = 2 * lax.axis_index("gy") + lax.axis_index("gc")
     lane, sub = lanes_of(8), subs_of(8)
-    zeros8 = jnp.zeros((GUARD, LANES), F32)
     step_x = 2 * nx // COARSE
     group = nz // 4
 
-    for ref in (lifted3, u3, w3, u2, w2):
+    for ref in (lifted3, u3, w3):
         ref[...] = jnp.zeros(ref.shape, F32)
     for t in range(1, nz + 1):
         pieces = []
@@ -463,20 +548,44 @@
                 center, total = around_tile(source, x, t + 1, 2, lane, sub)
                 target[x, t + 1] = 0.2 * center + window3[2, x, t] * (total + window3[1, x, t])
 
-    size2 = 4
+
+def up_kernel(
+    nx, nz, u3, own2, za, zb, sides_a, sides_b, c2, v_in, f_in, c_in, f1_in, c1_in, v1_in, near_a, near_b, xa, xb,
+    pressure, residual,
+    u2, w2, f2, f1, c1, u1, w1, lift1, ua, ub, g, lift0,
+):
+    even_x = lax.axis_index("gx") % 2 == 0
+    lane, sub = lanes_of(8), subs_of(8)
+    zeros8 = jnp.zeros((GUARD, LANES), F32)
+    for ref in (u2, w2, f2):
+        ref[...] = jnp.zeros(ref.shape, F32)
+
+    odd_z = lax.axis_index("gc") == 1
+    size2 = own2.shape[0] // 2
     planes2 = size2 + 8
+    for k in range(2 * size2):
+        target = u2 if k < size2 else f2
+        put_tiles(target, 4 + k % size2, own2[k], past_tiles(za, zb, k, odd_z, lane), lane)
+    at = 0
+    for target, count in ((u2, size2), (f2, size2 - 1)):
+        for k in range(count):
+            left = [jnp.where(even_x, sides_b[at + j], sides_a[at + j]) for j in (0, 1)]
+            right = [jnp.where(even_x, sides_a[at + j], sides_b[at + j]) for j in (0, 1)]
+            put_tiles(target, 3 - k, *left, lane)
+            put_tiles(target, 4 + size2 + k, *right, lane)
+            at += 2
     for x in range(planes2):
-        for t in range(3):
-            u2[x, t + 1] = window2[0, x, t] + u3[2 + x // 2, t + 1]
+        for t in (1, 2, 3):
+            u2[x, t] += u3[2 + x // 2, t]
     for source, target, margin in ((u2, w2, 1), (w2, u2, 2)):
         for x in range(margin, planes2 - margin):
-            for t in range(3):
-                center, total = around_tile(source, x, t + 1, 1, lane, sub)
-                target[x, t + 1] = 0.2 * center + window2[2, x, t] * (total + window2[1, x, t])
+            for t in (1, 2, 3):
+                center, total = around_tile(source, x, t, 1, lane, sub)
+                target[x, t] = 0.2 * center + weight_of(c2[x + 1, t]) * (total + f2[x, t])
 
     rows1 = f1_in.shape[1]
     size1 = 2 * size2
-    off1 = 5
+    off1 = 4
     here1 = pl.ds(GUARD, rows1)
     lane1 = lanes_of(rows1)
     side = lane >> 6
@@ -498,43 +607,44 @@
             start += 2 * count
 
     kept = v_in.shape[1]
-    base1 = 7 * kept
-
-    def arrived(start, rows):
-        a, b = xa[pl.ds(start, rows)], xb[pl.ds(start, rows)]
+
+    def arrived(start, rows, a=xa, b=xb):
+        a, b = a[pl.ds(start, rows)], b[pl.ds(start, rows)]
         return jnp.where(even_x, b, a), jnp.where(even_x, a, b)
 
     for x in range(-2, size1 + 2):
         f1[x + off1, here1] = f1_in[x + 2]
     for x in range(-3, size1 + 3):
-        c1[x + off1, here1] = c1_in[x + 3]
+        c1[x + off1, here1] = weight_of(c1_in[x + 3])
+    base1 = 40
     for k in range(7):
-        left, right = arrived(base1 + k * rows1, rows1)
+        left, right = arrived(base1 + k * rows1, rows1, near_a, near_b)
         if k < 4:
             f1[off1 + 1 - k, here1] += left
             f1[off1 + size1 - 2 + k, here1] += right
+        elif k == 4:
+            f1[off1 - 3, here1] = left
+            f1[off1 + size1 + 2, here1] = right
         else:
-            f1[off1 + 1 - k, here1] = left
-            f1[off1 + size1 - 2 + k, here1] = right
-    for k in range(2):
-        left, right = arrived(base1 + (7 + k) * rows1, rows1)
-        c1[off1 - 5 + (1 - k), here1] = left
-        c1[off1 + size1 + 3 + k, here1] = right
-    planes1 = size1 + 10
+            w1[off1 + 2 - k, here1] = left + v1_in[0] if k == 5 else left
+            w1[off1 + size1 - 3 + k, here1] = right + v1_in[1] if k == 5 else right
+    planes1 = size1 + 8
     for ref in (u1, w1):
         for at in range(planes1):
             ref[at, pl.ds(0, GUARD)] = zeros8
             ref[at, pl.ds(GUARD + rows1, GUARD)] = zeros8
+    for at in range(1, planes1 - 1):
+        u1[at, here1] = c1[at, here1] * f1[at, here1]
     for at in range(planes1):
-        c1[at, here1] = weight_of(c1[at, here1])
-        u1[at, here1] = c1[at, here1] * f1[at, here1]
-    for source, target, margin in ((u1, w1, 1), (w1, u1, 2), (u1, w1, 3)):
+        value = w1[at, here1]
+        if 2 <= at < planes1 - 2:
+            center, total = around(u1, at, GUARD, rows1, lane1, 64)
+            value = 0.2 * center + c1[at, here1] * (total + f1[at, here1])
+        w1[at, here1] = value + lift1[at // 2]
+    for source, target, margin in ((w1, u1, 1), (u1, w1, 2)):
         for at in range(margin, planes1 - margin):
             center, total = around(source, at, GUARD, rows1, lane1, 64)
-            value = 0.2 * center + c1[at, here1] * (total + f1[at, here1])
-            if margin == 1:
-                value = value + lift1[(at - 1) // 2]
-            target[at, here1] = value
+            target[at, here1] = 0.2 * center + c1[at, here1] * (total + f1[at, here1])
 
     size_x = f_in.shape[0]
     size_z = kept - 2 * KEEP
@@ -554,18 +664,16 @@
         for at in range(size_x + 6):
             ref[at, pl.ds(0, GUARD)] = zeros8
             ref[at, pl.ds(GUARD + kept, GUARD)] = zeros8
-    reach = {}
-    for k in range(5):
-        left, right = arrived(k * kept, kept)
-        reach[1 - k] = left
-        reach[size_x - 2 + k] = right
     for x in range(-3, size_x + 3):
         value = lift0[(x + 4) // 2]
         if -2 <= x <= size_x + 1:
             value = value + v_in[x + 2]
-        if x in reach:
-            value = value + reach[x]
         ua[x + off, here] = value
+    edges = ua[off - 1, here], ua[last + 1, here]
+    for k in range(3):
+        left, right = arrived(k * kept, kept)
+        ua[off + 1 - k, here] += left
+        ua[last - 1 + k, here] += right
     half = kept // 2
     parts = [(GUARD, half), (GUARD + half, half)]
     laneh = lanes_of(half)
@@ -573,19 +681,21 @@
         for start, rows in parts:
             g[x + 2, pl.ds(start, rows)] = weight_of(c_in[x + 2, pl.ds(start - GUARD, rows)])
 
-    def source_of(x, start, rows):
-        at = pl.ds(start - GUARD, rows)
+    def source_of(x, start, rows, sweep):
         if 0 <= x < size_x:
-            return f_in[x, at]
-        k = -1 - x if x < 0 else x - size_x
-        left, right = arrived((5 + k) * kept + start - GUARD, rows)
-        return left if x < 0 else right
-
-    for source, target, margin in ((ua, ub, 1), (ub, ua, 2)):
-        for at in range(margin, size_x + 6 - margin):
+            return f_in[x, pl.ds(start - GUARD, rows)]
+        return arrived((3 + sweep) * kept + start - GUARD, rows)[0 if x < 0 else 1]
+
+    for at, edge, outward in ((1, edges[0], -1), (size_x + 4, edges[1], 1)):
+        for start, rows in parts:
+            center, total = around(ua, at, start, rows, laneh, LANES, outward < 0, outward > 0)
+            total = total + edge[start - GUARD : start - GUARD + rows]
+            ub[at, pl.ds(start, rows)] = 0.2 * center + g[at - 1, pl.ds(start, rows)] * total
+    for source, target in ((ua, ub), (ub, ua)):
+        for at in range(2, size_x + 4):
             for start, rows in parts:
                 center, total = around(source, at, start, rows, laneh, LANES)
-                total = total + source_of(at - off, start, rows)
+                total = total + source_of(at - off, start, rows, 0 if source is ua else 1)
                 target[at, pl.ds(start, rows)] = 0.2 * center + g[at - 1, pl.ds(start, rows)] * total
     lane_z = lanes_of(size_z)
     own = GUARD + KEEP
@@ -617,60 +727,82 @@
     deep = wide + 2 * GUARD
     rows1 = size_z // 4 + 2 * GUARD
     size1, size2 = size_x // 2, size_x // 4
-    message = (2 * wide + 2 * rows1, LANES)
+    box2 = (size2 + 10, 5, 8, LANES)
+    near = (40 + 7 * rows1, LANES)
+    message = (2 * wide + 2 * rows1 + 32, LANES)
     mxa, mxb = call(
-        coefficient_kernel, "coefficients", (message, message), (c, za, zb), [(size_x, deep, LANES)]
+        coefficient_kernel, "coefficients", (message, message), (c, za, zb),
+        [(size_x, deep, LANES), (size1, rows1 + 2 * GUARD, LANES)],
     )
     even_x, odd_x = pairs_of(nx)
     xa = lax.ppermute(mxa, "gx", even_x)
     xb = lax.ppermute(mxb, "gx", odd_x)
 
     kept = size_z + 2 * KEEP
-    margin = (7 * kept + 9 * rows1, LANES)
+    margin = (5 * kept, LANES)
     field = (size_x + 8, deep, LANES)
     field1 = (size1 + 10, rows1 + 2 * GUARD, LANES)
-    chunk, v, f, c, f1, c1, mua, mub = call(
+    chunk, mna, mnb, mua, mub, v, f, c, f1, c1, v1, v2, f2, c2 = call(
         down_kernel, "down",
         (
-            (2 * size2 + 4, 8, LANES),
+            (nx * nz // 2, 2, 8, LANES),
+            near,
+            near,
+            margin,
+            margin,
             (size_x + 4, kept, LANES),
             (size_x, kept, LANES),
             (size_x + 4, kept, LANES),
             (size1 + 4, rows1, LANES),
             (size1 + 6, rows1, LANES),
-            margin,
-            margin,
+            (2, rows1, LANES),
+            box2,
+            box2,
+            box2,
         ),
         (f, c, v, za, zb, xa, xb),
-        [field, field, field, field, (size_x, deep, LANES), field1, field1, field1, field1],
+        [field, field, field, field, (size_x, deep, LANES), field1, field1, field1, field1, box2, (size2 + 10, 8, LANES)],
+    )
+    own = lax.all_to_all(chunk, ("gx", "gy"), 0, 0, tiled=True)
+    mna, mnb = call(hold_kernel, "hold", (near, near), (mna, mnb, own))
+    other = lax.ppermute(own, "gc", [(0, 1), (1, 0)])
+    na = lax.ppermute(mna, "gx", even_x)
+    nb = lax.ppermute(mnb, "gx", odd_x)
+
+    own2, mua, mub = call(
+        complete_kernel, "complete", ((2 * size2, 8, LANES), margin, margin), (v2, f2, na, nb, mua, mub)
     )
     ua = lax.ppermute(mua, "gx", even_x)
     ub = lax.ppermute(mub, "gx", odd_x)
-
-    copies = jnp.broadcast_to(chunk, (nx * nz // 2, *chunk.shape))
-    own = lax.all_to_all(copies, ("gx", "gy"), 0, 0, tiled=True)
-    other = lax.ppermute(own, "gc", [(0, 1), (1, 0)])
-
-    grid2 = (size2 * nx + 8, nz + 2, 8, LANES)
+    z2a = lax.ppermute(own2, ("gy", "gc"), even_z)
+    z2b = lax.ppermute(own2, ("gy", "gc"), odd_z)
+    sides = (4 * size2 - 2, 8, LANES)
+    msa, msb = call(side_kernel, "sides", (sides, sides), (own2, z2a, z2b))
+    sa = lax.ppermute(msa, "gx", even_x)
+    sb = lax.ppermute(msb, "gx", odd_x)
+
     grid3 = (2 * nx + 8, nz + 2, 8, LANES)
     rows = coarse_inverse.shape[0]
-    window2, window3, e = call(
+    window3, e = call(
         functools.partial(coarse_kernel, nx, nz), "coarse",
-        ((3, size2 + 8, 3, 8, LANES), (3, 10, 3, 8, LANES), (nx * nz, rows)),
-        (own, other, coarse_inverse),
-        [*[grid2] * 5, *[grid3] * 5, (LANES, LANES), (COARSE**3 // LANES, LANES)],
+        ((3, 10, 3, 8, LANES), (nx * nz, rows)),
+        (own, other, coarse_inverse, msa),
+        [*[grid3] * 5, (LANES, LANES), (COARSE**3 // LANES, LANES)],
     )
     e = lax.all_to_all(e, ("gx", "gy", "gc"), 0, 0, tiled=True).reshape(COARSE**3 // LANES, LANES)
 
-    box2 = (size2 + 8, 5, 8, LANES)
+    near2 = (size2 + 8, 5, 8, LANES)
     box3 = (10, 5, 8, LANES)
+    (u3,) = call(
+        functools.partial(top_kernel, nx, nz), "top", (box3,), (e, window3), [grid3, box3, (LANES, LANES)]
+    )
     box = (size_x + 6, kept + 2 * GUARD, LANES)
     return call(
         functools.partial(up_kernel, nx, nz), "up",
         ((size_x, LANES, size_z), (size_x, LANES, size_z)),
-        (e, window2, window3, v, f, c, f1, c1, ua, ub),
+        (u3, own2, z2a, z2b, sa, sb, c2, v, f, c, f1, c1, v1, na, nb, ua, ub),
         [
-            grid3, box3, box3, (LANES, LANES), box2, box2,
+            near2, near2, near2,
             field1, field1, field1, field1, (size2 + 4, rows1, LANES),
             box, box, box, (size1 + 4, kept, LANES),
         ],

time: 104 us -> 89.6 us (0.86)
  waiting for transfers between devices: 21.7 us -> 9.2 us
  starting transfers between devices: 11.3 us -> 21.1 us
  Pallas kernels: 23.7 us -> 17.6 us
  local copies, waits for them, and re-layouts: 8.71 us -> 3.67 us
    ppermute x1, waiting for transfers between devices: 17.8 us -> 0.01 us  [local(): ua = lax.ppermute(mua, 'gx', even_x)]
    ppermute x0 -> x6, starting transfers between devices: none -> 10.6 us  [the longest x1 5.48 us: local(): sa = lax.ppermute(msa, 'gx', even_x)]
    pallas_call x5 -> x9, Pallas kernels: 23.7 us -> 17.6 us  [call(): pl.pallas_call(kernel, out_shape=shapes, in_specs=[pl.BlockSpec(memory_sp...]
    ppermute x0 -> x6, waiting for transfers between devices: none -> 5.19 us  [the longest x1 4.32 us: local(): na = lax.ppermute(mna, 'gx', even_x)]
    unnamed x24 -> x8, local copies, waits for them, and re-layouts: 8.64 us -> 3.67 us
    ppermute x1, starting transfers between devices: 0.91 us -> 4.97 us  [local(): ua = lax.ppermute(mua, 'gx', even_x)]
    all_to_all x1 -> x0, starting transfers between devices: 4.04 us -> none  [local(): lax.all_to_all(e, ('gx', 'gy', 'gc'), 0, 0, tiled=True)]
    all_to_all x1 -> x2, blocking collectives: 37.8 us -> 36.8 us  [the longest x1 25.9 us: local(): own = lax.all_to_all(chunk, ('gx', 'gy'), 0, 0, tiled=True)]
  transfers between devices with their start and end apart: 8 -> 13, of which waited for: 3 -> 4; matrix products, arithmetic and copies ran while one was open for 0% -> 0% of each run, Pallas kernels for 8% -> 3%
where the time goes in v2:
time: 89.6 us; the launch traced here: 89.1 us
  blocking collectives  36.8 us (41%)
  starting transfers between devices  21.1 us (24%)
  Pallas kernels  17.6 us (20%)
  waiting for transfers between devices  9.2 us (10%)
  local copies, waits for them, and re-layouts  3.67 us (4%)
    all_to_all x1, blocking collectives, local(): own = lax.all_to_all(chunk, ('gx', 'gy'), 0, 0, tiled=True)  25.9 us
    pallas_call x9, Pallas kernels, call(): pl.pallas_call(kernel, out_shape=shapes, in_specs=[pl.BlockSpec(memory_sp...  17.6 us
    all_to_all x1, blocking collectives, local(): lax.all_to_all(e, ('gx', 'gy', 'gc'), 0, 0, tiled=True)  10.9 us
    ppermute x1, starting transfers between devices, local(): sa = lax.ppermute(msa, 'gx', even_x)  5.48 us
    ppermute x1, starting transfers between devices, local(): ua = lax.ppermute(mua, 'gx', even_x)  4.97 us
    ppermute x1, waiting for transfers between devices, local(): na = lax.ppermute(mna, 'gx', even_x)  4.32 us
    unnamed x8, local copies, waits for them, and re-layouts  3.67 us
    ppermute x1, waiting for transfers between devices, local(): xa = lax.ppermute(mxa, 'gx', even_x)  3.33 us
  transfers between devices with their start and end apart: 13, of which 4 were waited for; matrix products, arithmetic and copies ran while one was open for 0% of the time, Pallas kernels for 3%

profile of v2, /device:TPU:0, one launch (start us, length us, event | category | flops | bytes accessed | tf_op | source)
XLA Modules:
  0.0 89.1 jit_solution(10265720090565579666)
XLA Ops:
  0.6 0.0 copy-start.1
  0.6 1.2 %copy-done.1 = f32[16,128,128]{2,1,0:T(8,128)S(1)} copy-done((f32[16,128,128]{2,1,0:T(8,128)S(1)}, f32[16,128,128]{2,1,0:T(8,128)}, u32[]{:S(2)}) %copy-start.1) | copy-done | bytes 1048600
  1.9 0.0 copy-start.2
  1.9 1.2 %copy-done.2 = f32[16,128,128]{2,1,0:T(8,128)S(1)} copy-done((f32[16,128,128]{2,1,0:T(8,128)S(1)}, f32[16,128,128]{2,1,0:T(8,128)}, u32[]{:S(2)}) %copy-start.2) | copy-done | bytes 1048600
  3.1 0.0 copy-start.3
  3.1 1.2 %copy-done.3 = f32[16,128,128]{2,1,0:T(8,128)S(1)} copy-done((f32[16,128,128]{2,1,0:T(8,128)S(1)}, f32[16,128,128]{2,1,0:T(8,128)}, u32[]{:S(2)}) %copy-start.3) | copy-done | bytes 1048600
  4.3 0.9 turn.1
  5.2 0.5 collective-permute-start
  5.7 0.7 collective-permute-start.1
  6.4 0.7 collective-permute-done.za
  7.1 0.0 collective-permute-done.1.zb
  7.1 0.5 coefficients.1
  7.6 2.9 %collective-permute-start.2 = (f32[448,128]{1,0:T(8,128)S(1)}, f32[448,128]{1,0:T(8,128)S(1)}, u32[]{:S(2)}, u32[]{:S(2)}) collective-permute-start(f32[448,128]{1,0:T(8,128)S(1)} %get-tuple-element.37), channel_id=1, source_target_pairs={{0,4},{4,0},{8,12},{12,8},{16,20},{20,16},{24,28},{28,24},{1,5},{5... | collective-permute-start | bytes 688136 | tf_op jit(solution)/shard_map/ppermute | solution.py:738
  10.5 0.7 collective-permute-start.3
  11.2 3.3 %collective-permute-done.2.xa = f32[448,128]{1,0:T(8,128)S(1)} collective-permute-done((f32[448,128]{1,0:T(8,128)S(1)}, f32[448,128]{1,0:T(8,128)S(1)}, u32[]{:S(2)}, u32[]{:S(2)}) %collective-permute-start.2) | collective-permute-done | bytes 229408 | tf_op jit(solution)/shard_map/ppermute | solution.py:738
  14.5 0.0 collective-permute-done.3.xb
  14.5 8.2 %down.1 = (f32[16,2,8,128]{3,2,1,0:T(8,128)S(1)}, f32[376,128]{1,0:T(8,128)S(1)}, f32[376,128]{1,0:T(8,128)S(1)}, f32[720,128]{1,0:T(8,128)S(1)}, f32[720,128]{1...) custom-call(f32[16,128,128]{2,1,0:T(8,128)S(1)} %get-tuple-element.3, ...), custom_call_target="tpu_custom_call" | custom-call | tf_op jit(solution)/shard_map/down/pallas_call | solution.py:127
  22.7 0.0 copy-start
  22.7 25.9 %all_to_all.16._.own = f32[16,2,8,128]{3,2,1,0:T(8,128)S(1)} all-to-all(f32[16,2,8,128]{3,2,1,0:T(8,128)S(1)} %get-tuple-element.39), channel_id=1, replica_groups=mesh['gx'=8,'gy'=2,'gc'=2] {'gx','gy'}, dimensions={0} | all-to-all | bytes 262144 | tf_op jit(solution)/shard_map/all_to_all | solution.py:766
  48.7 0.7 collective-permute-start.5
  49.4 0.7 collective-permute-start.6
  50.1 4.3 %collective-permute-done.5.near_a = f32[376,128]{1,0:T(8,128)S(1)} collective-permute-done((f32[376,128]{1,0:T(8,128)S(1)}, f32[376,128]{1,0:T(8,128)S(1)}, u32[]{:S(2)}, u32[]{:S(2)}) %collective-permute-start.5) | collective-permute-done | bytes 192544 | tf_op jit(solution)/shard_map/ppermute | solution.py:769
  54.4 0.0 collective-permute-done.6.near_b
  54.4 0.1 complete.1
  54.5 5.0 %collective-permute-start.11 = (f32[720,128]{1,0:T(8,128)S(1)}, f32[720,128]{1,0:T(8,128)S(1)}, u32[]{:S(2)}, u32[]{:S(2)}) collective-permute-start(f32[720,128]{1,0:T(8,128)S(1)} %get-tuple-element.60), channel_id=1, source_target_pairs={{0,4},{4,0},{8,12},{12,8},{16,20},{20,16},{24,28},{28,24},{1,5},{5... | collective-permute-start | bytes 1105928 | tf_op jit(solution)/shard_map/ppermute | solution.py:775
  59.4 0.7 collective-permute-start.12
  60.1 0.1 collective-permute-start.4
  60.2 0.7 collective-permute-start.8
  60.9 2.4 %collective-permute-start.7 = (f32[8,8,128]{2,1,0:T(8,128)S(1)}, f32[8,8,128]{2,1,0:T(8,128)S(1)}, u32[]{:S(2)}, u32[]{:S(2)}) collective-permute-start(f32[8,8,128]{2,1,0:T(8,128)S(1)} %get-tuple-element.48.own.own2), channel_id=1, source_target_pairs={{0,1},{1,0},{2,3},{3,2},{4,5},{5,4},{6,7},{7,6},{8,9},{9,8},{10,11... | collective-permute-start | bytes 98312 | tf_op jit(solution)/shard_map/ppermute | solution.py:777
  63.3 0.0 collective-permute-done.8.zb
  63.3 0.9 collective-permute-done.7.za
  64.2 0.7 collective-permute-start.10
  64.8 5.5 %collective-permute-start.9 = (f32[14,8,128]{2,1,0:T(8,128)S(1)}, f32[14,8,128]{2,1,0:T(8,128)S(1)}, u32[]{:S(2)}, u32[]{:S(2)}) collective-permute-start(f32[14,8,128]{2,1,0:T(8,128)S(1)} %get-tuple-element.49._), channel_id=1, source_target_pairs={{0,4},{4,0},{8,12},{12,8},{16,20},{20,16},{24,28},{28,24},{1,5},{5... | collective-permute-start | bytes 172040 | tf_op jit(solution)/shard_map/ppermute | solution.py:781
  70.3 0.0 collective-permute-done.4.other
  70.3 0.0 copy-done
  70.3 1.7 %coarse.1 = (f32[3,10,3,8,128]{4,3,2,1,0:T(8,128)S(1)}, f32[32,128]{1,0:T(8,128)S(1)}) custom-call(f32[16,2,8,128]{3,2,1,0:T(8,128)S(1)} %all_to_all.16._.own, f32[16,2,8,128]{3,2,1,0:T(8,128)S(1)} %collective-permute-done.4.other, f32[128,4096]{1,0:T(8,128)S(1)} %copy-done, f32[14,8,128]{2,1,0:T(8,128)S(1)} %get-tuple-element.49._), custom_call_target="tpu_custom_call" | custom-call | tf_op jit(solution)/shard_map/coarse/pallas_call | solution.py:127
  72.1 10.9 %all_to_all.17 = f32[32,1,128]{2,1,0:T(1,128)S(1)} all-to-all(f32[32,1,128]{2,1,0:T(1,128)S(1)} %bitcast.5), channel_id=1, replica_groups=mesh['gx'=8,'gy'=2,'gc'=2] {'gx','gy','gc'}, dimensions={0} | all-to-all | bytes 32768 | tf_op jit(solution)/shard_map/all_to_all | solution.py:792
  82.9 0.5 top.1.u3
  83.5 0.0 collective-permute-done.10.sides_b
  83.5 0.0 collective-permute-done.9.sides_a
  83.5 0.0 collective-permute-done.11.xa
  83.5 0.0 collective-permute-done.12.xb
  83.5 5.6 %up.1 = (f32[16,128,128]{2,1,0:T(8,128)}, f32[16,128,128]{2,1,0:T(8,128)}) custom-call(f32[10,5,8,128]{3,2,1,0:T(8,128)S(1)} %top.1.u3, f32[8,8,128]{2,1,0:T(8,128)S(1)} %get-tuple-element.48.own.own2, f32[8,8,128]{2,1,0:T(8,128)S(1)} %collective-permute-done.7.za, f32[8,8,128]{2,1,0:T(8,128)S(1)} %collective-permute-done.8.zb, ...), custom_call_target="tpu_custom_call" | custom-call | tf_op jit(solution)/shard_map/up/pallas_call | solution.py:127
  (2 shorter events, 0.0 us)
Async XLA Ops:
  0.6 1.2 %copy-start.1 = (f32[16,128,128]{2,1,0:T(8,128)S(1)}, f32[16,128,128]{2,1,0:T(8,128)}, u32[]{:S(2)}) copy-start(f32[16,128,128]{2,1,0:T(8,128)} %f_in.1) | copy-start | bytes 3145732
  1.9 1.2 %copy-start.2 = (f32[16,128,128]{2,1,0:T(8,128)S(1)}, f32[16,128,128]{2,1,0:T(8,128)}, u32[]{:S(2)}) copy-start(f32[16,128,128]{2,1,0:T(8,128)} %c_in.1) | copy-start | bytes 3145732
  3.1 1.2 %copy-start.3 = (f32[16,128,128]{2,1,0:T(8,128)S(1)}, f32[16,128,128]{2,1,0:T(8,128)}, u32[]{:S(2)}) copy-start(f32[16,128,128]{2,1,0:T(8,128)} %v_in.1) | copy-start | bytes 3145732
  5.2 1.9 %collective-permute-start = (f32[3,16,16,128]{3,2,1,0:T(8,128)S(1)}, f32[3,16,16,128]{3,2,1,0:T(8,128)S(1)}, u32[]{:S(2)}, u32[]{:S(2)}) collective-permute-start(f32[3,16,16,128]{3,2,1,0:T(8,128)S(1)} %get-tuple-element.35), channel_id=1, source_target_pairs={{0,1},{1,0},{2,3},{3,2},{4,5},{5,4},{6,7},{7,6},{8,9},{9,8},{10,11... | collective-permute-start | bytes 1179656 | tf_op jit(solution)/shard_map/ppermute | solution.py:723
  5.7 1.4 %collective-permute-start.1 = (f32[3,16,16,128]{3,2,1,0:T(8,128)S(1)}, f32[3,16,16,128]{3,2,1,0:T(8,128)S(1)}, u32[]{:S(2)}, u32[]{:S(2)}) collective-permute-start(f32[3,16,16,128]{3,2,1,0:T(8,128)S(1)} %get-tuple-element.36), channel_id=1, source_target_pairs={{1,2},{2,1},{5,6},{6,5},{9,10},{10,9},{13,14},{14,13},{17,18},{18,... | collective-permute-start | bytes 1179656 | tf_op jit(solution)/shard_map/ppermute | solution.py:724
  7.6 6.9 %collective-permute-start.2 = (f32[448,128]{1,0:T(8,128)S(1)}, f32[448,128]{1,0:T(8,128)S(1)}, u32[]{:S(2)}, u32[]{:S(2)}) collective-permute-start(f32[448,128]{1,0:T(8,128)S(1)} %get-tuple-element.37), channel_id=1, source_target_pairs={{0,4},{4,0},{8,12},{12,8},{16,20},{20,16},{24,28},{28,24},{1,5},{5... | collective-permute-start | bytes 688136 | tf_op jit(solution)/shard_map/ppermute | solution.py:738
  10.5 4.0 %collective-permute-start.3 = (f32[448,128]{1,0:T(8,128)S(1)}, f32[448,128]{1,0:T(8,128)S(1)}, u32[]{:S(2)}, u32[]{:S(2)}) collective-permute-start(f32[448,128]{1,0:T(8,128)S(1)} %get-tuple-element.38), channel_id=1, source_target_pairs={{4,8},{8,4},{12,16},{16,12},{20,24},{24,20},{5,9},{9,5},{13,17},{1... | collective-permute-start | bytes 688136 | tf_op jit(solution)/shard_map/ppermute | solution.py:739
  22.7 47.6 %copy-start = (f32[128,4096]{1,0:T(8,128)S(1)}, f32[128,4096]{1,0:T(8,128)}, u32[]{:S(2)}) copy-start(f32[128,4096]{1,0:T(8,128)} %inverse.1) | copy-start | bytes 6291460
  48.7 5.7 %collective-permute-start.5 = (f32[376,128]{1,0:T(8,128)S(1)}, f32[376,128]{1,0:T(8,128)S(1)}, u32[]{:S(2)}, u32[]{:S(2)}) collective-permute-start(f32[376,128]{1,0:T(8,128)S(1)} %get-tuple-element.44), channel_id=1, source_target_pairs={{0,4},{4,0},{8,12},{12,8},{16,20},{20,16},{24,28},{28,24},{1,5},{5... | collective-permute-start | bytes 577544 | tf_op jit(solution)/shard_map/ppermute | solution.py:769
  49.4 5.0 %collective-permute-start.6 = (f32[376,128]{1,0:T(8,128)S(1)}, f32[376,128]{1,0:T(8,128)S(1)}, u32[]{:S(2)}, u32[]{:S(2)}) collective-permute-start(f32[376,128]{1,0:T(8,128)S(1)} %get-tuple-element.45), channel_id=1, source_target_pairs={{4,8},{8,4},{12,16},{16,12},{20,24},{24,20},{5,9},{9,5},{13,17},{1... | collective-permute-start | bytes 577544 | tf_op jit(solution)/shard_map/ppermute | solution.py:770
  54.5 29.0 %collective-permute-start.11 = (f32[720,128]{1,0:T(8,128)S(1)}, f32[720,128]{1,0:T(8,128)S(1)}, u32[]{:S(2)}, u32[]{:S(2)}) collective-permute-start(f32[720,128]{1,0:T(8,128)S(1)} %get-tuple-element.60), channel_id=1, source_target_pairs={{0,4},{4,0},{8,12},{12,8},{16,20},{20,16},{24,28},{28,24},{1,5},{5... | collective-permute-start | bytes 1105928 | tf_op jit(solution)/shard_map/ppermute | solution.py:775
  59.4 24.0 %collective-permute-start.12 = (f32[720,128]{1,0:T(8,128)S(1)}, f32[720,128]{1,0:T(8,128)S(1)}, u32[]{:S(2)}, u32[]{:S(2)}) collective-permute-start(f32[720,128]{1,0:T(8,128)S(1)} %get-tuple-element.61), channel_id=1, source_target_pairs={{4,8},{8,4},{12,16},{16,12},{20,24},{24,20},{5,9},{9,5},{13,17},{1... | collective-permute-start | bytes 1105928 | tf_op jit(solution)/shard_map/ppermute | solution.py:776
  60.1 10.2 %collective-permute-start.4 = (f32[16,2,8,128]{3,2,1,0:T(8,128)S(1)}, f32[16,2,8,128]{3,2,1,0:T(8,128)S(1)}, u32[]{:S(2)}, u32[]{:S(2)}) collective-permute-start(f32[16,2,8,128]{3,2,1,0:T(8,128)S(1)} %all_to_all.16._.own), channel_id=1, source_target_pairs={{0,1},{1,0},{2,3},{3,2},{4,5},{5,4},{6,7},{7,6},{8,9},{9,8},{10,11... | collective-permute-start | bytes 393224 | tf_op jit(solution)/shard_map/ppermute | solution.py:768
  60.2 3.1 %collective-permute-start.8 = (f32[8,8,128]{2,1,0:T(8,128)S(1)}, f32[8,8,128]{2,1,0:T(8,128)S(1)}, u32[]{:S(2)}, u32[]{:S(2)}) collective-permute-start(f32[8,8,128]{2,1,0:T(8,128)S(1)} %get-tuple-element.48.own.own2), channel_id=1, source_target_pairs={{1,2},{2,1},{5,6},{6,5},{9,10},{10,9},{13,14},{14,13},{17,18},{18,... | collective-permute-start | bytes 98312 | tf_op jit(solution)/shard_map/ppermute | solution.py:778
  60.9 3.3 %collective-permute-start.7 = (f32[8,8,128]{2,1,0:T(8,128)S(1)}, f32[8,8,128]{2,1,0:T(8,128)S(1)}, u32[]{:S(2)}, u32[]{:S(2)}) collective-permute-start(f32[8,8,128]{2,1,0:T(8,128)S(1)} %get-tuple-element.48.own.own2), channel_id=1, source_target_pairs={{0,1},{1,0},{2,3},{3,2},{4,5},{5,4},{6,7},{7,6},{8,9},{9,8},{10,11... | collective-permute-start | bytes 98312 | tf_op jit(solution)/shard_map/ppermute | solution.py:777
  64.2 19.3 %collective-permute-start.10 = (f32[14,8,128]{2,1,0:T(8,128)S(1)}, f32[14,8,128]{2,1,0:T(8,128)S(1)}, u32[]{:S(2)}, u32[]{:S(2)}) collective-permute-start(f32[14,8,128]{2,1,0:T(8,128)S(1)} %get-tuple-element.52), channel_id=1, source_target_pairs={{4,8},{8,4},{12,16},{16,12},{20,24},{24,20},{5,9},{9,5},{13,17},{1... | collective-permute-start | bytes 172040 | tf_op jit(solution)/shard_map/ppermute | solution.py:782
  64.8 18.6 %collective-permute-start.9 = (f32[14,8,128]{2,1,0:T(8,128)S(1)}, f32[14,8,128]{2,1,0:T(8,128)S(1)}, u32[]{:S(2)}, u32[]{:S(2)}) collective-permute-start(f32[14,8,128]{2,1,0:T(8,128)S(1)} %get-tuple-element.49._), channel_id=1, source_target_pairs={{0,4},{4,0},{8,12},{12,8},{16,20},{20,16},{24,28},{28,24},{1,5},{5... | collective-permute-start | bytes 172040 | tf_op jit(solution)/shard_map/ppermute | solution.py:781

commit v3 on v2

--- a/solution.py
+++ b/solution.py
@@ -15,6 +15,7 @@
 LANES = 128
 DEEP = 16
 KEEP = 8
+SENT = 4
 GUARD = 8
 MIB = 1 << 20
 
@@ -118,34 +119,58 @@
     target[at, 3] = jnp.where(lane < 32, past, 0.0)
 
 
-def call(kernel, name, outs, args, scratch=(), results=None):
+def call(kernel, name, outs, args, scratch=(), far_args=(), far_outs=(), copies=0, results=False, micros=1):
     limit = sum(4 * math.prod(s) for s in scratch) + 6 * MIB
-    args = [pltpu.with_memory_space_constraint(a, pltpu.VMEM) for a in args]
-    shapes = [
-        jax.ShapeDtypeStruct(s, F32) if results else pltpu.VMEM(s, F32) for s in outs
-    ]
+    spaces_in = [pltpu.HBM if k in far_args else pltpu.VMEM for k in range(len(args))]
+    spaces_out = [pltpu.HBM if k in far_outs else pltpu.VMEM for k in range(len(outs))]
+    args = [pltpu.with_memory_space_constraint(a, space) for a, space in zip(args, spaces_in, strict=True)]
     return pl.pallas_call(
         kernel,
-        out_shape=shapes,
-        in_specs=[pl.BlockSpec(memory_space=pltpu.VMEM)] * len(args),
-        out_specs=[pl.BlockSpec(memory_space=pltpu.VMEM)] * len(outs),
-        scratch_shapes=[pltpu.VMEM(s, F32) for s in scratch],
+        out_shape=[
+            jax.ShapeDtypeStruct(s, F32) if results else space(s, F32)
+            for s, space in zip(outs, spaces_out, strict=True)
+        ],
+        in_specs=[pl.BlockSpec(memory_space=space) for space in spaces_in],
+        out_specs=[pl.BlockSpec(memory_space=space) for space in spaces_out],
+        scratch_shapes=[pltpu.VMEM(s, F32) for s in scratch] + [pltpu.SemaphoreType.DMA((copies,))] * (copies > 0),
         compiler_params=pltpu.CompilerParams(vmem_limit_bytes=limit),
+        cost_estimate=pl.CostEstimate(flops=0, bytes_accessed=3_000_000 * micros, transcendentals=0),
         name=name,
     )(*args)
 
 
-def turn_kernel(f_in, c_in, v_in, f_out, c_out, v_out, to_a, to_b):
+def edge_rows(source, to_a, to_b):
     odd = lax.axis_index("gc")
-    size_x, _, size_z = f_in.shape
-    far = size_z - DEEP
-    start_a = pl.multiple_of((1 - odd) * far, DEEP)
-    start_b = pl.multiple_of(odd * far, DEEP)
-    for which, (source, target) in enumerate(((f_in, f_out), (c_in, c_out), (v_in, v_out))):
-        for x in range(size_x):
-            target[x] = source[x].T
-        to_a[which] = target[:, pl.ds(start_a, DEEP), :]
-        to_b[which] = target[:, pl.ds(start_b, DEEP), :]
+    far = source.shape[1] - DEEP
+    to_a[...] = source[:, pl.ds(pl.multiple_of((1 - odd) * far, DEEP), DEEP), :]
+    to_b[...] = source[:, pl.ds(pl.multiple_of(odd * far, DEEP), DEEP), :]
+
+
+def turn_kernel(*refs):
+    *refs, held, arrivals = refs
+    count = (len(refs) - 2) // 2
+    sources, targets, (to_a, to_b) = refs[:count], refs[count : 2 * count], refs[2 * count :]
+    piece = targets[0].shape[0] // 4
+    copies = []
+    for which, source in enumerate(sources):
+        for k in range(4):
+            planes = pl.ds(k * piece, piece)
+            copies.append(
+                pltpu.make_async_copy(source.at[planes], held.at[which, planes], arrivals.at[4 * which + k])
+            )
+            copies[-1].start()
+    for which, target in enumerate(targets):
+        for k in range(4):
+            copies[4 * which + k].wait()
+            for x in range(k * piece, (k + 1) * piece):
+                target[x] = held[which, x].T
+        edge_rows(target, to_a.at[which], to_b.at[which])
+
+
+def turn_again_kernel(v_in, _, v_out, to_a, to_b):
+    for x in range(v_out.shape[0]):
+        v_out[x] = v_in[x].T
+    edge_rows(v_out, to_a, to_b)
 
 
 def fill_rows(target, at, own, low, high):
@@ -164,10 +189,10 @@
     here1 = pl.ds(GUARD, rows1)
     lane, lane8, sub8 = lanes_of(rows1), lanes_of(8), subs_of(8)
     for x in range(size_x):
-        low = jnp.where(odd_z, za[1, x], zb[1, x])
-        high = jnp.where(odd_z, zb[1, x], za[1, x])
+        low = jnp.where(odd_z, za[0, x], zb[0, x])
+        high = jnp.where(odd_z, zb[0, x], za[0, x])
         fill_rows(padded, x, c_in[x], low, high)
-    for x in range(1, 7):
+    for x in range(size_x // 2):
         c1[x, here1] = 0.125 * halve_two(padded, (2 * x, 2 * x + 1), lane, GUARD, rows1)
     sides = []
     for order, order1 in ((range(size_x), range(8)), (range(size_x - 1, -1, -1), range(7, -1, -1))):
@@ -185,10 +210,10 @@
         start += left.shape[0]
 
 
-def down_kernel(
-    f_in, c_in, v_in, za, zb, xa, xb,
-    chunk, near_a, near_b, to_a, to_b, v_out, f_out, c_out, f1_out, c1_out, v1_out, v2, f2, c2,
-    va, vb, c, g, f, f1, c1, u1, w1, u2, r2,
+def inner_kernel(
+    f_in, v_in, c, za, zb, ya, yb,
+    f, v2, edges, f1, to_a, to_b, later_a, later_b, f_far, c_far,
+    va, vb, g, r, arrivals,
 ):
     odd_z = lax.axis_index("gc") == 1
     even_x = lax.axis_index("gx") % 2 == 0
@@ -196,78 +221,149 @@
     wide = size_z + 2 * DEEP
     half = wide // 2
     parts = [(GUARD, half), (GUARD + half, half)]
-    off = 4
-    last = size_x + off - 1
+    last = size_x - 1
     lane = lanes_of(half)
     zeros8 = jnp.zeros((GUARD, LANES), F32)
 
-    for which, (source, target, shift) in enumerate(((f_in, f, 0), (c_in, c, off), (v_in, va, off))):
+    kept = pl.ds(GUARD + DEEP - KEEP, size_z + 2 * KEEP)
+    copies = [pltpu.make_async_copy(c.at[:, kept], c_far, arrivals.at[0])]
+    copies[0].start()
+    for source, target, a, b in ((f_in, f, za.at[1], zb.at[1]), (v_in, va, ya, yb)):
         for x in range(size_x):
-            low = jnp.where(odd_z, za[which, x], zb[which, x])
-            high = jnp.where(odd_z, zb[which, x], za[which, x])
-            fill_rows(target, x + shift, source[x], low, high)
-    for ref in (va, vb):
-        for at in range(2, size_x + 6):
+            low = jnp.where(odd_z, a[x], b[x])
+            high = jnp.where(odd_z, b[x], a[x])
+            fill_rows(target, x, source[x], low, high)
+        if target is f:
+            copies.append(pltpu.make_async_copy(f.at[:, kept], f_far, arrivals.at[1]))
+            copies[1].start()
+    for ref in (va, vb, v2):
+        for x in range(size_x):
+            ref[x, pl.ds(0, GUARD)] = zeros8
+            ref[x, pl.ds(GUARD + wide, GUARD)] = zeros8
+    for x in range(size_x):
+        for start, rows in parts:
+            here = pl.ds(start, rows)
+            g[x, here] = weight_of(c[x, here])
+    for source, target in ((va, vb), (vb, v2)):
+        for x in range(size_x):
+            for start, rows in parts:
+                here = pl.ds(start, rows)
+                center, total = around(source, x, start, rows, lane, LANES, x > 0, x < last)
+                target[x, here] = 0.2 * center + g[x, here] * (total + f[x, here])
+    for x in range(2, last - 1):
+        for start, rows in parts:
+            here = pl.ds(start, rows)
+            center, total = around(v2, x, start, rows, lane, LANES)
+            r[x, here] = total + f[x, here] - (6.0 + c[x, here]) * center
+    rows1 = size_z // 4 + 2 * GUARD
+    lane1 = lanes_of(rows1)
+    for x in range(1, size_x // 2 - 1):
+        f1[x - 1] = 0.5 * halve_two(r, (2 * x, 2 * x + 1), lane1, GUARD, rows1)
+    edges[0], edges[1], edges[2], edges[3] = va[0], va[last], vb[0], vb[last]
+
+    sent = size_z + 2 * SENT
+    first = GUARD + DEEP - SENT
+    here = pl.ds(first, sent)
+    lane = lanes_of(sent)
+    sides = []
+    for edge, second in ((0, 1), (last, last - 1)):
+        center, total = around(v2, second, first, sent, lane, LANES, second != 1, second == 1)
+        swept = 0.2 * center + g[second, here] * (total + f[second, here])
+        source = f[edge, here]
+        sides.append((va[edge, here], vb[edge, here], source + vb[second, here], source + center, source + swept))
+    for k, (left, right) in enumerate(zip(*sides, strict=True)):
+        a, b, rows = (to_a, to_b, pl.ds(k * sent, sent)) if k < 3 else (later_a, later_b, pl.ds((k - 3) * sent, sent))
+        a[rows] = jnp.where(even_x, right, left)
+        b[rows] = jnp.where(even_x, left, right)
+    for copy in copies:
+        copy.wait()
+
+
+def outer_kernel(
+    f, c, v2_in, edges, f1_in, c1_in, xa, xb,
+    chunk, near_a, near_b, to_a, to_b, v_far, sides_far, f1_far, c1_far, v1_out, level2, c2_out,
+    v, c_out, v1, r, f1, c1, u1, w1, u2, r2, v2, f2, c2, arrivals,
+):
+    even_x = lax.axis_index("gx") % 2 == 0
+    size_x = f.shape[0]
+    size_z = f.shape[1] - 2 * DEEP - 2 * GUARD
+    wide = size_z + 2 * DEEP
+    half = wide // 2
+    parts = [(GUARD, half), (GUARD + half, half)]
+    lane = lanes_of(half)
+    zeros8 = jnp.zeros((GUARD, LANES), F32)
+
+    copies = []
+
+    def keep(source, target):
+        copies.append(pltpu.make_async_copy(source, target, arrivals.at[len(copies)]))
+        copies[-1].start()
+
+    for x in range(size_x):
+        v[x + 2] = v2_in[x]
+    for ref, planes in ((v, (0, 1, size_x + 2, size_x + 3)), (v1, (0, 1))):
+        for at in planes:
             ref[at, pl.ds(0, GUARD)] = zeros8
             ref[at, pl.ds(GUARD + wide, GUARD)] = zeros8
     for k in range(2):
-        rows = pl.ds(k * wide, wide)
-        c[off - 1 - k, pl.ds(GUARD, wide)] = jnp.where(even_x, xb[rows], xa[rows])
-        c[last + 1 + k, pl.ds(GUARD, wide)] = jnp.where(even_x, xa[rows], xb[rows])
-    for at in range(off - 2, last + 3):
-        for start, rows in parts:
-            g[at, pl.ds(start, rows)] = weight_of(c[at, pl.ds(start, rows)])
-
-    for at in range(off - 1, last + 2):
+        rows, here = pl.ds(k * wide, wide), pl.ds(GUARD, wide)
+        c_out[1 - k, here] = jnp.where(even_x, xb[rows], xa[rows])
+        c_out[2 + k, here] = jnp.where(even_x, xa[rows], xb[rows])
+    last = size_x - 1
+    for side, (edge, inward) in enumerate(((0, 1), (last, -1))):
+        at = edge + 2
+        beside, past = (1, 0) if side == 0 else (2, 3)
         for start, rows in parts:
             here = pl.ds(start, rows)
-            if at < off:
-                vb[at, here] = g[at, here] * va[off, here]
-            elif at > last:
-                vb[at, here] = g[at, here] * va[last, here]
-            else:
-                center, total = around(va, at, start, rows, lane, LANES, at > off, at < last)
-                vb[at, here] = 0.2 * center + g[at, here] * (total + f[at - off, here])
-    for at in range(off - 2, last + 3):
+            v1[side, here] = weight_of(c_out[beside, here]) * edges[side, here]
         for start, rows in parts:
             here = pl.ds(start, rows)
-            if at == off - 2:
-                va[at, here] = g[at, here] * vb[at + 1, here]
-            elif at == last + 2:
-                va[at, here] = g[at, here] * vb[at - 1, here]
-            else:
-                center, total = around(vb, at, start, rows, lane, LANES, at > off - 1, at < last + 1)
-                if off <= at <= last:
-                    total = total + f[at - off, here]
-                va[at, here] = 0.2 * center + g[at, here] * total
-    for at in range(off - 3, last + 4):
+            center, total = around(v1, side, start, rows, lane, LANES, False, False)
+            v[at - inward, here] = 0.2 * center + weight_of(c_out[beside, here]) * (total + edges[2 + side, here])
+            v[at - 2 * inward, here] = weight_of(c_out[past, here]) * center
+            v[at, here] += weight_of(c[edge, here]) * center
+        base = 0 if side == 0 else 11
         for start, rows in parts:
             here = pl.ds(start, rows)
-            if at == off - 3:
-                vb[at, here] = va[at + 1, here]
-            elif at == last + 3:
-                vb[at, here] = va[at - 1, here]
-            else:
-                center, total = around(va, at, start, rows, lane, LANES, at > off - 2, at < last + 2)
-                if off <= at <= last:
-                    total = total + f[at - off, here]
-                vb[at, here] = total - (6.0 + c[at, here]) * center
+            r[base + inward, here] = v[at - 2 * inward, here]
+            for k in range(-2, 2):
+                plane = at + k * inward
+                center, total = around(
+                    v, plane, start, rows, lane, LANES, not (side == 0 and k == -2), not (side == 1 and k == -2)
+                )
+                if k >= 0:
+                    total = total + f[plane - 2, here]
+                    weight = 6.0 + c[plane - 2, here]
+                else:
+                    weight = 6.0 + c_out[beside if k == -1 else past, here]
+                r[base + (4 + k) * inward, here] = total - weight * center
+
+    kept = pl.ds(GUARD + DEEP - KEEP, size_z + 2 * KEEP)
+    keep(v.at[:, kept], v_far)
+    keep(c_out.at[:, kept], sides_far)
 
     rows1 = size_z // 4 + 2 * GUARD
     size1 = size_x // 2
     off1 = 5
     here1 = pl.ds(GUARD, rows1)
     lane1 = lanes_of(rows1)
-    for x in range(-2, size1 + 2):
-        planes = [at for at in (2 * x + off, 2 * x + off + 1) if off - 3 <= at <= last + 3]
-        f1[x + off1, here1] = 0.5 * halve_two(vb, planes, lane1, GUARD, rows1)
-    for x in range(-1, size1 + 1):
-        c1[x + off1, here1] = 0.125 * halve_two(c, (2 * x + off, 2 * x + off + 1), lane1, GUARD, rows1)
+    for x in range(1, size1 - 1):
+        f1[x + off1, here1] = f1_in[x - 1]
+    for x, planes in (
+        (-2, (1,)), (-1, (2, 3)), (0, (4, 5)), (size1 - 1, (6, 7)), (size1, (8, 9)), (size1 + 1, (10,))
+    ):
+        f1[x + off1, here1] = 0.5 * halve_two(r, planes, lane1, GUARD, rows1)
+    for x in range(size1):
+        c1[x + off1, here1] = c1_in[x, here1]
+    c1[off1 - 1, here1] = 0.125 * halve_two(c_out, (0, 1), lane1, GUARD, rows1)
+    c1[off1 + size1, here1] = 0.125 * halve_two(c_out, (2, 3), lane1, GUARD, rows1)
     for k in range(2):
         rows = pl.ds(2 * wide + k * rows1, rows1)
         c1[off1 - 2 - k, here1] = jnp.where(even_x, xb[rows], xa[rows])
         c1[off1 + size1 + 1 + k, here1] = jnp.where(even_x, xa[rows], xb[rows])
     low1, high1 = off1 - 2, off1 + size1 + 1
+    keep(f1.at[pl.ds(off1 - 2, size1 + 4), here1], f1_far)
+    keep(c1.at[pl.ds(off1 - 3, size1 + 6), here1], c1_far)
     for at in range(low1 - 1, high1 + 2):
         for ref in (u1, w1):
             ref[at, pl.ds(0, GUARD)] = zeros8
@@ -342,60 +438,40 @@
     pairs += [(f2, 2, off2 - k, off2 + size2 - 1 + k) for k in (1, 2)]
     pairs += [(f1, here1, off1 + k, off1 + size1 - 1 - k) for k in (-2, -1, 0, 1, 2)]
     pairs += [(w1, here1, off1 + k, off1 + size1 - 1 - k) for k in (2, 3)]
-    start = 0
-    for ref, rows, at_left, at_right in pairs:
+    for k, (ref, rows, at_left, at_right) in enumerate(pairs):
         left, right = ref[at_left, rows], ref[at_right, rows]
-        target = pl.ds(start, left.shape[0])
-        near_a[target] = jnp.where(even_x, right, left)
-        near_b[target] = jnp.where(even_x, left, right)
-        start += left.shape[0]
-
-    inner = pl.ds(GUARD + DEEP - KEEP, size_z + 2 * KEEP)
-    v_out[...] = va[pl.ds(off - 2, size_x + 4), inner]
-    c_out[...] = c[pl.ds(off - 2, size_x + 4), inner]
-    f_out[...] = f[:, inner]
-    f1_out[...] = f1[pl.ds(off1 - 2, size1 + 4), here1]
-    c1_out[...] = c1[pl.ds(off1 - 3, size1 + 6), here1]
+        a, b, at = (near_a, near_b, 8 * k) if k < 5 else (to_a, to_b, (k - 5) * rows1)
+        target = pl.ds(at, left.shape[0])
+        a[target] = jnp.where(even_x, right, left)
+        b[target] = jnp.where(even_x, left, right)
+
+    for at in range(size2 + 6):
+        level2[at] = v2[at + 2, 2]
+    for at in range(size2 + 4):
+        level2[size2 + 6 + at] = f2[at + 3, 2]
+    c2_out[...] = c2[pl.ds(2, size2 + 6), pl.ds(1, 3)]
     v1_out[0] = w1[off1 - 3, here1]
     v1_out[1] = w1[off1 + size1 + 2, here1]
-
-    kept = size_z + 2 * KEEP
-    lane = lanes_of(kept)
-    first = GUARD + DEEP - KEEP
-    sides = []
-    for edge, inward in ((off, 1), (last, -1)):
-        second = edge + inward
-        center, total = around(va, second, first, kept, lane, LANES)
-        swept = 0.2 * center + g[second, inner] * (total + f[second - off, inner])
-        source = f[edge - off, inner]
-        sides.append(
-            (va[edge - 2 * inward, inner], va[edge - inward, inner], va[edge, inner], source + center, source + swept)
-        )
-    for k, (left, right) in enumerate(zip(*sides, strict=True)):
-        rows = pl.ds(k * kept, kept)
-        to_a[rows] = jnp.where(even_x, right, left)
-        to_b[rows] = jnp.where(even_x, left, right)
-
-
-def hold_kernel(a, b, _, out_a, out_b):
-    out_a[...] = a[...]
-    out_b[...] = b[...]
-
-
-def complete_kernel(v2, f2, near_a, near_b, to_a, to_b, own, out_a, out_b):
+    for copy in copies:
+        copy.wait()
+
+
+def meet_kernel(level2, xa, xb, level1_a, level1_b, later_a, later_b, _, __, ___, own, to_a, to_b):
     even_x = lax.axis_index("gx") % 2 == 0
     size2 = own.shape[0] // 2
-    planes = [ref[5 + x, 2] for ref in (v2, f2) for x in range(size2)]
+    planes = [level2[3 + x] for x in range(size2)] + [level2[size2 + 8 + x] for x in range(size2)]
     for k, (base, step) in enumerate(((0, 0), (0, 1), (0, 2), (size2, 0), (size2, 1))):
         rows = pl.ds(8 * k, 8)
-        left = jnp.where(even_x, near_b[rows], near_a[rows])
-        right = jnp.where(even_x, near_a[rows], near_b[rows])
+        left = jnp.where(even_x, xb[rows], xa[rows])
+        right = jnp.where(even_x, xa[rows], xb[rows])
         planes[base + step] = planes[base + step] + left
         planes[base + size2 - 1 - step] = planes[base + size2 - 1 - step] + right
     for k, plane in enumerate(planes):
         own[k] = plane
-    out_a[...] = to_a[...]
-    out_b[...] = to_b[...]
+    size = level1_a.shape[0]
+    for first, second, target in ((level1_a, later_a, to_a), (level1_b, later_b, to_b)):
+        target[pl.ds(0, size)] = first[...]
+        target[pl.ds(size, second.shape[0])] = second[...]
 
 
 def past_tiles(za, zb, k, odd_z, lane):
@@ -428,13 +504,19 @@
 
 
 def coarse_kernel(
-    nx, nz, own, other, inverse, _,
+    nx, nz, own, other, inverse_far, _,
     window3, e_out,
-    v3, f3, g3, c3, u3, turned, flat,
+    v3, f3, g3, c3, u3, turned, flat, inverse, arrivals,
 ):
     core = lax.axis_index("gc")
     ny = nz // 2
     lane, sub = lanes_of(8), subs_of(8)
+    copies = []
+    piece = inverse.shape[0] // 4
+    for k in range(4):
+        rows = pl.ds(k * piece, piece)
+        copies.append(pltpu.make_async_copy(inverse_far.at[rows], inverse.at[rows], arrivals.at[k]))
+        copies[k].start()
     for ref in (v3, f3, g3, u3):
         ref[...] = jnp.zeros(ref.shape, F32)
 
@@ -505,6 +587,8 @@
         for t in range(3):
             window3[k, :, t] = ref[pl.ds(2 * at_x, 10), at_z + t]
 
+    for copy in copies:
+        copy.wait()
     total = None
     for t in range(inverse.shape[1] // LANES):
         piece = inverse[:, t * LANES : (t + 1) * LANES] * flat[t : t + 1]
@@ -515,7 +599,7 @@
     e_out[...] = jnp.broadcast_to(column, (inverse.shape[0], width)).T[:copies]
 
 
-def top_kernel(nx, nz, e, window3, u3, lifted3, w3, turned):
+def top_level(nx, nz, e, window3, u3, lifted3, w3, turned):
     at_x = lax.axis_index("gx")
     at_z = 2 * lax.axis_index("gy") + lax.axis_index("gc")
     lane, sub = lanes_of(8), subs_of(8)
@@ -550,15 +634,21 @@
 
 
 def up_kernel(
-    nx, nz, u3, own2, za, zb, sides_a, sides_b, c2, v_in, f_in, c_in, f1_in, c1_in, v1_in, near_a, near_b, xa, xb,
+    nx, nz, e, window3, own2, za, zb, sides_a, sides_b, c2, v_far, f_far, c_far, sides_far, f1_far, c1_far, v1_in, xa, xb, later_a, later_b,
     pressure, residual,
-    u2, w2, f2, f1, c1, u1, w1, lift1, ua, ub, g, lift0,
+    u3, lifted3, w3, turned, u2, w2, f2, f1, c1, u1, w1, lift1, ua, ub, g, lift0, before_in, after_in, sources, v_in, f_in, c_in, c_sides, f1_in, c1_in, arrivals,
 ):
     even_x = lax.axis_index("gx") % 2 == 0
     lane, sub = lanes_of(8), subs_of(8)
     zeros8 = jnp.zeros((GUARD, LANES), F32)
+    pairs = (f1_far, f1_in), (c1_far, c1_in), (sides_far, c_sides), (c_far, c_in), (v_far, v_in), (f_far, f_in)
+    copies = [pltpu.make_async_copy(*pair, arrivals.at[k]) for k, pair in enumerate(pairs)]
+    for copy in copies:
+        copy.start()
     for ref in (u2, w2, f2):
         ref[...] = jnp.zeros(ref.shape, F32)
+
+    top_level(nx, nz, e, window3, u3, lifted3, w3, turned)
 
     odd_z = lax.axis_index("gc") == 1
     size2 = own2.shape[0] // 2
@@ -581,7 +671,7 @@
         for x in range(margin, planes2 - margin):
             for t in (1, 2, 3):
                 center, total = around_tile(source, x, t, 1, lane, sub)
-                target[x, t] = 0.2 * center + weight_of(c2[x + 1, t]) * (total + f2[x, t])
+                target[x, t] = 0.2 * center + weight_of(c2[x - 1, t - 1]) * (total + f2[x, t])
 
     rows1 = f1_in.shape[1]
     size1 = 2 * size2
@@ -612,13 +702,14 @@
         a, b = a[pl.ds(start, rows)], b[pl.ds(start, rows)]
         return jnp.where(even_x, b, a), jnp.where(even_x, a, b)
 
+    copies[0].wait()
+    copies[1].wait()
     for x in range(-2, size1 + 2):
         f1[x + off1, here1] = f1_in[x + 2]
     for x in range(-3, size1 + 3):
         c1[x + off1, here1] = weight_of(c1_in[x + 3])
-    base1 = 40
     for k in range(7):
-        left, right = arrived(base1 + k * rows1, rows1, near_a, near_b)
+        left, right = arrived(k * rows1, rows1, later_a, later_b)
         if k < 4:
             f1[off1 + 1 - k, here1] += left
             f1[off1 + size1 - 2 + k, here1] += right
@@ -664,46 +755,61 @@
         for at in range(size_x + 6):
             ref[at, pl.ds(0, GUARD)] = zeros8
             ref[at, pl.ds(GUARD + kept, GUARD)] = zeros8
+    for copy in copies[2:]:
+        copy.wait()
+    shift = -GUARD
     for x in range(-3, size_x + 3):
         value = lift0[(x + 4) // 2]
         if -2 <= x <= size_x + 1:
-            value = value + v_in[x + 2]
+            value = value + v_in[x + 2, pl.ds(GUARD + shift, kept)]
         ua[x + off, here] = value
-    edges = ua[off - 1, here], ua[last + 1, here]
-    for k in range(3):
-        left, right = arrived(k * kept, kept)
-        ua[off + 1 - k, here] += left
-        ua[last - 1 + k, here] += right
     half = kept // 2
     parts = [(GUARD, half), (GUARD + half, half)]
     laneh = lanes_of(half)
+    beyond = {-2: 0, -1: 1, size_x: 2, size_x + 1: 3}
     for x in range(-2, size_x + 2):
         for start, rows in parts:
-            g[x + 2, pl.ds(start, rows)] = weight_of(c_in[x + 2, pl.ds(start - GUARD, rows)])
-
-    def source_of(x, start, rows, sweep):
-        if 0 <= x < size_x:
-            return f_in[x, pl.ds(start - GUARD, rows)]
-        return arrived((3 + sweep) * kept + start - GUARD, rows)[0 if x < 0 else 1]
-
-    for at, edge, outward in ((1, edges[0], -1), (size_x + 4, edges[1], 1)):
-        for start, rows in parts:
-            center, total = around(ua, at, start, rows, laneh, LANES, outward < 0, outward > 0)
-            total = total + edge[start - GUARD : start - GUARD + rows]
-            ub[at, pl.ds(start, rows)] = 0.2 * center + g[at - 1, pl.ds(start, rows)] * total
-    for source, target in ((ua, ub), (ub, ua)):
-        for at in range(2, size_x + 4):
+            at = pl.ds(start + shift, rows)
+            g[x + 2, pl.ds(start, rows)] = weight_of(c_sides[beyond[x], at] if x in beyond else c_in[x, at])
+
+    sent = size_z + 2 * SENT
+    begin = GUARD + KEEP - SENT
+    taken = pl.ds(begin, sent)
+    lane_s = lanes_of(sent)
+    for ref in (before_in, after_in, sources):
+        ref[...] = jnp.zeros(ref.shape, F32)
+    messages = [arrived(k * sent, sent) for k in range(3)]
+    messages += [arrived(7 * rows1 + k * sent, sent, later_a, later_b) for k in range(2)]
+    for side, (edge, inward) in enumerate(((off, 1), (last, -1))):
+        before, after, source0, source1, source2 = (message[side] for message in messages)
+        before_in[side, taken] = g[edge - 1, taken] * before
+        after_in[side, taken] = after
+        sources[side, taken] = source1
+        sources[2 + side, taken] = source2
+        center, total = around(before_in, side, begin, sent, lane_s, LANES, False, False)
+        ua[edge, taken] += 0.2 * center + g[edge - 1, taken] * (total + after)
+        ua[edge + inward, taken] += g[edge + inward - 1, taken] * center
+        _, total = around(after_in, side, begin, sent, lane_s, LANES, False, False)
+        ua[edge - inward, taken] += 0.2 * after + g[edge - inward - 1, taken] * (total + source0 + center)
+
+    for sweep, (origin, target) in enumerate(((ua, ub), (ub, ua))):
+        for at in range(1 + sweep, size_x + 5 - sweep):
             for start, rows in parts:
-                center, total = around(source, at, start, rows, laneh, LANES)
-                total = total + source_of(at - off, start, rows, 0 if source is ua else 1)
+                center, total = around(origin, at, start, rows, laneh, LANES)
+                x = at - off
+                if 0 <= x < size_x:
+                    total = total + f_in[x, pl.ds(start + shift, rows)]
+                elif x in (-1, size_x):
+                    total = total + sources[2 * sweep + (x > 0), pl.ds(start, rows)]
                 target[at, pl.ds(start, rows)] = 0.2 * center + g[at - 1, pl.ds(start, rows)] * total
     lane_z = lanes_of(size_z)
     own = GUARD + KEEP
     for x in range(size_x):
         center, total = around(ua, x + off, own, size_z, lane_z, LANES)
-        total = total + f_in[x, pl.ds(KEEP, size_z)]
+        mine = pl.ds(own + shift, size_z)
+        total = total + f_in[x, mine]
         pressure[x] = center.T
-        residual[x] = (total - (6.0 + c_in[x + 2, pl.ds(KEEP, size_z)]) * center).T
+        residual[x] = (total - (6.0 + c_in[x, mine]) * center).T
 
 
 def pairs_of(count):
@@ -712,68 +818,80 @@
     return even, odd
 
 
+def gather(copies, axes):
+    always = lax.optimization_barrier(jnp.int32(1)) > 0
+    return lax.cond(always, lambda x: lax.all_to_all(x, axes, 0, 0, tiled=True), lambda x: x, copies)
+
+
 def local(nx, nz, right_side, reaction, initial, coarse_inverse):
     size_x, _, size_z = right_side.shape
+    size1, size2 = size_x // 2, size_x // 4
+    wide, kept, sent = (size_z + 2 * rows for rows in (DEEP, KEEP, SENT))
+    deep = wide + 2 * GUARD
+    rows1 = size_z // 4 + 2 * GUARD
     brick = (size_x, size_z, LANES)
-    slab = (3, size_x, DEEP, LANES)
-    f, c, v, mza, mzb = call(
-        turn_kernel, "turn", (brick, brick, brick, slab, slab), (right_side, reaction, initial)
+    padded = (size_x, deep, LANES)
+    padded1 = (size1, rows1 + 2 * GUARD, LANES)
+    slab = (size_x, DEEP, LANES)
+    c, f, mza, mzb = call(
+        turn_kernel, "turn", (brick, brick, (2, *slab), (2, *slab)), (reaction, right_side),
+        [(2, *right_side.shape)], far_args=(0, 1), copies=8,
     )
     even_z, odd_z = pairs_of(nz)
     za = lax.ppermute(mza, ("gy", "gc"), even_z)
     zb = lax.ppermute(mzb, ("gy", "gc"), odd_z)
-
-    wide = size_z + 2 * DEEP
-    deep = wide + 2 * GUARD
-    rows1 = size_z // 4 + 2 * GUARD
-    size1, size2 = size_x // 2, size_x // 4
-    box2 = (size2 + 10, 5, 8, LANES)
-    near = (40 + 7 * rows1, LANES)
+    v, mya, myb = call(turn_again_kernel, "turn_again", (brick, slab, slab), (initial, mza))
+    ya = lax.ppermute(mya, ("gy", "gc"), even_z)
+    yb = lax.ppermute(myb, ("gy", "gc"), odd_z)
+
     message = (2 * wide + 2 * rows1 + 32, LANES)
-    mxa, mxb = call(
-        coefficient_kernel, "coefficients", (message, message), (c, za, zb),
-        [(size_x, deep, LANES), (size1, rows1 + 2 * GUARD, LANES)],
+    mxa, mxb, c, c1 = call(
+        coefficient_kernel, "coefficients", (message, message, padded, padded1), (c, za, zb)
     )
     even_x, odd_x = pairs_of(nx)
     xa = lax.ppermute(mxa, "gx", even_x)
     xb = lax.ppermute(mxb, "gx", odd_x)
 
-    kept = size_z + 2 * KEEP
-    margin = (5 * kept, LANES)
-    field = (size_x + 8, deep, LANES)
-    field1 = (size1 + 10, rows1 + 2 * GUARD, LANES)
-    chunk, mna, mnb, mua, mub, v, f, c, f1, c1, v1, v2, f2, c2 = call(
-        down_kernel, "down",
-        (
-            (nx * nz // 2, 2, 8, LANES),
-            near,
-            near,
-            margin,
-            margin,
-            (size_x + 4, kept, LANES),
-            (size_x, kept, LANES),
-            (size_x + 4, kept, LANES),
-            (size1 + 4, rows1, LANES),
-            (size1 + 6, rows1, LANES),
-            (2, rows1, LANES),
-            box2,
-            box2,
-            box2,
-        ),
-        (f, c, v, za, zb, xa, xb),
-        [field, field, field, field, (size_x, deep, LANES), field1, field1, field1, field1, box2, (size2 + 10, 8, LANES)],
-    )
-    own = lax.all_to_all(chunk, ("gx", "gy"), 0, 0, tiled=True)
-    mna, mnb = call(hold_kernel, "hold", (near, near), (mna, mnb, own))
-    other = lax.ppermute(own, "gc", [(0, 1), (1, 0)])
-    na = lax.ppermute(mna, "gx", even_x)
-    nb = lax.ppermute(mnb, "gx", odd_x)
-
-    own2, mua, mub = call(
-        complete_kernel, "complete", ((2 * size2, 8, LANES), margin, margin), (v2, f2, na, nb, mua, mub)
+    margin, later = (3 * sent, LANES), (2 * sent, LANES)
+    held = (size_x, kept, LANES)
+    f, v, edges, f1, mua, mub, mla, mlb, f_far, c_far = call(
+        inner_kernel, "inner",
+        (padded, padded, (4, deep, LANES), (size1 - 2, rows1, LANES), margin, margin, later, later, held, held),
+        (f, v, c, za, zb, ya, yb),
+        [padded] * 4, far_outs=(8, 9), copies=2,
     )
     ua = lax.ppermute(mua, "gx", even_x)
     ub = lax.ppermute(mub, "gx", odd_x)
+
+    box2 = (size2 + 10, 5, 8, LANES)
+    near, level1 = (40, LANES), (7 * rows1, LANES)
+    sides0, sides1 = (4, deep, LANES), (2, rows1, LANES)
+    parts1 = (size1 + 4, rows1, LANES), (size1 + 6, rows1, LANES)
+    field0 = (size_x + 4, deep, LANES)
+    field1 = (size1 + 10, rows1 + 2 * GUARD, LANES)
+    chunk, mna, mnb, m1a, m1b, v, c_sides, f1, c1, v1, level2, c2 = call(
+        outer_kernel, "outer",
+        (
+            (nx * nz // 2, 2, 8, LANES), near, near, level1, level1,
+            (size_x + 4, kept, LANES), (4, kept, LANES), *parts1, sides1, (2 * size2 + 10, 8, LANES), (size2 + 6, 3, 8, LANES),
+        ),
+        (f, c, v, edges, f1, c1, xa, xb),
+        [
+            field0, sides0, (2, deep, LANES), (12, deep, LANES), field1, field1, field1, field1,
+            box2, (size2 + 10, 8, LANES), box2, box2, box2,
+        ],
+        far_outs=range(5, 9), copies=4,
+    )
+    na = lax.ppermute(mna, "gx", even_x)
+    nb = lax.ppermute(mnb, "gx", odd_x)
+    own = gather(chunk, ("gx", "gy"))
+    both = (7 * rows1 + 2 * sent, LANES)
+    own2, mla, mlb = call(
+        meet_kernel, "meet", ((2 * size2, 8, LANES), both, both), (level2, na, nb, m1a, m1b, mla, mlb, ua, ub, own)
+    )
+    la = lax.ppermute(mla, "gx", even_x)
+    lb = lax.ppermute(mlb, "gx", odd_x)
+    other = lax.ppermute(own, "gc", [(0, 1), (1, 0)])
     z2a = lax.ppermute(own2, ("gy", "gc"), even_z)
     z2b = lax.ppermute(own2, ("gy", "gc"), odd_z)
     sides = (4 * size2 - 2, 8, LANES)
@@ -787,26 +905,25 @@
         functools.partial(coarse_kernel, nx, nz), "coarse",
         ((3, 10, 3, 8, LANES), (nx * nz, rows)),
         (own, other, coarse_inverse, msa),
-        [*[grid3] * 5, (LANES, LANES), (COARSE**3 // LANES, LANES)],
+        [*[grid3] * 5, (LANES, LANES), (COARSE**3 // LANES, LANES), coarse_inverse.shape],
+        far_args=(2,), copies=4,
     )
-    e = lax.all_to_all(e, ("gx", "gy", "gc"), 0, 0, tiled=True).reshape(COARSE**3 // LANES, LANES)
+    e = gather(e, ("gx", "gy", "gc")).reshape(COARSE**3 // LANES, LANES)
 
     near2 = (size2 + 8, 5, 8, LANES)
     box3 = (10, 5, 8, LANES)
-    (u3,) = call(
-        functools.partial(top_kernel, nx, nz), "top", (box3,), (e, window3), [grid3, box3, (LANES, LANES)]
-    )
     box = (size_x + 6, kept + 2 * GUARD, LANES)
     return call(
         functools.partial(up_kernel, nx, nz), "up",
         ((size_x, LANES, size_z), (size_x, LANES, size_z)),
-        (u3, own2, z2a, z2b, sa, sb, c2, v, f, c, f1, c1, v1, na, nb, ua, ub),
+        (e, window3, own2, z2a, z2b, sa, sb, c2, v, f_far, c_far, c_sides, f1, c1, v1, ua, ub, la, lb),
         [
-            near2, near2, near2,
+            box3, grid3, box3, (LANES, LANES), near2, near2, near2,
             field1, field1, field1, field1, (size2 + 4, rows1, LANES),
-            box, box, box, (size1 + 4, kept, LANES),
+            box, box, box, (size1 + 4, kept, LANES), *[(2, kept + 2 * GUARD, LANES)] * 2, (4, kept + 2 * GUARD, LANES),
+            (size_x + 4, kept, LANES), held, held, (4, kept, LANES), *parts1,
         ],
-        results=True,
+        far_args=range(8, 14), copies=6, results=True,
     )
 
 

time: 89.6 us -> 85.5 us (0.954)
  waiting for transfers between devices: 9.2 us -> 0.27 us
  Pallas kernels: 17.6 us -> 23.9 us
  local copies, waits for them, and re-layouts: 3.67 us -> 0.02 us
  starting transfers between devices: 21.1 us -> 22.2 us
  blocking collectives: 36.8 us -> 37.7 us
    pallas_call x9, Pallas kernels: 17.6 us -> 23.9 us  [call(): pl.pallas_call(kernel, out_shape=[jax.ShapeDtypeStruct(s, F32) if results...]
    ppermute x0 -> x4, starting transfers between devices: none -> 5.98 us  [the longest x1 3.95 us: local(): ya = lax.ppermute(mya, ('gy', 'gc'), even_z)]
    ppermute x1, waiting for transfers between devices: 4.32 us -> 0.01 us  [local(): na = lax.ppermute(mna, 'gx', even_x)]
    unnamed x8 -> x2, local copies, waits for them, and re-layouts: 3.67 us -> 0.01 us
    ppermute x1, waiting for transfers between devices: 3.33 us -> 0.01 us  [local(): xa = lax.ppermute(mxa, 'gx', even_x)]
    ppermute x1, starting transfers between devices: 5.48 us -> 3.49 us  [local(): sa = lax.ppermute(msa, 'gx', even_x)]
    ppermute x1, starting transfers between devices: 2.42 us -> 0.5 us  [local(): z2a = lax.ppermute(own2, ('gy', 'gc'), even_z)]
    ppermute x1, starting transfers between devices: 2.93 us -> 1.56 us  [local(): xa = lax.ppermute(mxa, 'gx', even_x)]
  transfers between devices with their start and end apart: 13 -> 17, of which waited for: 4 -> 1; matrix products, arithmetic and copies ran while one was open for 0% -> 0% of each run, Pallas kernels for 3% -> 17%
where the time goes in v3:
time: 85.5 us; the launch traced here: 85.1 us
  blocking collectives  37.7 us (44%)
  Pallas kernels  23.9 us (28%)
  starting transfers between devices  22.2 us (26%)
  between operations  1 us (1%)
    all_to_all x2, blocking collectives, gather(): lax.all_to_all(x, axes, 0, 0, tiled=True)  37.7 us
    pallas_call x9, Pallas kernels, call(): pl.pallas_call(kernel, out_shape=[jax.ShapeDtypeStruct(s, F32) if results...  23.9 us
    ppermute x1, starting transfers between devices, local(): ua = lax.ppermute(mua, 'gx', even_x)  5.99 us
    ppermute x1, starting transfers between devices, local(): ya = lax.ppermute(mya, ('gy', 'gc'), even_z)  3.95 us
    ppermute x1, starting transfers between devices, local(): sa = lax.ppermute(msa, 'gx', even_x)  3.49 us
  transfers between devices with their start and end apart: 17, of which 1 were waited for; matrix products, arithmetic and copies ran while one was open for 0% of the time, Pallas kernels for 17%

profile of v3, /device:TPU:0, one launch (start us, length us, event | category | flops | bytes accessed | tf_op | source)
XLA Modules:
  0.0 85.1 jit_solution(3170011872419174427)
XLA Ops:
  0.6 0.0 copy-start
  0.6 2.2 %turn.1 = (f32[16,128,128]{2,1,0:T(8,128)S(1)}, f32[16,128,128]{2,1,0:T(8,128)S(1)}, f32[2,16,16,128]{3,2,1,0:T(8,128)S(1)}, f32[2,16,16,128]{3,2,1,0:T(8,128)S(1)}) custom-call(f32[16,128,128]{2,1,0:T(8,128)} %refs_0_.1, f32[16,128,128]{2,1,0:T(8,128)} %refs_1_.1), custom_call_target="tpu_custom_call" | custom-call | bytes 3000000 | tf_op jit(solution)/shard_map/turn/pallas_call | solution.py:127
  2.9 0.5 collective-permute-start
  3.4 0.7 collective-permute-start.1
  4.0 0.0 copy-done
  4.1 0.3 turn_again.1
  4.4 4.0 %collective-permute-start.2 = (f32[16,16,128]{2,1,0:T(8,128)S(1)}, f32[16,16,128]{2,1,0:T(8,128)S(1)}, u32[]{:S(2)}, u32[]{:S(2)}) collective-permute-start(f32[16,16,128]{2,1,0:T(8,128)S(1)} %get-tuple-element.58), channel_id=1, source_target_pairs={{0,1},{1,0},{2,3},{3,2},{4,5},{5,4},{6,7},{7,6},{8,9},{9,8},{10,11... | collective-permute-start | bytes 393224 | tf_op jit(solution)/shard_map/ppermute | solution.py:844
  8.4 0.7 collective-permute-start.3
  9.0 0.0 collective-permute-done.za
  9.0 0.0 collective-permute-done.1.zb
  9.0 0.8 coefficients.1
  9.9 1.6 %collective-permute-start.4 = (f32[448,128]{1,0:T(8,128)S(1)}, f32[448,128]{1,0:T(8,128)S(1)}, u32[]{:S(2)}, u32[]{:S(2)}) collective-permute-start(f32[448,128]{1,0:T(8,128)S(1)} %get-tuple-element.65), channel_id=1, source_target_pairs={{0,4},{4,0},{8,12},{12,8},{16,20},{20,16},{24,28},{28,24},{1,5},{5... | collective-permute-start | bytes 688136 | tf_op jit(solution)/shard_map/ppermute | solution.py:852
  11.4 0.7 collective-permute-start.5
  12.1 0.0 collective-permute-done.2.ya
  12.1 0.0 collective-permute-done.3.yb
  12.1 4.7 %inner.1 = (f32[16,176,128]{2,1,0:T(8,128)S(1)}, f32[16,176,128]{2,1,0:T(8,128)S(1)}, f32[4,176,128]{2,1,0:T(8,128)S(1)}, f32[6,48,128]{2,1,0:T(8,128)S(1)}, f32...) custom-call(f32[16,128,128]{2,1,0:T(8,128)S(1)} %get-tuple-element.5, ...), custom_call_target="tpu_custom_call" | custom-call | bytes 3000000 | tf_op jit(solution)/shard_map/inner/pallas_call | solution.py:127
  16.8 0.7 collective-permute-start.10
  17.5 6.0 %collective-permute-start.9 = (f32[408,128]{1,0:T(8,128)S(1)}, f32[408,128]{1,0:T(8,128)S(1)}, u32[]{:S(2)}, u32[]{:S(2)}) collective-permute-start(f32[408,128]{1,0:T(8,128)S(1)} %get-tuple-element.75), channel_id=1, source_target_pairs={{0,4},{4,0},{8,12},{12,8},{16,20},{20,16},{24,28},{28,24},{1,5},{5... | collective-permute-start | bytes 626696 | tf_op jit(solution)/shard_map/ppermute | solution.py:863
  23.5 0.0 collective-permute-done.4.xa
  23.5 0.0 collective-permute-done.5.xb
  23.5 5.0 %outer.1 = (f32[16,2,8,128]{3,2,1,0:T(8,128)S(1)}, f32[40,128]{1,0:T(8,128)S(1)}, f32[40,128]{1,0:T(8,128)S(1)}, f32[336,128]{1,0:T(8,128)S(1)}, f32[336,128]{1,...) custom-call(f32[16,176,128]{2,1,0:T(8,128)S(1)} %get-tuple-element.6, ...), custom_call_target="tpu_custom_call" | custom-call | bytes 3000000 | tf_op jit(solution)/shard_map/outer/pallas_call | solution.py:127
  28.5 0.1 collective-permute-start.7
  28.6 0.7 collective-permute-start.8
  29.2 20.9 %conditional.2 = (f32[16,2,8,128]{3,2,1,0:T(8,128)S(1)}) conditional(s32[]{:T(128)} %convert_element_type.4, f32[16,2,8,128]{3,2,1,0:T(8,128)S(1)} %get-tuple-element.67, f32[16,2,8,128]{3,2,1,0:T(8,128)S(1)} %get-tuple-element.67), branch_computations={%region_0.0_spmd, %region_1.0_spmd} | conditional | bytes 524296 | solution.py:823
  29.2 20.8 %all_to_all.13 = f32[16,2,8,128]{3,2,1,0:T(8,128)S(1)} all-to-all(f32[16,2,8,128]{3,2,1,0:T(8,128)S(1)} %copy.10), channel_id=1, replica_groups=mesh['gx'=8,'gy'=2,'gc'=2] {'gx','gy'}, dimensions={0} | all-to-all | bytes 262144 | tf_op jit(solution)/shard_map/cond/branch_1_fun/all_to_all | solution.py:823
  50.1 0.0 collective-permute-done.10.__.xb
  50.1 0.0 collective-permute-done.9._.xa
  50.1 0.0 collective-permute-done.7.xa
  50.1 0.0 collective-permute-done.8.xb
  50.1 0.1 meet.1
  50.2 0.7 collective-permute-start.15
  50.9 0.7 collective-permute-start.16
  51.5 0.1 collective-permute-start.6
  51.6 0.5 collective-permute-start.11
  52.1 0.7 collective-permute-start.12
  52.8 0.2 collective-permute-done.11.za
  53.0 0.0 collective-permute-done.12.zb
  53.0 3.5 %collective-permute-start.13 = (f32[14,8,128]{2,1,0:T(8,128)S(1)}, f32[14,8,128]{2,1,0:T(8,128)S(1)}, u32[]{:S(2)}, u32[]{:S(2)}) collective-permute-start(f32[14,8,128]{2,1,0:T(8,128)S(1)} %get-tuple-element.78._), channel_id=1, source_target_pairs={{0,4},{4,0},{8,12},{12,8},{16,20},{20,16},{24,28},{28,24},{1,5},{5... | collective-permute-start | bytes 172040 | tf_op jit(solution)/shard_map/ppermute | solution.py:899
  56.5 0.7 collective-permute-start.14
  57.2 0.0 collective-permute-done.6.other
  57.2 3.4 %coarse.1 = (f32[3,10,3,8,128]{4,3,2,1,0:T(8,128)S(1)}, f32[32,128]{1,0:T(8,128)S(1)}) custom-call(f32[16,2,8,128]{3,2,1,0:T(8,128)S(1)} %get-tuple-element.92.___.own, f32[16,2,8,128]{3,2,1,0:T(8,128)S(1)} %collective-permute-done.6.other, f32[128,4096]{1,0:T(8,128)} %inverse_far.1, f32[14,8,128]{2,1,0:T(8,128)S(1)} %get-tuple-element.78._), custom_call_target="tpu_custom_call" | custom-call | bytes 3000000 | tf_op jit(solution)/shard_map/coarse/pallas_call | solution.py:127
  60.6 16.9 %conditional.3 = (f32[32,128]{1,0:T(8,128)S(1)}) conditional(s32[]{:T(128)} %convert_element_type.4, f32[32,128]{1,0:T(8,128)S(1)} %get-tuple-element.79, f32[32,128]{1,0:T(8,128)S(1)} %get-tuple-element.79), branch_computations={%region_2.0_spmd, %region_3.0_spmd} | conditional | bytes 65544 | solution.py:823
  60.6 16.9 %all_to_all.14 = f32[32,1,128]{2,1,0:T(1,128)S(1)} all-to-all(f32[32,1,128]{2,1,0:T(1,128)S(1)} %copy.11), channel_id=1, replica_groups=mesh['gx'=8,'gy'=2,'gc'=2] {'gx','gy','gc'}, dimensions={0} | all-to-all | bytes 32768 | tf_op jit(solution)/shard_map/cond/branch_1_fun/all_to_all | solution.py:823
  77.5 0.0 collective-permute-done.13.sides_a
  77.5 0.0 collective-permute-done.14.sides_b
  77.5 0.0 collective-permute-done.15.later_a
  77.5 0.0 collective-permute-done.16.later_b
  77.5 7.4 %up.1 = (f32[16,128,128]{2,1,0:T(8,128)}, f32[16,128,128]{2,1,0:T(8,128)}) custom-call(f32[32,128]{1,0:T(8,128)S(1)} %get-tuple-element.93.e, f32[3,10,3,8,128]{4,3,2,1,0:T(8,128)S(1)} %get-tuple-element.80.window3, f32[8,8,128]{2,1,0:T(8,128)S(1)} %get-tuple-element.77.own.own2, f32[8,8,128]{2,1,0:T(8,128)S(1)} %collective-permute-done.11.za, ...), custom_call_target="tpu_custom_call" | custom-call | bytes 3000000 | tf_op jit(solution)/shard_map/up/pallas_call | solution.py:127
  (3 shorter events, 0.0 us)
Async XLA Ops:
  0.6 3.4 %copy-start = (f32[16,128,128]{2,1,0:T(8,128)S(1)}, f32[16,128,128]{2,1,0:T(8,128)}, u32[]{:S(2)}) copy-start(f32[16,128,128]{2,1,0:T(8,128)} %v_in.1) | copy-start | bytes 3145732
  2.9 6.2 %collective-permute-start = (f32[2,16,16,128]{3,2,1,0:T(8,128)S(1)}, f32[2,16,16,128]{3,2,1,0:T(8,128)S(1)}, u32[]{:S(2)}, u32[]{:S(2)}) collective-permute-start(f32[2,16,16,128]{3,2,1,0:T(8,128)S(1)} %get-tuple-element.53._), channel_id=1, source_target_pairs={{0,1},{1,0},{2,3},{3,2},{4,5},{5,4},{6,7},{7,6},{8,9},{9,8},{10,11... | collective-permute-start | bytes 786440 | tf_op jit(solution)/shard_map/ppermute | solution.py:841
  3.4 5.7 %collective-permute-start.1 = (f32[2,16,16,128]{3,2,1,0:T(8,128)S(1)}, f32[2,16,16,128]{3,2,1,0:T(8,128)S(1)}, u32[]{:S(2)}, u32[]{:S(2)}) collective-permute-start(f32[2,16,16,128]{3,2,1,0:T(8,128)S(1)} %get-tuple-element.56), channel_id=1, source_target_pairs={{1,2},{2,1},{5,6},{6,5},{9,10},{10,9},{13,14},{14,13},{17,18},{18,... | collective-permute-start | bytes 786440 | tf_op jit(solution)/shard_map/ppermute | solution.py:842
  4.4 7.7 %collective-permute-start.2 = (f32[16,16,128]{2,1,0:T(8,128)S(1)}, f32[16,16,128]{2,1,0:T(8,128)S(1)}, u32[]{:S(2)}, u32[]{:S(2)}) collective-permute-start(f32[16,16,128]{2,1,0:T(8,128)S(1)} %get-tuple-element.58), channel_id=1, source_target_pairs={{0,1},{1,0},{2,3},{3,2},{4,5},{5,4},{6,7},{7,6},{8,9},{9,8},{10,11... | collective-permute-start | bytes 393224 | tf_op jit(solution)/shard_map/ppermute | solution.py:844
  8.4 3.8 %collective-permute-start.3 = (f32[16,16,128]{2,1,0:T(8,128)S(1)}, f32[16,16,128]{2,1,0:T(8,128)S(1)}, u32[]{:S(2)}, u32[]{:S(2)}) collective-permute-start(f32[16,16,128]{2,1,0:T(8,128)S(1)} %get-tuple-element.59), channel_id=1, source_target_pairs={{1,2},{2,1},{5,6},{6,5},{9,10},{10,9},{13,14},{14,13},{17,18},{18,... | collective-permute-start | bytes 393224 | tf_op jit(solution)/shard_map/ppermute | solution.py:845
  9.9 13.6 %collective-permute-start.4 = (f32[448,128]{1,0:T(8,128)S(1)}, f32[448,128]{1,0:T(8,128)S(1)}, u32[]{:S(2)}, u32[]{:S(2)}) collective-permute-start(f32[448,128]{1,0:T(8,128)S(1)} %get-tuple-element.65), channel_id=1, source_target_pairs={{0,4},{4,0},{8,12},{12,8},{16,20},{20,16},{24,28},{28,24},{1,5},{5... | collective-permute-start | bytes 688136 | tf_op jit(solution)/shard_map/ppermute | solution.py:852
  11.4 12.0 %collective-permute-start.5 = (f32[448,128]{1,0:T(8,128)S(1)}, f32[448,128]{1,0:T(8,128)S(1)}, u32[]{:S(2)}, u32[]{:S(2)}) collective-permute-start(f32[448,128]{1,0:T(8,128)S(1)} %get-tuple-element.66), channel_id=1, source_target_pairs={{4,8},{8,4},{12,16},{16,12},{20,24},{24,20},{5,9},{9,5},{13,17},{1... | collective-permute-start | bytes 688136 | tf_op jit(solution)/shard_map/ppermute | solution.py:853
  16.8 33.3 %collective-permute-start.10 = (f32[408,128]{1,0:T(8,128)S(1)}, f32[408,128]{1,0:T(8,128)S(1)}, u32[]{:S(2)}, u32[]{:S(2)}) collective-permute-start(f32[408,128]{1,0:T(8,128)S(1)} %get-tuple-element.76), channel_id=1, source_target_pairs={{4,8},{8,4},{12,16},{16,12},{20,24},{24,20},{5,9},{9,5},{13,17},{1... | collective-permute-start | bytes 626696 | tf_op jit(solution)/shard_map/ppermute | solution.py:864
  17.5 32.6 %collective-permute-start.9 = (f32[408,128]{1,0:T(8,128)S(1)}, f32[408,128]{1,0:T(8,128)S(1)}, u32[]{:S(2)}, u32[]{:S(2)}) collective-permute-start(f32[408,128]{1,0:T(8,128)S(1)} %get-tuple-element.75), channel_id=1, source_target_pairs={{0,4},{4,0},{8,12},{12,8},{16,20},{20,16},{24,28},{28,24},{1,5},{5... | collective-permute-start | bytes 626696 | tf_op jit(solution)/shard_map/ppermute | solution.py:863
  28.5 21.6 %collective-permute-start.7 = (f32[40,128]{1,0:T(8,128)S(1)}, f32[40,128]{1,0:T(8,128)S(1)}, u32[]{:S(2)}, u32[]{:S(2)}) collective-permute-start(f32[40,128]{1,0:T(8,128)S(1)} %get-tuple-element.69), channel_id=1, source_target_pairs={{0,4},{4,0},{8,12},{12,8},{16,20},{20,16},{24,28},{28,24},{1,5},{5... | collective-permute-start | bytes 61448 | tf_op jit(solution)/shard_map/ppermute | solution.py:885
  28.6 21.5 %collective-permute-start.8 = (f32[40,128]{1,0:T(8,128)S(1)}, f32[40,128]{1,0:T(8,128)S(1)}, u32[]{:S(2)}, u32[]{:S(2)}) collective-permute-start(f32[40,128]{1,0:T(8,128)S(1)} %get-tuple-element.70), channel_id=1, source_target_pairs={{4,8},{8,4},{12,16},{16,12},{20,24},{24,20},{5,9},{9,5},{13,17},{1... | collective-permute-start | bytes 61448 | tf_op jit(solution)/shard_map/ppermute | solution.py:886
  50.2 27.3 %collective-permute-start.15 = (f32[608,128]{1,0:T(8,128)S(1)}, f32[608,128]{1,0:T(8,128)S(1)}, u32[]{:S(2)}, u32[]{:S(2)}) collective-permute-start(f32[608,128]{1,0:T(8,128)S(1)} %get-tuple-element.90), channel_id=1, source_target_pairs={{0,4},{4,0},{8,12},{12,8},{16,20},{20,16},{24,28},{28,24},{1,5},{5... | collective-permute-start | bytes 933896 | tf_op jit(solution)/shard_map/ppermute | solution.py:892
  50.9 26.6 %collective-permute-start.16 = (f32[608,128]{1,0:T(8,128)S(1)}, f32[608,128]{1,0:T(8,128)S(1)}, u32[]{:S(2)}, u32[]{:S(2)}) collective-permute-start(f32[608,128]{1,0:T(8,128)S(1)} %get-tuple-element.91), channel_id=1, source_target_pairs={{4,8},{8,4},{12,16},{16,12},{20,24},{24,20},{5,9},{9,5},{13,17},{1... | collective-permute-start | bytes 933896 | tf_op jit(solution)/shard_map/ppermute | solution.py:893
  51.5 5.6 %collective-permute-start.6 = (f32[16,2,8,128]{3,2,1,0:T(8,128)S(1)}, f32[16,2,8,128]{3,2,1,0:T(8,128)S(1)}, u32[]{:S(2)}, u32[]{:S(2)}) collective-permute-start(f32[16,2,8,128]{3,2,1,0:T(8,128)S(1)} %get-tuple-element.92.___.own), channel_id=1, source_target_pairs={{0,1},{1,0},{2,3},{3,2},{4,5},{5,4},{6,7},{7,6},{8,9},{9,8},{10,11... | collective-permute-start | bytes 393224 | tf_op jit(solution)/shard_map/ppermute | solution.py:894
  51.6 1.4 %collective-permute-start.11 = (f32[8,8,128]{2,1,0:T(8,128)S(1)}, f32[8,8,128]{2,1,0:T(8,128)S(1)}, u32[]{:S(2)}, u32[]{:S(2)}) collective-permute-start(f32[8,8,128]{2,1,0:T(8,128)S(1)} %get-tuple-element.77.own.own2), channel_id=1, source_target_pairs={{0,1},{1,0},{2,3},{3,2},{4,5},{5,4},{6,7},{7,6},{8,9},{9,8},{10,11... | collective-permute-start | bytes 98312 | tf_op jit(solution)/shard_map/ppermute | solution.py:895
  52.1 0.9 %collective-permute-start.12 = (f32[8,8,128]{2,1,0:T(8,128)S(1)}, f32[8,8,128]{2,1,0:T(8,128)S(1)}, u32[]{:S(2)}, u32[]{:S(2)}) collective-permute-start(f32[8,8,128]{2,1,0:T(8,128)S(1)} %get-tuple-element.77.own.own2), channel_id=1, source_target_pairs={{1,2},{2,1},{5,6},{6,5},{9,10},{10,9},{13,14},{14,13},{17,18},{18,... | collective-permute-start | bytes 98312 | tf_op jit(solution)/shard_map/ppermute | solution.py:896
  53.0 24.4 %collective-permute-start.13 = (f32[14,8,128]{2,1,0:T(8,128)S(1)}, f32[14,8,128]{2,1,0:T(8,128)S(1)}, u32[]{:S(2)}, u32[]{:S(2)}) collective-permute-start(f32[14,8,128]{2,1,0:T(8,128)S(1)} %get-tuple-element.78._), channel_id=1, source_target_pairs={{0,4},{4,0},{8,12},{12,8},{16,20},{20,16},{24,28},{28,24},{1,5},{5... | collective-permute-start | bytes 172040 | tf_op jit(solution)/shard_map/ppermute | solution.py:899
  56.5 21.0 %collective-permute-start.14 = (f32[14,8,128]{2,1,0:T(8,128)S(1)}, f32[14,8,128]{2,1,0:T(8,128)S(1)}, u32[]{:S(2)}, u32[]{:S(2)}) collective-permute-start(f32[14,8,128]{2,1,0:T(8,128)S(1)} %get-tuple-element.81), channel_id=1, source_target_pairs={{4,8},{8,4},{12,16},{16,12},{20,24},{24,20},{5,9},{9,5},{13,17},{1... | collective-permute-start | bytes 172040 | tf_op jit(solution)/shard_map/ppermute | solution.py:900

commit v4 on v3

--- a/solution.py
+++ b/solution.py
@@ -17,6 +17,7 @@
 KEEP = 8
 SENT = 4
 GUARD = 8
+EARLY = 2
 MIB = 1 << 20
 
 
@@ -123,7 +124,11 @@
     limit = sum(4 * math.prod(s) for s in scratch) + 6 * MIB
     spaces_in = [pltpu.HBM if k in far_args else pltpu.VMEM for k in range(len(args))]
     spaces_out = [pltpu.HBM if k in far_outs else pltpu.VMEM for k in range(len(outs))]
-    args = [pltpu.with_memory_space_constraint(a, space) for a, space in zip(args, spaces_in, strict=True)]
+    spaces_in = [pltpu.SMEM if a.dtype == jnp.int32 else space for a, space in zip(args, spaces_in, strict=True)]
+    args = [
+        a if space == pltpu.SMEM else pltpu.with_memory_space_constraint(a, space)
+        for a, space in zip(args, spaces_in, strict=True)
+    ]
     return pl.pallas_call(
         kernel,
         out_shape=[
@@ -148,8 +153,8 @@
 
 def turn_kernel(*refs):
     *refs, held, arrivals = refs
-    count = (len(refs) - 2) // 2
-    sources, targets, (to_a, to_b) = refs[:count], refs[count : 2 * count], refs[2 * count :]
+    count = (len(refs) - 3) // 2
+    sources, targets, (to_a, to_b) = refs[:count], refs[count + 1 : 2 * count + 1], refs[2 * count + 1 :]
     piece = targets[0].shape[0] // 4
     copies = []
     for which, source in enumerate(sources):
@@ -212,8 +217,8 @@
 
 def inner_kernel(
     f_in, v_in, c, za, zb, ya, yb,
-    f, v2, edges, f1, to_a, to_b, later_a, later_b, f_far, c_far,
-    va, vb, g, r, arrivals,
+    f, v2, edges, f1, to_a, to_b, later_a, later_b, f_ends, c_ends,
+    va, vb, g, r,
 ):
     odd_z = lax.axis_index("gc") == 1
     even_x = lax.axis_index("gx") % 2 == 0
@@ -225,17 +230,11 @@
     lane = lanes_of(half)
     zeros8 = jnp.zeros((GUARD, LANES), F32)
 
-    kept = pl.ds(GUARD + DEEP - KEEP, size_z + 2 * KEEP)
-    copies = [pltpu.make_async_copy(c.at[:, kept], c_far, arrivals.at[0])]
-    copies[0].start()
     for source, target, a, b in ((f_in, f, za.at[1], zb.at[1]), (v_in, va, ya, yb)):
         for x in range(size_x):
             low = jnp.where(odd_z, a[x], b[x])
             high = jnp.where(odd_z, b[x], a[x])
             fill_rows(target, x, source[x], low, high)
-        if target is f:
-            copies.append(pltpu.make_async_copy(f.at[:, kept], f_far, arrivals.at[1]))
-            copies[1].start()
     for ref in (va, vb, v2):
         for x in range(size_x):
             ref[x, pl.ds(0, GUARD)] = zeros8
@@ -272,11 +271,12 @@
         source = f[edge, here]
         sides.append((va[edge, here], vb[edge, here], source + vb[second, here], source + center, source + swept))
     for k, (left, right) in enumerate(zip(*sides, strict=True)):
-        a, b, rows = (to_a, to_b, pl.ds(k * sent, sent)) if k < 3 else (later_a, later_b, pl.ds((k - 3) * sent, sent))
+        a, b, rows = (to_a, to_b, pl.ds(k * sent, sent)) if k < EARLY else (later_a, later_b, pl.ds((k - EARLY) * sent, sent))
         a[rows] = jnp.where(even_x, right, left)
         b[rows] = jnp.where(even_x, left, right)
-    for copy in copies:
-        copy.wait()
+    for source, target in ((f, f_ends), (c, c_ends)):
+        target[:, pl.ds(0, KEEP)] = source[:, pl.ds(GUARD + DEEP - KEEP, KEEP)]
+        target[:, pl.ds(KEEP, KEEP)] = source[:, pl.ds(GUARD + DEEP + size_z, KEEP)]
 
 
 def outer_kernel(
@@ -298,6 +298,9 @@
     def keep(source, target):
         copies.append(pltpu.make_async_copy(source, target, arrivals.at[len(copies)]))
         copies[-1].start()
+
+    kept = pl.ds(GUARD + DEEP - KEEP, size_z + 2 * KEEP)
+    keep(v2_in.at[pl.ds(1, size_x - 2), kept], v_far.at[pl.ds(3, size_x - 2)])
 
     for x in range(size_x):
         v[x + 2] = v2_in[x]
@@ -338,8 +341,8 @@
                     weight = 6.0 + c_out[beside if k == -1 else past, here]
                 r[base + (4 + k) * inward, here] = total - weight * center
 
-    kept = pl.ds(GUARD + DEEP - KEEP, size_z + 2 * KEEP)
-    keep(v.at[:, kept], v_far)
+    for at in (0, size_x + 1):
+        keep(v.at[pl.ds(at, 3), kept], v_far.at[pl.ds(at, 3)])
     keep(c_out.at[:, kept], sides_far)
 
     rows1 = size_z // 4 + 2 * GUARD
@@ -474,13 +477,17 @@
         target[pl.ds(size, second.shape[0])] = second[...]
 
 
+def follow_kernel(values, _, out):
+    out[...] = values[...]
+
+
 def past_tiles(za, zb, k, odd_z, lane):
     below = jnp.where(odd_z, za[k], zb[k])
     above = jnp.where(odd_z, zb[k], za[k])
     return jnp.where(lane >= 96, below, jnp.where(lane < 32, above, 0.0))
 
 
-def side_kernel(own, za, zb, to_a, to_b):
+def side_kernel(own, za, zb, _, to_a, to_b):
     odd_z = lax.axis_index("gc") == 1
     even_x = lax.axis_index("gx") % 2 == 0
     size2 = own.shape[0] // 2
@@ -504,7 +511,7 @@
 
 
 def coarse_kernel(
-    nx, nz, own, other, inverse_far, _,
+    nx, nz, own, other, inverse_far,
     window3, e_out,
     v3, f3, g3, c3, u3, turned, flat, inverse, arrivals,
 ):
@@ -634,14 +641,14 @@
 
 
 def up_kernel(
-    nx, nz, e, window3, own2, za, zb, sides_a, sides_b, c2, v_far, f_far, c_far, sides_far, f1_far, c1_far, v1_in, xa, xb, later_a, later_b,
-    pressure, residual,
-    u3, lifted3, w3, turned, u2, w2, f2, f1, c1, u1, w1, lift1, ua, ub, g, lift0, before_in, after_in, sources, v_in, f_in, c_in, c_sides, f1_in, c1_in, arrivals,
+    nx, nz, e, window3, own2, za, zb, sides_a, sides_b, c2, v_far, f_far, c_far, sides_far, f1_far, c1_far, f_ends, c_ends, v1_in, xa, xb, later_a, later_b,
+    pressure_far, residual_far,
+    u3, lifted3, w3, turned, u2, w2, f2, f1, c1, u1, w1, lift1, ua, ub, g, lift0, before_in, after_in, sources, v_in, f_in, c_in, f_held, c_held, c_sides, f1_in, c1_in, pressure, residual, arrivals,
 ):
     even_x = lax.axis_index("gx") % 2 == 0
     lane, sub = lanes_of(8), subs_of(8)
     zeros8 = jnp.zeros((GUARD, LANES), F32)
-    pairs = (f1_far, f1_in), (c1_far, c1_in), (sides_far, c_sides), (c_far, c_in), (v_far, v_in), (f_far, f_in)
+    pairs = (f1_far, f1_in), (c1_far, c1_in), (sides_far, c_sides), (v_far, v_in), (c_far, c_held), (f_far, f_held)
     copies = [pltpu.make_async_copy(*pair, arrivals.at[k]) for k, pair in enumerate(pairs)]
     for copy in copies:
         copy.start()
@@ -757,6 +764,11 @@
             ref[at, pl.ds(GUARD + kept, GUARD)] = zeros8
     for copy in copies[2:]:
         copy.wait()
+    for held, part, target in ((f_held, f_ends, f_in), (c_held, c_ends, c_in)):
+        for x in range(size_x):
+            target[x, pl.ds(KEEP, size_z)] = held[x].T
+        target[:, pl.ds(0, KEEP)] = part[:, pl.ds(0, KEEP)]
+        target[:, pl.ds(KEEP + size_z, KEEP)] = part[:, pl.ds(KEEP, KEEP)]
     shift = -GUARD
     for x in range(-3, size_x + 3):
         value = lift0[(x + 4) // 2]
@@ -778,8 +790,8 @@
     lane_s = lanes_of(sent)
     for ref in (before_in, after_in, sources):
         ref[...] = jnp.zeros(ref.shape, F32)
-    messages = [arrived(k * sent, sent) for k in range(3)]
-    messages += [arrived(7 * rows1 + k * sent, sent, later_a, later_b) for k in range(2)]
+    messages = [arrived(k * sent, sent) for k in range(EARLY)]
+    messages += [arrived(7 * rows1 + k * sent, sent, later_a, later_b) for k in range(5 - EARLY)]
     for side, (edge, inward) in enumerate(((off, 1), (last, -1))):
         before, after, source0, source1, source2 = (message[side] for message in messages)
         before_in[side, taken] = g[edge - 1, taken] * before
@@ -804,12 +816,26 @@
                 target[at, pl.ds(start, rows)] = 0.2 * center + g[at - 1, pl.ds(start, rows)] * total
     lane_z = lanes_of(size_z)
     own = GUARD + KEEP
+    piece = size_x // 4
+    copies = []
+
+    def leave(source, target, x):
+        if (x + 1) % piece == 0:
+            planes = pl.ds(x + 1 - piece, piece)
+            copies.append(pltpu.make_async_copy(source.at[planes], target.at[planes], arrivals.at[len(copies)]))
+            copies[-1].start()
+
+    for x in range(size_x):
+        pressure[x] = ua[x + off, pl.ds(own, size_z)].T
+        leave(pressure, pressure_far, x)
     for x in range(size_x):
         center, total = around(ua, x + off, own, size_z, lane_z, LANES)
         mine = pl.ds(own + shift, size_z)
         total = total + f_in[x, mine]
-        pressure[x] = center.T
         residual[x] = (total - (6.0 + c_in[x, mine]) * center).T
+        leave(residual, residual_far, x)
+    for copy in copies:
+        copy.wait()
 
 
 def pairs_of(count):
@@ -818,8 +844,7 @@
     return even, odd
 
 
-def gather(copies, axes):
-    always = lax.optimization_barrier(jnp.int32(1)) > 0
+def gather(copies, axes, always):
     return lax.cond(always, lambda x: lax.all_to_all(x, axes, 0, 0, tiled=True), lambda x: x, copies)
 
 
@@ -833,8 +858,10 @@
     padded = (size_x, deep, LANES)
     padded1 = (size1, rows1 + 2 * GUARD, LANES)
     slab = (size_x, DEEP, LANES)
+    always = lax.optimization_barrier(jnp.int32(1)) > 0
+    flag = always.astype(jnp.int32).reshape(1, 1)
     c, f, mza, mzb = call(
-        turn_kernel, "turn", (brick, brick, (2, *slab), (2, *slab)), (reaction, right_side),
+        turn_kernel, "turn", (brick, brick, (2, *slab), (2, *slab)), (reaction, right_side, flag),
         [(2, *right_side.shape)], far_args=(0, 1), copies=8,
     )
     even_z, odd_z = pairs_of(nz)
@@ -852,13 +879,13 @@
     xa = lax.ppermute(mxa, "gx", even_x)
     xb = lax.ppermute(mxb, "gx", odd_x)
 
-    margin, later = (3 * sent, LANES), (2 * sent, LANES)
-    held = (size_x, kept, LANES)
-    f, v, edges, f1, mua, mub, mla, mlb, f_far, c_far = call(
+    margin, later = (EARLY * sent, LANES), ((5 - EARLY) * sent, LANES)
+    held, ends = (size_x, kept, LANES), (size_x, 2 * KEEP, LANES)
+    f, v, edges, f1, mua, mub, mla, mlb, f_ends, c_ends = call(
         inner_kernel, "inner",
-        (padded, padded, (4, deep, LANES), (size1 - 2, rows1, LANES), margin, margin, later, later, held, held),
+        (padded, padded, (4, deep, LANES), (size1 - 2, rows1, LANES), margin, margin, later, later, ends, ends),
         (f, v, c, za, zb, ya, yb),
-        [padded] * 4, far_outs=(8, 9), copies=2,
+        [padded] * 4,
     )
     ua = lax.ppermute(mua, "gx", even_x)
     ub = lax.ppermute(mub, "gx", odd_x)
@@ -880,12 +907,12 @@
             field0, sides0, (2, deep, LANES), (12, deep, LANES), field1, field1, field1, field1,
             box2, (size2 + 10, 8, LANES), box2, box2, box2,
         ],
-        far_outs=range(5, 9), copies=4,
+        far_outs=range(5, 9), copies=6,
     )
     na = lax.ppermute(mna, "gx", even_x)
     nb = lax.ppermute(mnb, "gx", odd_x)
-    own = gather(chunk, ("gx", "gy"))
-    both = (7 * rows1 + 2 * sent, LANES)
+    own = gather(chunk, ("gx", "gy"), always)
+    both = (7 * rows1 + (5 - EARLY) * sent, LANES)
     own2, mla, mlb = call(
         meet_kernel, "meet", ((2 * size2, 8, LANES), both, both), (level2, na, nb, m1a, m1b, mla, mlb, ua, ub, own)
     )
@@ -894,21 +921,21 @@
     other = lax.ppermute(own, "gc", [(0, 1), (1, 0)])
     z2a = lax.ppermute(own2, ("gy", "gc"), even_z)
     z2b = lax.ppermute(own2, ("gy", "gc"), odd_z)
-    sides = (4 * size2 - 2, 8, LANES)
-    msa, msb = call(side_kernel, "sides", (sides, sides), (own2, z2a, z2b))
-    sa = lax.ppermute(msa, "gx", even_x)
-    sb = lax.ppermute(msb, "gx", odd_x)
-
     grid3 = (2 * nx + 8, nz + 2, 8, LANES)
     rows = coarse_inverse.shape[0]
     window3, e = call(
         functools.partial(coarse_kernel, nx, nz), "coarse",
         ((3, 10, 3, 8, LANES), (nx * nz, rows)),
-        (own, other, coarse_inverse, msa),
+        (own, other, coarse_inverse),
         [*[grid3] * 5, (LANES, LANES), (COARSE**3 // LANES, LANES), coarse_inverse.shape],
         far_args=(2,), copies=4,
     )
-    e = gather(e, ("gx", "gy", "gc")).reshape(COARSE**3 // LANES, LANES)
+    sides = (4 * size2 - 2, 8, LANES)
+    msa, msb = call(side_kernel, "sides", (sides, sides), (own2, z2a, z2b, e))
+    sa = lax.ppermute(msa, "gx", even_x)
+    sb = lax.ppermute(msb, "gx", odd_x)
+    (e,) = call(follow_kernel, "follow", (e.shape,), (e, msa))
+    e = gather(e, ("gx", "gy", "gc"), always).reshape(COARSE**3 // LANES, LANES)
 
     near2 = (size2 + 8, 5, 8, LANES)
     box3 = (10, 5, 8, LANES)
@@ -916,14 +943,15 @@
     return call(
         functools.partial(up_kernel, nx, nz), "up",
         ((size_x, LANES, size_z), (size_x, LANES, size_z)),
-        (e, window3, own2, z2a, z2b, sa, sb, c2, v, f_far, c_far, c_sides, f1, c1, v1, ua, ub, la, lb),
+        (e, window3, own2, z2a, z2b, sa, sb, c2, v, right_side, reaction, c_sides, f1, c1, f_ends, c_ends, v1, ua, ub, la, lb),
         [
             box3, grid3, box3, (LANES, LANES), near2, near2, near2,
             field1, field1, field1, field1, (size2 + 4, rows1, LANES),
             box, box, box, (size1 + 4, kept, LANES), *[(2, kept + 2 * GUARD, LANES)] * 2, (4, kept + 2 * GUARD, LANES),
-            (size_x + 4, kept, LANES), held, held, (4, kept, LANES), *parts1,
+            (size_x + 4, kept, LANES), held, held, right_side.shape, right_side.shape, (4, kept, LANES), *parts1,
+            right_side.shape, right_side.shape,
         ],
-        far_args=range(8, 14), copies=6, results=True,
+        far_args=range(8, 14), far_outs=(0, 1), copies=8, results=True,
     )
 
 

time: 85.5 us -> 80.7 us (0.944)
  blocking collectives: 37.7 us -> 26.5 us
  starting transfers between devices: 22.2 us -> 30.3 us
  Pallas kernels: 23.9 us -> 22.4 us
    all_to_all x2, blocking collectives: 37.7 us -> 26.5 us  [gather(): lax.all_to_all(x, axes, 0, 0, tiled=True)]
    ppermute x1, starting transfers between devices: 0.1 us -> 4.34 us  [local(): na = lax.ppermute(mna, 'gx', even_x)]
    ppermute x1, starting transfers between devices: 3.49 us -> 7.38 us  [local(): sa = lax.ppermute(msa, 'gx', even_x)]
    ppermute x1, starting transfers between devices: 3.95 us -> 0.09 us  [local(): ya = lax.ppermute(mya, ('gy', 'gc'), even_z)]
    ppermute x1, starting transfers between devices: 0.52 us -> 4.38 us  [local(): za = lax.ppermute(mza, ('gy', 'gc'), even_z)]
    ppermute x1, starting transfers between devices: 5.99 us -> 4.34 us  [local(): ua = lax.ppermute(mua, 'gx', even_x)]
    pallas_call x9 -> x10, Pallas kernels: 23.9 us -> 22.4 us  [call(): pl.pallas_call(kernel, out_shape=[jax.ShapeDtypeStruct(s, F32) if results...]
    ppermute x1, starting transfers between devices: 0.5 us -> 1.88 us  [local(): z2a = lax.ppermute(own2, ('gy', 'gc'), even_z)]
  transfers between devices with their start and end apart: 17 -> 17, of which waited for: 1 -> 0; matrix products, arithmetic and copies ran while one was open for 0% -> 0% of each run, Pallas kernels for 17% -> 16%
where the time goes in v4:
time: 80.7 us; the launch traced here: 80.3 us
  starting transfers between devices  30.3 us (38%)
  blocking collectives  26.5 us (33%)
  Pallas kernels  22.4 us (28%)
  between operations  1.01 us (1%)
    all_to_all x2, blocking collectives, gather(): lax.all_to_all(x, axes, 0, 0, tiled=True)  26.5 us
    pallas_call x10, Pallas kernels, call(): pl.pallas_call(kernel, out_shape=[jax.ShapeDtypeStruct(s, F32) if results...  22.4 us
    ppermute x1, starting transfers between devices, local(): sa = lax.ppermute(msa, 'gx', even_x)  7.38 us
    ppermute x1, starting transfers between devices, local(): za = lax.ppermute(mza, ('gy', 'gc'), even_z)  4.38 us
    ppermute x1, starting transfers between devices, local(): na = lax.ppermute(mna, 'gx', even_x)  4.34 us
    ppermute x1, starting transfers between devices, local(): ua = lax.ppermute(mua, 'gx', even_x)  4.34 us
    ppermute x1, starting transfers between devices, local(): z2a = lax.ppermute(own2, ('gy', 'gc'), even_z)  1.88 us
  transfers between devices with their start and end apart: 17, of which 0 were waited for; matrix products, arithmetic and copies ran while one was open for 0% of the time, Pallas kernels for 16%

profile of v4, /device:TPU:0, one launch (start us, length us, event | category | flops | bytes accessed | tf_op | source)
XLA Modules:
  0.0 80.3 jit_solution(4527723605694454738)
XLA Ops:
  0.6 0.0 copy-start
  0.6 2.2 %turn.1 = (f32[16,128,128]{2,1,0:T(8,128)S(1)}, f32[16,128,128]{2,1,0:T(8,128)S(1)}, f32[2,16,16,128]{3,2,1,0:T(8,128)S(1)}, f32[2,16,16,128]{3,2,1,0:T(8,128)S(1)}) custom-call(f32[16,128,128]{2,1,0:T(8,128)} %c_far.1, f32[16,128,128]{2,1,0:T(8,128)} %f_far.1, s32[1,1]{1,0:T(1,128)} %bitcast.2.refs_2_), custom_call_target="tpu_custom_call" | custom-call | bytes 3000000 | tf_op jit(solution)/shard_map/turn/pallas_call | solution.py:132
  2.9 0.7 collective-permute-start.1
  3.5 4.4 %collective-permute-start = (f32[2,16,16,128]{3,2,1,0:T(8,128)S(1)}, f32[2,16,16,128]{3,2,1,0:T(8,128)S(1)}, u32[]{:S(2)}, u32[]{:S(2)}) collective-permute-start(f32[2,16,16,128]{3,2,1,0:T(8,128)S(1)} %get-tuple-element.53._), channel_id=1, source_target_pairs={{0,1},{1,0},{2,3},{3,2},{4,5},{5,4},{6,7},{7,6},{8,9},{9,8},{10,11... | collective-permute-start | bytes 786440 | tf_op jit(solution)/shard_map/ppermute | solution.py:868
  7.9 0.0 copy-done
  7.9 0.3 turn_again.1
  8.3 0.1 collective-permute-start.2
  8.4 0.7 collective-permute-start.3
  9.0 0.0 collective-permute-done.1.zb
  9.0 0.0 collective-permute-done.za
  9.1 0.8 %coefficients.1 = (f32[448,128]{1,0:T(8,128)S(1)}, f32[448,128]{1,0:T(8,128)S(1)}, f32[16,176,128]{2,1,0:T(8,128)S(1)}, f32[8,64,128]{2,1,0:T(8,128)S(1)}) custom-call(f32[16,128,128]{2,1,0:T(8,128)S(1)} %get-tuple-element.55.c_in, f32[2,16,16,128]{3,2,1,0:T(8,128)S(1)} %collective-permute-done.za, f32[2,16,16,128]{3,2,1,0:T(8,128)S(1)} %collective-permute-done.1.zb), custom_call_target="tpu_custom_call" | custom-call | bytes 3000000 | tf_op jit(solution)/shard_map/coefficients/pallas_call | solution.py:132
  9.9 1.6 %collective-permute-start.4 = (f32[448,128]{1,0:T(8,128)S(1)}, f32[448,128]{1,0:T(8,128)S(1)}, u32[]{:S(2)}, u32[]{:S(2)}) collective-permute-start(f32[448,128]{1,0:T(8,128)S(1)} %get-tuple-element.65), channel_id=1, source_target_pairs={{0,4},{4,0},{8,12},{12,8},{16,20},{20,16},{24,28},{28,24},{1,5},{5... | collective-permute-start | bytes 688136 | tf_op jit(solution)/shard_map/ppermute | solution.py:879
  11.5 0.7 collective-permute-start.5
  12.1 0.0 collective-permute-done.2.ya
  12.2 0.0 collective-permute-done.3.yb
  12.2 3.3 %inner.1 = (f32[16,176,128]{2,1,0:T(8,128)S(1)}, f32[16,176,128]{2,1,0:T(8,128)S(1)}, f32[4,176,128]{2,1,0:T(8,128)S(1)}, f32[6,48,128]{2,1,0:T(8,128)S(1)}, f32...) custom-call(f32[16,128,128]{2,1,0:T(8,128)S(1)} %get-tuple-element.5, ...), custom_call_target="tpu_custom_call" | custom-call | bytes 3000000 | tf_op jit(solution)/shard_map/inner/pallas_call | solution.py:132
  15.5 4.3 %collective-permute-start.9 = (f32[272,128]{1,0:T(8,128)S(1)}, f32[272,128]{1,0:T(8,128)S(1)}, u32[]{:S(2)}, u32[]{:S(2)}) collective-permute-start(f32[272,128]{1,0:T(8,128)S(1)} %get-tuple-element.76), channel_id=1, source_target_pairs={{0,4},{4,0},{8,12},{12,8},{16,20},{20,16},{24,28},{28,24},{1,5},{5... | collective-permute-start | bytes 417800 | tf_op jit(solution)/shard_map/ppermute | solution.py:890
  19.8 0.7 collective-permute-start.10
  20.5 0.0 collective-permute-done.4.xa
  20.5 0.0 collective-permute-done.5.xb
  20.5 4.9 %outer.1 = (f32[16,2,8,128]{3,2,1,0:T(8,128)S(1)}, f32[40,128]{1,0:T(8,128)S(1)}, f32[40,128]{1,0:T(8,128)S(1)}, f32[336,128]{1,0:T(8,128)S(1)}, f32[336,128]{1,...) custom-call(f32[16,176,128]{2,1,0:T(8,128)S(1)} %get-tuple-element.6, ...), custom_call_target="tpu_custom_call" | custom-call | bytes 3000000 | tf_op jit(solution)/shard_map/outer/pallas_call | solution.py:132
  25.4 4.3 %collective-permute-start.7 = (f32[40,128]{1,0:T(8,128)S(1)}, f32[40,128]{1,0:T(8,128)S(1)}, u32[]{:S(2)}, u32[]{:S(2)}) collective-permute-start(f32[40,128]{1,0:T(8,128)S(1)} %get-tuple-element.70), channel_id=1, source_target_pairs={{0,4},{4,0},{8,12},{12,8},{16,20},{20,16},{24,28},{28,24},{1,5},{5... | collective-permute-start | bytes 61448 | tf_op jit(solution)/shard_map/ppermute | solution.py:912
  29.8 0.7 collective-permute-start.8
  30.4 17.5 %conditional.2 = (f32[16,2,8,128]{3,2,1,0:T(8,128)S(1)}) conditional(s32[]{:T(128)} %convert_element_type.2, f32[16,2,8,128]{3,2,1,0:T(8,128)S(1)} %get-tuple-element.67, f32[16,2,8,128]{3,2,1,0:T(8,128)S(1)} %get-tuple-element.67), branch_computations={%region_0.0_spmd, %region_1.0_spmd} | conditional | bytes 524296 | solution.py:848
  30.4 17.5 %all_to_all.13 = f32[16,2,8,128]{3,2,1,0:T(8,128)S(1)} all-to-all(f32[16,2,8,128]{3,2,1,0:T(8,128)S(1)} %copy.10), channel_id=1, replica_groups=mesh['gx'=8,'gy'=2,'gc'=2] {'gx','gy'}, dimensions={0} | all-to-all | bytes 262144 | tf_op jit(solution)/shard_map/cond/branch_1_fun/all_to_all | solution.py:848
  47.9 0.0 collective-permute-done.9._.xa
  47.9 0.0 collective-permute-done.10.__.xb
  47.9 0.0 collective-permute-done.7.xa
  47.9 0.0 collective-permute-done.8.xb
  47.9 0.1 meet.1
  48.0 0.9 %collective-permute-start.15 = (f32[744,128]{1,0:T(8,128)S(1)}, f32[744,128]{1,0:T(8,128)S(1)}, u32[]{:S(2)}, u32[]{:S(2)}) collective-permute-start(f32[744,128]{1,0:T(8,128)S(1)} %get-tuple-element.90), channel_id=1, source_target_pairs={{0,4},{4,0},{8,12},{12,8},{16,20},{20,16},{24,28},{28,24},{1,5},{5... | collective-permute-start | bytes 1142792 | tf_op jit(solution)/shard_map/ppermute | solution.py:919
  48.9 0.7 collective-permute-start.16
  49.6 0.1 collective-permute-start.6
  49.7 0.7 collective-permute-start.12
  50.3 1.9 %collective-permute-start.11 = (f32[8,8,128]{2,1,0:T(8,128)S(1)}, f32[8,8,128]{2,1,0:T(8,128)S(1)}, u32[]{:S(2)}, u32[]{:S(2)}) collective-permute-start(f32[8,8,128]{2,1,0:T(8,128)S(1)} %get-tuple-element.78.own.own2), channel_id=1, source_target_pairs={{0,1},{1,0},{2,3},{3,2},{4,5},{5,4},{6,7},{7,6},{8,9},{9,8},{10,11... | collective-permute-start | bytes 98312 | tf_op jit(solution)/shard_map/ppermute | solution.py:922
  52.2 0.0 collective-permute-done.6.other
  52.2 3.4 %coarse.1 = (f32[3,10,3,8,128]{4,3,2,1,0:T(8,128)S(1)}, f32[32,128]{1,0:T(8,128)S(1)}) custom-call(f32[16,2,8,128]{3,2,1,0:T(8,128)S(1)} %get-tuple-element.92.own.___, f32[16,2,8,128]{3,2,1,0:T(8,128)S(1)} %collective-permute-done.6.other, f32[128,4096]{1,0:T(8,128)} %inverse_far.1), custom_call_target="tpu_custom_call" | custom-call | bytes 3000000 | tf_op jit(solution)/shard_map/coarse/pallas_call | solution.py:132
  55.6 0.0 collective-permute-done.12.zb
  55.6 0.0 collective-permute-done.11.za
  55.6 0.7 collective-permute-start.14
  56.3 7.4 %collective-permute-start.13 = (f32[14,8,128]{2,1,0:T(8,128)S(1)}, f32[14,8,128]{2,1,0:T(8,128)S(1)}, u32[]{:S(2)}, u32[]{:S(2)}) collective-permute-start(f32[14,8,128]{2,1,0:T(8,128)S(1)} %get-tuple-element.79._), channel_id=1, source_target_pairs={{0,4},{4,0},{8,12},{12,8},{16,20},{20,16},{24,28},{28,24},{1,5},{5... | collective-permute-start | bytes 172040 | tf_op jit(solution)/shard_map/ppermute | solution.py:935
  63.7 9.0 %conditional.3 = (f32[32,128]{1,0:T(8,128)S(1)}) conditional(s32[]{:T(128)} %convert_element_type.2, f32[32,128]{1,0:T(8,128)S(1)} %follow.1, f32[32,128]{1,0:T(8,128)S(1)} %follow.1), branch_computations={%region_2.0_spmd, %region_3.0_spmd} | conditional | bytes 65544 | solution.py:848
  63.7 9.0 %all_to_all.14 = f32[32,1,128]{2,1,0:T(1,128)S(1)} all-to-all(f32[32,1,128]{2,1,0:T(1,128)S(1)} %copy.11), channel_id=1, replica_groups=mesh['gx'=8,'gy'=2,'gc'=2] {'gx','gy','gc'}, dimensions={0} | all-to-all | bytes 32768 | tf_op jit(solution)/shard_map/cond/branch_1_fun/all_to_all | solution.py:848
  72.7 0.0 collective-permute-done.14.sides_b
  72.7 0.0 collective-permute-done.13.sides_a
  72.7 0.0 collective-permute-done.15.later_a
  72.7 0.0 collective-permute-done.16.later_b
  72.7 7.4 %up.1 = (f32[16,128,128]{2,1,0:T(8,128)}, f32[16,128,128]{2,1,0:T(8,128)}) custom-call(f32[32,128]{1,0:T(8,128)S(1)} %get-tuple-element.93.e, f32[3,10,3,8,128]{4,3,2,1,0:T(8,128)S(1)} %get-tuple-element.80.window3, f32[8,8,128]{2,1,0:T(8,128)S(1)} %get-tuple-element.78.own.own2, f32[8,8,128]{2,1,0:T(8,128)S(1)} %collective-permute-done.11.za, ...), custom_call_target="tpu_custom_call" | custom-call | bytes 3000000 | tf_op jit(solution)/shard_map/up/pallas_call | solution.py:132
  (4 shorter events, 0.0 us)
Async XLA Ops:
  0.6 7.3 %copy-start = (f32[16,128,128]{2,1,0:T(8,128)S(1)}, f32[16,128,128]{2,1,0:T(8,128)}, u32[]{:S(2)}) copy-start(f32[16,128,128]{2,1,0:T(8,128)} %v_in.1) | copy-start | bytes 3145732
  2.9 6.2 %collective-permute-start.1 = (f32[2,16,16,128]{3,2,1,0:T(8,128)S(1)}, f32[2,16,16,128]{3,2,1,0:T(8,128)S(1)}, u32[]{:S(2)}, u32[]{:S(2)}) collective-permute-start(f32[2,16,16,128]{3,2,1,0:T(8,128)S(1)} %get-tuple-element.56), channel_id=1, source_target_pairs={{1,2},{2,1},{5,6},{6,5},{9,10},{10,9},{13,14},{14,13},{17,18},{18,... | collective-permute-start | bytes 786440 | tf_op jit(solution)/shard_map/ppermute | solution.py:869
  3.5 5.5 %collective-permute-start = (f32[2,16,16,128]{3,2,1,0:T(8,128)S(1)}, f32[2,16,16,128]{3,2,1,0:T(8,128)S(1)}, u32[]{:S(2)}, u32[]{:S(2)}) collective-permute-start(f32[2,16,16,128]{3,2,1,0:T(8,128)S(1)} %get-tuple-element.53._), channel_id=1, source_target_pairs={{0,1},{1,0},{2,3},{3,2},{4,5},{5,4},{6,7},{7,6},{8,9},{9,8},{10,11... | collective-permute-start | bytes 786440 | tf_op jit(solution)/shard_map/ppermute | solution.py:868
  8.3 3.9 %collective-permute-start.2 = (f32[16,16,128]{2,1,0:T(8,128)S(1)}, f32[16,16,128]{2,1,0:T(8,128)S(1)}, u32[]{:S(2)}, u32[]{:S(2)}) collective-permute-start(f32[16,16,128]{2,1,0:T(8,128)S(1)} %get-tuple-element.58), channel_id=1, source_target_pairs={{0,1},{1,0},{2,3},{3,2},{4,5},{5,4},{6,7},{7,6},{8,9},{9,8},{10,11... | collective-permute-start | bytes 393224 | tf_op jit(solution)/shard_map/ppermute | solution.py:871
  8.4 3.8 %collective-permute-start.3 = (f32[16,16,128]{2,1,0:T(8,128)S(1)}, f32[16,16,128]{2,1,0:T(8,128)S(1)}, u32[]{:S(2)}, u32[]{:S(2)}) collective-permute-start(f32[16,16,128]{2,1,0:T(8,128)S(1)} %get-tuple-element.59), channel_id=1, source_target_pairs={{1,2},{2,1},{5,6},{6,5},{9,10},{10,9},{13,14},{14,13},{17,18},{18,... | collective-permute-start | bytes 393224 | tf_op jit(solution)/shard_map/ppermute | solution.py:872
  9.9 10.6 %collective-permute-start.4 = (f32[448,128]{1,0:T(8,128)S(1)}, f32[448,128]{1,0:T(8,128)S(1)}, u32[]{:S(2)}, u32[]{:S(2)}) collective-permute-start(f32[448,128]{1,0:T(8,128)S(1)} %get-tuple-element.65), channel_id=1, source_target_pairs={{0,4},{4,0},{8,12},{12,8},{16,20},{20,16},{24,28},{28,24},{1,5},{5... | collective-permute-start | bytes 688136 | tf_op jit(solution)/shard_map/ppermute | solution.py:879
  11.5 9.1 %collective-permute-start.5 = (f32[448,128]{1,0:T(8,128)S(1)}, f32[448,128]{1,0:T(8,128)S(1)}, u32[]{:S(2)}, u32[]{:S(2)}) collective-permute-start(f32[448,128]{1,0:T(8,128)S(1)} %get-tuple-element.66), channel_id=1, source_target_pairs={{4,8},{8,4},{12,16},{16,12},{20,24},{24,20},{5,9},{9,5},{13,17},{1... | collective-permute-start | bytes 688136 | tf_op jit(solution)/shard_map/ppermute | solution.py:880
  15.5 32.4 %collective-permute-start.9 = (f32[272,128]{1,0:T(8,128)S(1)}, f32[272,128]{1,0:T(8,128)S(1)}, u32[]{:S(2)}, u32[]{:S(2)}) collective-permute-start(f32[272,128]{1,0:T(8,128)S(1)} %get-tuple-element.76), channel_id=1, source_target_pairs={{0,4},{4,0},{8,12},{12,8},{16,20},{20,16},{24,28},{28,24},{1,5},{5... | collective-permute-start | bytes 417800 | tf_op jit(solution)/shard_map/ppermute | solution.py:890
  19.8 28.1 %collective-permute-start.10 = (f32[272,128]{1,0:T(8,128)S(1)}, f32[272,128]{1,0:T(8,128)S(1)}, u32[]{:S(2)}, u32[]{:S(2)}) collective-permute-start(f32[272,128]{1,0:T(8,128)S(1)} %get-tuple-element.77), channel_id=1, source_target_pairs={{4,8},{8,4},{12,16},{16,12},{20,24},{24,20},{5,9},{9,5},{13,17},{1... | collective-permute-start | bytes 417800 | tf_op jit(solution)/shard_map/ppermute | solution.py:891
  25.4 22.5 %collective-permute-start.7 = (f32[40,128]{1,0:T(8,128)S(1)}, f32[40,128]{1,0:T(8,128)S(1)}, u32[]{:S(2)}, u32[]{:S(2)}) collective-permute-start(f32[40,128]{1,0:T(8,128)S(1)} %get-tuple-element.70), channel_id=1, source_target_pairs={{0,4},{4,0},{8,12},{12,8},{16,20},{20,16},{24,28},{28,24},{1,5},{5... | collective-permute-start | bytes 61448 | tf_op jit(solution)/shard_map/ppermute | solution.py:912
  29.8 18.2 %collective-permute-start.8 = (f32[40,128]{1,0:T(8,128)S(1)}, f32[40,128]{1,0:T(8,128)S(1)}, u32[]{:S(2)}, u32[]{:S(2)}) collective-permute-start(f32[40,128]{1,0:T(8,128)S(1)} %get-tuple-element.71), channel_id=1, source_target_pairs={{4,8},{8,4},{12,16},{16,12},{20,24},{24,20},{5,9},{9,5},{13,17},{1... | collective-permute-start | bytes 61448 | tf_op jit(solution)/shard_map/ppermute | solution.py:913
  48.0 24.7 %collective-permute-start.15 = (f32[744,128]{1,0:T(8,128)S(1)}, f32[744,128]{1,0:T(8,128)S(1)}, u32[]{:S(2)}, u32[]{:S(2)}) collective-permute-start(f32[744,128]{1,0:T(8,128)S(1)} %get-tuple-element.90), channel_id=1, source_target_pairs={{0,4},{4,0},{8,12},{12,8},{16,20},{20,16},{24,28},{28,24},{1,5},{5... | collective-permute-start | bytes 1142792 | tf_op jit(solution)/shard_map/ppermute | solution.py:919
  48.9 23.8 %collective-permute-start.16 = (f32[744,128]{1,0:T(8,128)S(1)}, f32[744,128]{1,0:T(8,128)S(1)}, u32[]{:S(2)}, u32[]{:S(2)}) collective-permute-start(f32[744,128]{1,0:T(8,128)S(1)} %get-tuple-element.91), channel_id=1, source_target_pairs={{4,8},{8,4},{12,16},{16,12},{20,24},{24,20},{5,9},{9,5},{13,17},{1... | collective-permute-start | bytes 1142792 | tf_op jit(solution)/shard_map/ppermute | solution.py:920
  49.6 2.6 %collective-permute-start.6 = (f32[16,2,8,128]{3,2,1,0:T(8,128)S(1)}, f32[16,2,8,128]{3,2,1,0:T(8,128)S(1)}, u32[]{:S(2)}, u32[]{:S(2)}) collective-permute-start(f32[16,2,8,128]{3,2,1,0:T(8,128)S(1)} %get-tuple-element.92.own.___), channel_id=1, source_target_pairs={{0,1},{1,0},{2,3},{3,2},{4,5},{5,4},{6,7},{7,6},{8,9},{9,8},{10,11... | collective-permute-start | bytes 393224 | tf_op jit(solution)/shard_map/ppermute | solution.py:921
  49.7 5.9 %collective-permute-start.12 = (f32[8,8,128]{2,1,0:T(8,128)S(1)}, f32[8,8,128]{2,1,0:T(8,128)S(1)}, u32[]{:S(2)}, u32[]{:S(2)}) collective-permute-start(f32[8,8,128]{2,1,0:T(8,128)S(1)} %get-tuple-element.78.own.own2), channel_id=1, source_target_pairs={{1,2},{2,1},{5,6},{6,5},{9,10},{10,9},{13,14},{14,13},{17,18},{18,... | collective-permute-start | bytes 98312 | tf_op jit(solution)/shard_map/ppermute | solution.py:923
  50.3 5.3 %collective-permute-start.11 = (f32[8,8,128]{2,1,0:T(8,128)S(1)}, f32[8,8,128]{2,1,0:T(8,128)S(1)}, u32[]{:S(2)}, u32[]{:S(2)}) collective-permute-start(f32[8,8,128]{2,1,0:T(8,128)S(1)} %get-tuple-element.78.own.own2), channel_id=1, source_target_pairs={{0,1},{1,0},{2,3},{3,2},{4,5},{5,4},{6,7},{7,6},{8,9},{9,8},{10,11... | collective-permute-start | bytes 98312 | tf_op jit(solution)/shard_map/ppermute | solution.py:922
  55.6 17.1 %collective-permute-start.14 = (f32[14,8,128]{2,1,0:T(8,128)S(1)}, f32[14,8,128]{2,1,0:T(8,128)S(1)}, u32[]{:S(2)}, u32[]{:S(2)}) collective-permute-start(f32[14,8,128]{2,1,0:T(8,128)S(1)} %get-tuple-element.81), channel_id=1, source_target_pairs={{4,8},{8,4},{12,16},{16,12},{20,24},{24,20},{5,9},{9,5},{13,17},{1... | collective-permute-start | bytes 172040 | tf_op jit(solution)/shard_map/ppermute | solution.py:936
  56.3 16.4 %collective-permute-start.13 = (f32[14,8,128]{2,1,0:T(8,128)S(1)}, f32[14,8,128]{2,1,0:T(8,128)S(1)}, u32[]{:S(2)}, u32[]{:S(2)}) collective-permute-start(f32[14,8,128]{2,1,0:T(8,128)S(1)} %get-tuple-element.79._), channel_id=1, source_target_pairs={{0,4},{4,0},{8,12},{12,8},{16,20},{20,16},{24,28},{28,24},{1,5},{5... | collective-permute-start | bytes 172040 | tf_op jit(solution)/shard_map/ppermute | solution.py:935

commit v5 on v4

--- a/solution.py
+++ b/solution.py
@@ -185,7 +185,7 @@
     target[at, pl.ds(GUARD + DEEP + rows, DEEP)] = high
 
 
-def coefficient_kernel(c_in, za, zb, to_a, to_b, padded, c1):
+def coefficient_kernel(c_in, za, zb, _, __, to_a, to_b, padded, c1):
     odd_z = lax.axis_index("gc") == 1
     even_x = lax.axis_index("gx") % 2 == 0
     size_x, size_z, _ = c_in.shape
@@ -217,8 +217,8 @@
 
 def inner_kernel(
     f_in, v_in, c, za, zb, ya, yb,
-    f, v2, edges, f1, to_a, to_b, later_a, later_b, f_ends, c_ends,
-    va, vb, g, r,
+    f, v2, edges, f1, to_a, to_b, later_a, later_b, f_ends, c_ends, v_far,
+    va, vb, g, r, arrivals,
 ):
     odd_z = lax.axis_index("gc") == 1
     even_x = lax.axis_index("gx") % 2 == 0
@@ -249,6 +249,10 @@
                 here = pl.ds(start, rows)
                 center, total = around(source, x, start, rows, lane, LANES, x > 0, x < last)
                 target[x, here] = 0.2 * center + g[x, here] * (total + f[x, here])
+    copy = pltpu.make_async_copy(
+        v2.at[pl.ds(1, size_x - 2), pl.ds(GUARD + DEEP - KEEP, size_z + 2 * KEEP)], v_far, arrivals.at[0]
+    )
+    copy.start()
     for x in range(2, last - 1):
         for start, rows in parts:
             here = pl.ds(start, rows)
@@ -277,11 +281,12 @@
     for source, target in ((f, f_ends), (c, c_ends)):
         target[:, pl.ds(0, KEEP)] = source[:, pl.ds(GUARD + DEEP - KEEP, KEEP)]
         target[:, pl.ds(KEEP, KEEP)] = source[:, pl.ds(GUARD + DEEP + size_z, KEEP)]
+    copy.wait()
 
 
 def outer_kernel(
-    f, c, v2_in, edges, f1_in, c1_in, xa, xb,
-    chunk, near_a, near_b, to_a, to_b, v_far, sides_far, f1_far, c1_far, v1_out, level2, c2_out,
+    f, c, v2_in, edges, f1_in, c1_in, early_a, early_b, xa, xb,
+    chunk, near_a, near_b, to_a, to_b, v_far, sides_far, f1_far, c1_out, v1_out, level2, c2_out,
     v, c_out, v1, r, f1, c1, u1, w1, u2, r2, v2, f2, c2, arrivals,
 ):
     even_x = lax.axis_index("gx") % 2 == 0
@@ -300,9 +305,8 @@
         copies[-1].start()
 
     kept = pl.ds(GUARD + DEEP - KEEP, size_z + 2 * KEEP)
-    keep(v2_in.at[pl.ds(1, size_x - 2), kept], v_far.at[pl.ds(3, size_x - 2)])
-
-    for x in range(size_x):
+
+    for x in (0, 1, 2, size_x - 3, size_x - 2, size_x - 1):
         v[x + 2] = v2_in[x]
     for ref, planes in ((v, (0, 1, size_x + 2, size_x + 3)), (v1, (0, 1))):
         for at in planes:
@@ -341,8 +345,8 @@
                     weight = 6.0 + c_out[beside if k == -1 else past, here]
                 r[base + (4 + k) * inward, here] = total - weight * center
 
-    for at in (0, size_x + 1):
-        keep(v.at[pl.ds(at, 3), kept], v_far.at[pl.ds(at, 3)])
+    for k, at in enumerate((0, size_x + 1)):
+        keep(v.at[pl.ds(at, 3), kept], v_far.at[pl.ds(3 * k, 3)])
     keep(c_out.at[:, kept], sides_far)
 
     rows1 = size_z // 4 + 2 * GUARD
@@ -366,7 +370,7 @@
         c1[off1 + size1 + 1 + k, here1] = jnp.where(even_x, xa[rows], xb[rows])
     low1, high1 = off1 - 2, off1 + size1 + 1
     keep(f1.at[pl.ds(off1 - 2, size1 + 4), here1], f1_far)
-    keep(c1.at[pl.ds(off1 - 3, size1 + 6), here1], c1_far)
+    c1_out[...] = c1[pl.ds(off1 - 3, size1 + 6), here1]
     for at in range(low1 - 1, high1 + 2):
         for ref in (u1, w1):
             ref[at, pl.ds(0, GUARD)] = zeros8
@@ -448,6 +452,9 @@
         a[target] = jnp.where(even_x, right, left)
         b[target] = jnp.where(even_x, left, right)
 
+    for early, near in ((early_a, near_a), (early_b, near_b)):
+        near[pl.ds(40, early.shape[0])] = early[...]
+
     for at in range(size2 + 6):
         level2[at] = v2[at + 2, 2]
     for at in range(size2 + 4):
@@ -459,7 +466,7 @@
         copy.wait()
 
 
-def meet_kernel(level2, xa, xb, level1_a, level1_b, later_a, later_b, _, __, ___, own, to_a, to_b):
+def meet_kernel(level2, xa, xb, level1_a, level1_b, later_a, later_b, _, own, to_a, to_b):
     even_x = lax.axis_index("gx") % 2 == 0
     size2 = own.shape[0] // 2
     planes = [level2[3 + x] for x in range(size2)] + [level2[size2 + 8 + x] for x in range(size2)]
@@ -641,14 +648,19 @@
 
 
 def up_kernel(
-    nx, nz, e, window3, own2, za, zb, sides_a, sides_b, c2, v_far, f_far, c_far, sides_far, f1_far, c1_far, f_ends, c_ends, v1_in, xa, xb, later_a, later_b,
+    nx, nz, e, window3, own2, za, zb, sides_a, sides_b, c2, v_mid, v_edges, f_far, c_far, sides_far, f1_far, c1_in, f_ends, c_ends, v1_in, xa, xb, later_a, later_b,
     pressure_far, residual_far,
-    u3, lifted3, w3, turned, u2, w2, f2, f1, c1, u1, w1, lift1, ua, ub, g, lift0, before_in, after_in, sources, v_in, f_in, c_in, f_held, c_held, c_sides, f1_in, c1_in, pressure, residual, arrivals,
+    u3, lifted3, w3, turned, u2, w2, f2, f1, c1, u1, w1, lift1, ua, ub, g, lift0, before_in, after_in, sources, v_in, f_in, c_in, f_held, c_held, c_sides, f1_in, pressure, residual, arrivals,
 ):
     even_x = lax.axis_index("gx") % 2 == 0
     lane, sub = lanes_of(8), subs_of(8)
     zeros8 = jnp.zeros((GUARD, LANES), F32)
-    pairs = (f1_far, f1_in), (c1_far, c1_in), (sides_far, c_sides), (v_far, v_in), (c_far, c_held), (f_far, f_held)
+    size_x = f_ends.shape[0]
+    pairs = (
+        (f1_far, f1_in), (sides_far, c_sides), (v_mid, v_in.at[pl.ds(3, size_x - 2)]),
+        (v_edges.at[pl.ds(0, 3)], v_in.at[pl.ds(0, 3)]), (v_edges.at[pl.ds(3, 3)], v_in.at[pl.ds(size_x + 1, 3)]),
+        (c_far, c_held), (f_far, f_held),
+    )
     copies = [pltpu.make_async_copy(*pair, arrivals.at[k]) for k, pair in enumerate(pairs)]
     for copy in copies:
         copy.start()
@@ -710,7 +722,6 @@
         return jnp.where(even_x, b, a), jnp.where(even_x, a, b)
 
     copies[0].wait()
-    copies[1].wait()
     for x in range(-2, size1 + 2):
         f1[x + off1, here1] = f1_in[x + 2]
     for x in range(-3, size1 + 3):
@@ -762,7 +773,7 @@
         for at in range(size_x + 6):
             ref[at, pl.ds(0, GUARD)] = zeros8
             ref[at, pl.ds(GUARD + kept, GUARD)] = zeros8
-    for copy in copies[2:]:
+    for copy in copies[1:]:
         copy.wait()
     for held, part, target in ((f_held, f_ends, f_in), (c_held, c_ends, c_in)):
         for x in range(size_x):
@@ -790,7 +801,7 @@
     lane_s = lanes_of(sent)
     for ref in (before_in, after_in, sources):
         ref[...] = jnp.zeros(ref.shape, F32)
-    messages = [arrived(k * sent, sent) for k in range(EARLY)]
+    messages = [arrived(40 + k * sent, sent) for k in range(EARLY)]
     messages += [arrived(7 * rows1 + k * sent, sent, later_a, later_b) for k in range(5 - EARLY)]
     for side, (edge, inward) in enumerate(((off, 1), (last, -1))):
         before, after, source0, source1, source2 = (message[side] for message in messages)
@@ -873,7 +884,7 @@
 
     message = (2 * wide + 2 * rows1 + 32, LANES)
     mxa, mxb, c, c1 = call(
-        coefficient_kernel, "coefficients", (message, message, padded, padded1), (c, za, zb)
+        coefficient_kernel, "coefficients", (message, message, padded, padded1), (c, za, zb, ya, yb)
     )
     even_x, odd_x = pairs_of(nx)
     xa = lax.ppermute(mxa, "gx", even_x)
@@ -881,17 +892,15 @@
 
     margin, later = (EARLY * sent, LANES), ((5 - EARLY) * sent, LANES)
     held, ends = (size_x, kept, LANES), (size_x, 2 * KEEP, LANES)
-    f, v, edges, f1, mua, mub, mla, mlb, f_ends, c_ends = call(
+    f, v, edges, f1, mua, mub, mla, mlb, f_ends, c_ends, v_mid = call(
         inner_kernel, "inner",
-        (padded, padded, (4, deep, LANES), (size1 - 2, rows1, LANES), margin, margin, later, later, ends, ends),
+        (padded, padded, (4, deep, LANES), (size1 - 2, rows1, LANES), margin, margin, later, later, ends, ends, (size_x - 2, kept, LANES)),
         (f, v, c, za, zb, ya, yb),
-        [padded] * 4,
+        [padded] * 4, far_outs=(10,), copies=1,
     )
-    ua = lax.ppermute(mua, "gx", even_x)
-    ub = lax.ppermute(mub, "gx", odd_x)
 
     box2 = (size2 + 10, 5, 8, LANES)
-    near, level1 = (40, LANES), (7 * rows1, LANES)
+    near, level1 = (40 + EARLY * sent, LANES), (7 * rows1, LANES)
     sides0, sides1 = (4, deep, LANES), (2, rows1, LANES)
     parts1 = (size1 + 4, rows1, LANES), (size1 + 6, rows1, LANES)
     field0 = (size_x + 4, deep, LANES)
@@ -900,21 +909,21 @@
         outer_kernel, "outer",
         (
             (nx * nz // 2, 2, 8, LANES), near, near, level1, level1,
-            (size_x + 4, kept, LANES), (4, kept, LANES), *parts1, sides1, (2 * size2 + 10, 8, LANES), (size2 + 6, 3, 8, LANES),
+            (6, kept, LANES), (4, kept, LANES), *parts1, sides1, (2 * size2 + 10, 8, LANES), (size2 + 6, 3, 8, LANES),
         ),
-        (f, c, v, edges, f1, c1, xa, xb),
+        (f, c, v, edges, f1, c1, mua, mub, xa, xb),
         [
             field0, sides0, (2, deep, LANES), (12, deep, LANES), field1, field1, field1, field1,
             box2, (size2 + 10, 8, LANES), box2, box2, box2,
         ],
-        far_outs=range(5, 9), copies=6,
+        far_outs=range(5, 8), copies=4,
     )
     na = lax.ppermute(mna, "gx", even_x)
     nb = lax.ppermute(mnb, "gx", odd_x)
     own = gather(chunk, ("gx", "gy"), always)
     both = (7 * rows1 + (5 - EARLY) * sent, LANES)
     own2, mla, mlb = call(
-        meet_kernel, "meet", ((2 * size2, 8, LANES), both, both), (level2, na, nb, m1a, m1b, mla, mlb, ua, ub, own)
+        meet_kernel, "meet", ((2 * size2, 8, LANES), both, both), (level2, na, nb, m1a, m1b, mla, mlb, own)
     )
     la = lax.ppermute(mla, "gx", even_x)
     lb = lax.ppermute(mlb, "gx", odd_x)
@@ -943,12 +952,12 @@
     return call(
         functools.partial(up_kernel, nx, nz), "up",
         ((size_x, LANES, size_z), (size_x, LANES, size_z)),
-        (e, window3, own2, z2a, z2b, sa, sb, c2, v, right_side, reaction, c_sides, f1, c1, f_ends, c_ends, v1, ua, ub, la, lb),
+        (e, window3, own2, z2a, z2b, sa, sb, c2, v_mid, v, right_side, reaction, c_sides, f1, c1, f_ends, c_ends, v1, na, nb, la, lb),
         [
             box3, grid3, box3, (LANES, LANES), near2, near2, near2,
             field1, field1, field1, field1, (size2 + 4, rows1, LANES),
             box, box, box, (size1 + 4, kept, LANES), *[(2, kept + 2 * GUARD, LANES)] * 2, (4, kept + 2 * GUARD, LANES),
-            (size_x + 4, kept, LANES), held, held, right_side.shape, right_side.shape, (4, kept, LANES), *parts1,
+            (size_x + 4, kept, LANES), held, held, right_side.shape, right_side.shape, (4, kept, LANES), parts1[0],
             right_side.shape, right_side.shape,
         ],
         far_args=range(8, 14), far_outs=(0, 1), copies=8, results=True,

time: 80.7 us -> 79.3 us (0.983)
  starting transfers between devices: 30.3 us -> 25.8 us
  blocking collectives: 26.5 us -> 29 us
  waiting for transfers between devices: 0.09 us -> 1.23 us
    ppermute x2 -> x0, starting transfers between devices: 4.99 us -> none  [the longest x1 4.34 us: local(): ua = lax.ppermute(mua, 'gx', even_x)]
    all_to_all x2, blocking collectives: 26.5 us -> 29 us  [gather(): lax.all_to_all(x, axes, 0, 0, tiled=True)]
  transfers between devices with their start and end apart: 17 -> 15, of which waited for: 0 -> 2; matrix products, arithmetic and copies ran while one was open for 0% -> 0% of each run, Pallas kernels for 16% -> 9%
where the time goes in v5:
time: 79.3 us; the launch traced here: 78.9 us
  blocking collectives  29 us (37%)
  starting transfers between devices  25.8 us (33%)
  Pallas kernels  21.9 us (28%)
  waiting for transfers between devices  1.23 us (2%)
  between operations  0.96 us (1%)
    all_to_all x2, blocking collectives, gather(): lax.all_to_all(x, axes, 0, 0, tiled=True)  29 us
    pallas_call x10, Pallas kernels, call(): pl.pallas_call(kernel, out_shape=[jax.ShapeDtypeStruct(s, F32) if results...  21.9 us
    ppermute x1, starting transfers between devices, local(): sa = lax.ppermute(msa, 'gx', even_x)  7.27 us
    ppermute x1, starting transfers between devices, local(): na = lax.ppermute(mna, 'gx', even_x)  4.97 us
    ppermute x1, starting transfers between devices, local(): za = lax.ppermute(mza, ('gy', 'gc'), even_z)  4.38 us
    ppermute x1, starting transfers between devices, local(): z2a = lax.ppermute(own2, ('gy', 'gc'), even_z)  1.99 us
  transfers between devices with their start and end apart: 15, of which 2 were waited for; matrix products, arithmetic and copies ran while one was open for 0% of the time, Pallas kernels for 9%

profile of v5, /device:TPU:0, one launch (start us, length us, event | category | flops | bytes accessed | tf_op | source)
XLA Modules:
  0.0 78.9 jit_solution(17521308360857572960)
XLA Ops:
  0.6 0.0 copy-start
  0.6 2.2 %turn.1 = (f32[16,128,128]{2,1,0:T(8,128)S(1)}, f32[16,128,128]{2,1,0:T(8,128)S(1)}, f32[2,16,16,128]{3,2,1,0:T(8,128)S(1)}, f32[2,16,16,128]{3,2,1,0:T(8,128)S(1)}) custom-call(f32[16,128,128]{2,1,0:T(8,128)} %c_far.1, f32[16,128,128]{2,1,0:T(8,128)} %f_far.1, s32[1,1]{1,0:T(1,128)} %bitcast.2.refs_2_), custom_call_target="tpu_custom_call" | custom-call | bytes 3000000 | tf_op jit(solution)/shard_map/turn/pallas_call | solution.py:132
  2.9 0.7 collective-permute-start.1
  3.5 4.4 %collective-permute-start = (f32[2,16,16,128]{3,2,1,0:T(8,128)S(1)}, f32[2,16,16,128]{3,2,1,0:T(8,128)S(1)}, u32[]{:S(2)}, u32[]{:S(2)}) collective-permute-start(f32[2,16,16,128]{3,2,1,0:T(8,128)S(1)} %get-tuple-element.54._), channel_id=1, source_target_pairs={{0,1},{1,0},{2,3},{3,2},{4,5},{5,4},{6,7},{7,6},{8,9},{9,8},{10,11... | collective-permute-start | bytes 786440 | tf_op jit(solution)/shard_map/ppermute | solution.py:879
  7.9 0.0 copy-done
  7.9 0.3 turn_again.1
  8.3 0.1 collective-permute-start.2
  8.4 0.7 collective-permute-start.3
  9.0 0.7 collective-permute-done.2._.ya
  9.7 0.0 collective-permute-done.3.__.yb
  9.7 0.0 collective-permute-done.1.zb
  9.7 0.0 collective-permute-done.za
  9.7 0.8 %coefficients.1 = (f32[448,128]{1,0:T(8,128)S(1)}, f32[448,128]{1,0:T(8,128)S(1)}, f32[16,176,128]{2,1,0:T(8,128)S(1)}, f32[8,64,128]{2,1,0:T(8,128)S(1)}) custom-call(f32[16,128,128]{2,1,0:T(8,128)S(1)} %get-tuple-element.56.c_in, f32[2,16,16,128]{3,2,1,0:T(8,128)S(1)} %collective-permute-done.za, f32[2,16,16,128]{3,2,1,0:T(8,128)S(1)} %collective-permute-done.1.zb, ...), custom_call_target="tpu_custom_call" | custom-call | bytes 3000000 | tf_op jit(solution)/shard_map/coefficients/pallas_call | solution.py:132
  10.5 1.6 %collective-permute-start.4 = (f32[448,128]{1,0:T(8,128)S(1)}, f32[448,128]{1,0:T(8,128)S(1)}, u32[]{:S(2)}, u32[]{:S(2)}) collective-permute-start(f32[448,128]{1,0:T(8,128)S(1)} %get-tuple-element.68), channel_id=1, source_target_pairs={{0,4},{4,0},{8,12},{12,8},{16,20},{20,16},{24,28},{28,24},{1,5},{5... | collective-permute-start | bytes 688136 | tf_op jit(solution)/shard_map/ppermute | solution.py:890
  12.1 0.7 collective-permute-start.5
  12.7 3.3 %inner.1 = (f32[16,176,128]{2,1,0:T(8,128)S(1)}, f32[16,176,128]{2,1,0:T(8,128)S(1)}, f32[4,176,128]{2,1,0:T(8,128)S(1)}, f32[6,48,128]{2,1,0:T(8,128)S(1)}, f32...) custom-call(f32[16,128,128]{2,1,0:T(8,128)S(1)} %get-tuple-element.5, ...), custom_call_target="tpu_custom_call" | custom-call | bytes 3000000 | tf_op jit(solution)/shard_map/inner/pallas_call | solution.py:132
  16.1 0.5 collective-permute-done.4.xa
  16.6 0.0 collective-permute-done.5.xb
  16.6 4.4 %outer.1 = (f32[16,2,8,128]{3,2,1,0:T(8,128)S(1)}, f32[312,128]{1,0:T(8,128)S(1)}, f32[312,128]{1,0:T(8,128)S(1)}, f32[336,128]{1,0:T(8,128)S(1)}, f32[336,128]{...) custom-call(f32[16,176,128]{2,1,0:T(8,128)S(1)} %get-tuple-element.6, ...), custom_call_target="tpu_custom_call" | custom-call | bytes 3000000 | tf_op jit(solution)/shard_map/outer/pallas_call | solution.py:132
  21.1 5.0 %collective-permute-start.7 = (f32[312,128]{1,0:T(8,128)S(1)}, f32[312,128]{1,0:T(8,128)S(1)}, u32[]{:S(2)}, u32[]{:S(2)}) collective-permute-start(f32[312,128]{1,0:T(8,128)S(1)} %get-tuple-element.73), channel_id=1, source_target_pairs={{0,4},{4,0},{8,12},{12,8},{16,20},{20,16},{24,28},{28,24},{1,5},{5... | collective-permute-start | bytes 479240 | tf_op jit(solution)/shard_map/ppermute | solution.py:921
  26.0 0.7 collective-permute-start.8
  26.7 19.9 %conditional.2 = (f32[16,2,8,128]{3,2,1,0:T(8,128)S(1)}) conditional(s32[]{:T(128)} %convert_element_type.2, f32[16,2,8,128]{3,2,1,0:T(8,128)S(1)} %get-tuple-element.70, f32[16,2,8,128]{3,2,1,0:T(8,128)S(1)} %get-tuple-element.70), branch_computations={%region_0.0_spmd, %region_1.0_spmd} | conditional | bytes 524296 | solution.py:859
  26.7 19.9 %all_to_all.13 = f32[16,2,8,128]{3,2,1,0:T(8,128)S(1)} all-to-all(f32[16,2,8,128]{3,2,1,0:T(8,128)S(1)} %copy.10), channel_id=1, replica_groups=mesh['gx'=8,'gy'=2,'gc'=2] {'gx','gy'}, dimensions={0} | all-to-all | bytes 262144 | tf_op jit(solution)/shard_map/cond/branch_1_fun/all_to_all | solution.py:859
  46.6 0.0 collective-permute-done.7.xa
  46.6 0.0 collective-permute-done.8.xb
  46.6 0.1 meet.1
  46.6 0.8 %collective-permute-start.13 = (f32[744,128]{1,0:T(8,128)S(1)}, f32[744,128]{1,0:T(8,128)S(1)}, u32[]{:S(2)}, u32[]{:S(2)}) collective-permute-start(f32[744,128]{1,0:T(8,128)S(1)} %get-tuple-element.92), channel_id=1, source_target_pairs={{0,4},{4,0},{8,12},{12,8},{16,20},{20,16},{24,28},{28,24},{1,5},{5... | collective-permute-start | bytes 1142792 | tf_op jit(solution)/shard_map/ppermute | solution.py:928
  47.5 0.7 collective-permute-start.14
  48.1 0.1 collective-permute-start.6
  48.2 0.7 collective-permute-start.10
  48.9 2.0 %collective-permute-start.9 = (f32[8,8,128]{2,1,0:T(8,128)S(1)}, f32[8,8,128]{2,1,0:T(8,128)S(1)}, u32[]{:S(2)}, u32[]{:S(2)}) collective-permute-start(f32[8,8,128]{2,1,0:T(8,128)S(1)} %get-tuple-element.79.own.own2), channel_id=1, source_target_pairs={{0,1},{1,0},{2,3},{3,2},{4,5},{5,4},{6,7},{7,6},{8,9},{9,8},{10,11... | collective-permute-start | bytes 98312 | tf_op jit(solution)/shard_map/ppermute | solution.py:931
  50.9 0.0 collective-permute-done.6.other
  50.9 3.4 %coarse.1 = (f32[3,10,3,8,128]{4,3,2,1,0:T(8,128)S(1)}, f32[32,128]{1,0:T(8,128)S(1)}) custom-call(f32[16,2,8,128]{3,2,1,0:T(8,128)S(1)} %get-tuple-element.94.own._, f32[16,2,8,128]{3,2,1,0:T(8,128)S(1)} %collective-permute-done.6.other, f32[128,4096]{1,0:T(8,128)} %inverse_far.1), custom_call_target="tpu_custom_call" | custom-call | bytes 3000000 | tf_op jit(solution)/shard_map/coarse/pallas_call | solution.py:132
  54.2 0.0 collective-permute-done.10.zb
  54.2 0.0 collective-permute-done.9.za
  54.3 0.7 collective-permute-start.12
  55.0 7.3 %collective-permute-start.11 = (f32[14,8,128]{2,1,0:T(8,128)S(1)}, f32[14,8,128]{2,1,0:T(8,128)S(1)}, u32[]{:S(2)}, u32[]{:S(2)}) collective-permute-start(f32[14,8,128]{2,1,0:T(8,128)S(1)} %get-tuple-element.80._), channel_id=1, source_target_pairs={{0,4},{4,0},{8,12},{12,8},{16,20},{20,16},{24,28},{28,24},{1,5},{5... | collective-permute-start | bytes 172040 | tf_op jit(solution)/shard_map/ppermute | solution.py:944
  62.2 9.1 %conditional.3 = (f32[32,128]{1,0:T(8,128)S(1)}) conditional(s32[]{:T(128)} %convert_element_type.2, f32[32,128]{1,0:T(8,128)S(1)} %follow.1, f32[32,128]{1,0:T(8,128)S(1)} %follow.1), branch_computations={%region_2.0_spmd, %region_3.0_spmd} | conditional | bytes 65544 | solution.py:859
  62.2 9.1 %all_to_all.14 = f32[32,1,128]{2,1,0:T(1,128)S(1)} all-to-all(f32[32,1,128]{2,1,0:T(1,128)S(1)} %copy.11), channel_id=1, replica_groups=mesh['gx'=8,'gy'=2,'gc'=2] {'gx','gy','gc'}, dimensions={0} | all-to-all | bytes 32768 | tf_op jit(solution)/shard_map/cond/branch_1_fun/all_to_all | solution.py:859
  71.4 0.0 collective-permute-done.12.sides_b
  71.4 0.0 collective-permute-done.11.sides_a
  71.4 0.0 collective-permute-done.13.later_a
  71.4 0.0 collective-permute-done.14.later_b
  71.4 7.4 %up.1 = (f32[16,128,128]{2,1,0:T(8,128)}, f32[16,128,128]{2,1,0:T(8,128)}) custom-call(f32[32,128]{1,0:T(8,128)S(1)} %get-tuple-element.95.e, f32[3,10,3,8,128]{4,3,2,1,0:T(8,128)S(1)} %get-tuple-element.81.window3, f32[8,8,128]{2,1,0:T(8,128)S(1)} %get-tuple-element.79.own.own2, f32[8,8,128]{2,1,0:T(8,128)S(1)} %collective-permute-done.9.za, ...), custom_call_target="tpu_custom_call" | custom-call | bytes 3000000 | tf_op jit(solution)/shard_map/up/pallas_call | solution.py:132
  (4 shorter events, 0.0 us)
Async XLA Ops:
  0.6 7.3 %copy-start = (f32[16,128,128]{2,1,0:T(8,128)S(1)}, f32[16,128,128]{2,1,0:T(8,128)}, u32[]{:S(2)}) copy-start(f32[16,128,128]{2,1,0:T(8,128)} %v_in.1) | copy-start | bytes 3145732
  2.9 6.8 %collective-permute-start.1 = (f32[2,16,16,128]{3,2,1,0:T(8,128)S(1)}, f32[2,16,16,128]{3,2,1,0:T(8,128)S(1)}, u32[]{:S(2)}, u32[]{:S(2)}) collective-permute-start(f32[2,16,16,128]{3,2,1,0:T(8,128)S(1)} %get-tuple-element.57), channel_id=1, source_target_pairs={{1,2},{2,1},{5,6},{6,5},{9,10},{10,9},{13,14},{14,13},{17,18},{18,... | collective-permute-start | bytes 786440 | tf_op jit(solution)/shard_map/ppermute | solution.py:880
  3.5 6.2 %collective-permute-start = (f32[2,16,16,128]{3,2,1,0:T(8,128)S(1)}, f32[2,16,16,128]{3,2,1,0:T(8,128)S(1)}, u32[]{:S(2)}, u32[]{:S(2)}) collective-permute-start(f32[2,16,16,128]{3,2,1,0:T(8,128)S(1)} %get-tuple-element.54._), channel_id=1, source_target_pairs={{0,1},{1,0},{2,3},{3,2},{4,5},{5,4},{6,7},{7,6},{8,9},{9,8},{10,11... | collective-permute-start | bytes 786440 | tf_op jit(solution)/shard_map/ppermute | solution.py:879
  8.3 1.4 %collective-permute-start.2 = (f32[16,16,128]{2,1,0:T(8,128)S(1)}, f32[16,16,128]{2,1,0:T(8,128)S(1)}, u32[]{:S(2)}, u32[]{:S(2)}) collective-permute-start(f32[16,16,128]{2,1,0:T(8,128)S(1)} %get-tuple-element.58), channel_id=1, source_target_pairs={{0,1},{1,0},{2,3},{3,2},{4,5},{5,4},{6,7},{7,6},{8,9},{9,8},{10,11... | collective-permute-start | bytes 393224 | tf_op jit(solution)/shard_map/ppermute | solution.py:882
  8.4 1.3 %collective-permute-start.3 = (f32[16,16,128]{2,1,0:T(8,128)S(1)}, f32[16,16,128]{2,1,0:T(8,128)S(1)}, u32[]{:S(2)}, u32[]{:S(2)}) collective-permute-start(f32[16,16,128]{2,1,0:T(8,128)S(1)} %get-tuple-element.59), channel_id=1, source_target_pairs={{1,2},{2,1},{5,6},{6,5},{9,10},{10,9},{13,14},{14,13},{17,18},{18,... | collective-permute-start | bytes 393224 | tf_op jit(solution)/shard_map/ppermute | solution.py:883
  10.5 6.1 %collective-permute-start.4 = (f32[448,128]{1,0:T(8,128)S(1)}, f32[448,128]{1,0:T(8,128)S(1)}, u32[]{:S(2)}, u32[]{:S(2)}) collective-permute-start(f32[448,128]{1,0:T(8,128)S(1)} %get-tuple-element.68), channel_id=1, source_target_pairs={{0,4},{4,0},{8,12},{12,8},{16,20},{20,16},{24,28},{28,24},{1,5},{5... | collective-permute-start | bytes 688136 | tf_op jit(solution)/shard_map/ppermute | solution.py:890
  12.1 4.5 %collective-permute-start.5 = (f32[448,128]{1,0:T(8,128)S(1)}, f32[448,128]{1,0:T(8,128)S(1)}, u32[]{:S(2)}, u32[]{:S(2)}) collective-permute-start(f32[448,128]{1,0:T(8,128)S(1)} %get-tuple-element.69), channel_id=1, source_target_pairs={{4,8},{8,4},{12,16},{16,12},{20,24},{24,20},{5,9},{9,5},{13,17},{1... | collective-permute-start | bytes 688136 | tf_op jit(solution)/shard_map/ppermute | solution.py:891
  21.1 25.5 %collective-permute-start.7 = (f32[312,128]{1,0:T(8,128)S(1)}, f32[312,128]{1,0:T(8,128)S(1)}, u32[]{:S(2)}, u32[]{:S(2)}) collective-permute-start(f32[312,128]{1,0:T(8,128)S(1)} %get-tuple-element.73), channel_id=1, source_target_pairs={{0,4},{4,0},{8,12},{12,8},{16,20},{20,16},{24,28},{28,24},{1,5},{5... | collective-permute-start | bytes 479240 | tf_op jit(solution)/shard_map/ppermute | solution.py:921
  26.0 20.6 %collective-permute-start.8 = (f32[312,128]{1,0:T(8,128)S(1)}, f32[312,128]{1,0:T(8,128)S(1)}, u32[]{:S(2)}, u32[]{:S(2)}) collective-permute-start(f32[312,128]{1,0:T(8,128)S(1)} %get-tuple-element.74), channel_id=1, source_target_pairs={{4,8},{8,4},{12,16},{16,12},{20,24},{24,20},{5,9},{9,5},{13,17},{1... | collective-permute-start | bytes 479240 | tf_op jit(solution)/shard_map/ppermute | solution.py:922
  46.6 24.7 %collective-permute-start.13 = (f32[744,128]{1,0:T(8,128)S(1)}, f32[744,128]{1,0:T(8,128)S(1)}, u32[]{:S(2)}, u32[]{:S(2)}) collective-permute-start(f32[744,128]{1,0:T(8,128)S(1)} %get-tuple-element.92), channel_id=1, source_target_pairs={{0,4},{4,0},{8,12},{12,8},{16,20},{20,16},{24,28},{28,24},{1,5},{5... | collective-permute-start | bytes 1142792 | tf_op jit(solution)/shard_map/ppermute | solution.py:928
  47.5 23.9 %collective-permute-start.14 = (f32[744,128]{1,0:T(8,128)S(1)}, f32[744,128]{1,0:T(8,128)S(1)}, u32[]{:S(2)}, u32[]{:S(2)}) collective-permute-start(f32[744,128]{1,0:T(8,128)S(1)} %get-tuple-element.93), channel_id=1, source_target_pairs={{4,8},{8,4},{12,16},{16,12},{20,24},{24,20},{5,9},{9,5},{13,17},{1... | collective-permute-start | bytes 1142792 | tf_op jit(solution)/shard_map/ppermute | solution.py:929
  48.1 2.7 %collective-permute-start.6 = (f32[16,2,8,128]{3,2,1,0:T(8,128)S(1)}, f32[16,2,8,128]{3,2,1,0:T(8,128)S(1)}, u32[]{:S(2)}, u32[]{:S(2)}) collective-permute-start(f32[16,2,8,128]{3,2,1,0:T(8,128)S(1)} %get-tuple-element.94.own._), channel_id=1, source_target_pairs={{0,1},{1,0},{2,3},{3,2},{4,5},{5,4},{6,7},{7,6},{8,9},{9,8},{10,11... | collective-permute-start | bytes 393224 | tf_op jit(solution)/shard_map/ppermute | solution.py:930
  48.2 6.0 %collective-permute-start.10 = (f32[8,8,128]{2,1,0:T(8,128)S(1)}, f32[8,8,128]{2,1,0:T(8,128)S(1)}, u32[]{:S(2)}, u32[]{:S(2)}) collective-permute-start(f32[8,8,128]{2,1,0:T(8,128)S(1)} %get-tuple-element.79.own.own2), channel_id=1, source_target_pairs={{1,2},{2,1},{5,6},{6,5},{9,10},{10,9},{13,14},{14,13},{17,18},{18,... | collective-permute-start | bytes 98312 | tf_op jit(solution)/shard_map/ppermute | solution.py:932
  48.9 5.4 %collective-permute-start.9 = (f32[8,8,128]{2,1,0:T(8,128)S(1)}, f32[8,8,128]{2,1,0:T(8,128)S(1)}, u32[]{:S(2)}, u32[]{:S(2)}) collective-permute-start(f32[8,8,128]{2,1,0:T(8,128)S(1)} %get-tuple-element.79.own.own2), channel_id=1, source_target_pairs={{0,1},{1,0},{2,3},{3,2},{4,5},{5,4},{6,7},{7,6},{8,9},{9,8},{10,11... | collective-permute-start | bytes 98312 | tf_op jit(solution)/shard_map/ppermute | solution.py:931
  54.3 17.1 %collective-permute-start.12 = (f32[14,8,128]{2,1,0:T(8,128)S(1)}, f32[14,8,128]{2,1,0:T(8,128)S(1)}, u32[]{:S(2)}, u32[]{:S(2)}) collective-permute-start(f32[14,8,128]{2,1,0:T(8,128)S(1)} %get-tuple-element.82), channel_id=1, source_target_pairs={{4,8},{8,4},{12,16},{16,12},{20,24},{24,20},{5,9},{9,5},{13,17},{1... | collective-permute-start | bytes 172040 | tf_op jit(solution)/shard_map/ppermute | solution.py:945
  55.0 16.4 %collective-permute-start.11 = (f32[14,8,128]{2,1,0:T(8,128)S(1)}, f32[14,8,128]{2,1,0:T(8,128)S(1)}, u32[]{:S(2)}, u32[]{:S(2)}) collective-permute-start(f32[14,8,128]{2,1,0:T(8,128)S(1)} %get-tuple-element.80._), channel_id=1, source_target_pairs={{0,4},{4,0},{8,12},{12,8},{16,20},{20,16},{24,28},{28,24},{1,5},{5... | collective-permute-start | bytes 172040 | tf_op jit(solution)/shard_map/ppermute | solution.py:944

commit v6 on v5

--- a/solution.py
+++ b/solution.py
@@ -749,7 +749,7 @@
         if 2 <= at < planes1 - 2:
             center, total = around(u1, at, GUARD, rows1, lane1, 64)
             value = 0.2 * center + c1[at, here1] * (total + f1[at, here1])
-        w1[at, here1] = value + lift1[at // 2]
+        w1[at, here1] = value + lift1[at // 2, pl.ds(0, rows1)]
     for source, target, margin in ((w1, u1, 1), (u1, w1, 2)):
         for at in range(margin, planes1 - margin):
             center, total = around(source, at, GUARD, rows1, lane1, 64)
@@ -782,7 +782,7 @@
         target[:, pl.ds(KEEP + size_z, KEEP)] = part[:, pl.ds(KEEP, KEEP)]
     shift = -GUARD
     for x in range(-3, size_x + 3):
-        value = lift0[(x + 4) // 2]
+        value = lift0[(x + 4) // 2, pl.ds(0, kept)]
         if -2 <= x <= size_x + 1:
             value = value + v_in[x + 2, pl.ds(GUARD + shift, kept)]
         ua[x + off, here] = value
@@ -955,8 +955,8 @@
         (e, window3, own2, z2a, z2b, sa, sb, c2, v_mid, v, right_side, reaction, c_sides, f1, c1, f_ends, c_ends, v1, na, nb, la, lb),
         [
             box3, grid3, box3, (LANES, LANES), near2, near2, near2,
-            field1, field1, field1, field1, (size2 + 4, rows1, LANES),
-            box, box, box, (size1 + 4, kept, LANES), *[(2, kept + 2 * GUARD, LANES)] * 2, (4, kept + 2 * GUARD, LANES),
+            field1, field1, field1, field1, (size2 + 4, rows1 + 2 * GUARD, LANES),
+            box, box, box, (size1 + 4, kept + 2 * GUARD, LANES), *[(2, kept + 2 * GUARD, LANES)] * 2, (4, kept + 2 * GUARD, LANES),
             (size_x + 4, kept, LANES), held, held, right_side.shape, right_side.shape, (4, kept, LANES), parts1[0],
             right_side.shape, right_side.shape,
         ],

time: 79.3 us -> 79.3 us (level)
  no operation moved by 1% of the time
where the time goes in v6:
time: 79.3 us; the launch traced here: 78.9 us
  blocking collectives  29 us (37%)
  starting transfers between devices  25.8 us (33%)
  Pallas kernels  21.9 us (28%)
  waiting for transfers between devices  1.23 us (2%)
  between operations  0.96 us (1%)
    all_to_all x2, blocking collectives, gather(): lax.all_to_all(x, axes, 0, 0, tiled=True)  29 us
    pallas_call x10, Pallas kernels, call(): pl.pallas_call(kernel, out_shape=[jax.ShapeDtypeStruct(s, F32) if results...  21.9 us
    ppermute x1, starting transfers between devices, local(): sa = lax.ppermute(msa, 'gx', even_x)  7.27 us
    ppermute x1, starting transfers between devices, local(): na = lax.ppermute(mna, 'gx', even_x)  4.97 us
    ppermute x1, starting transfers between devices, local(): za = lax.ppermute(mza, ('gy', 'gc'), even_z)  4.38 us
    ppermute x1, starting transfers between devices, local(): z2a = lax.ppermute(own2, ('gy', 'gc'), even_z)  1.99 us
  transfers between devices with their start and end apart: 15, of which 2 were waited for; matrix products, arithmetic and copies ran while one was open for 0% of the time, Pallas kernels for 9%

profile of v6, /device:TPU:0, one launch (start us, length us, event | category | flops | bytes accessed | tf_op | source)
XLA Modules:
  0.0 78.9 jit_solution(9131457016444869435)
XLA Ops:
  0.6 0.0 copy-start
  0.6 2.2 %turn.1 = (f32[16,128,128]{2,1,0:T(8,128)S(1)}, f32[16,128,128]{2,1,0:T(8,128)S(1)}, f32[2,16,16,128]{3,2,1,0:T(8,128)S(1)}, f32[2,16,16,128]{3,2,1,0:T(8,128)S(1)}) custom-call(f32[16,128,128]{2,1,0:T(8,128)} %c_far.1, f32[16,128,128]{2,1,0:T(8,128)} %f_far.1, s32[1,1]{1,0:T(1,128)} %bitcast.2.refs_2_), custom_call_target="tpu_custom_call" | custom-call | bytes 3000000 | tf_op jit(solution)/shard_map/turn/pallas_call | solution.py:132
  2.9 0.7 collective-permute-start.1
  3.5 4.4 %collective-permute-start = (f32[2,16,16,128]{3,2,1,0:T(8,128)S(1)}, f32[2,16,16,128]{3,2,1,0:T(8,128)S(1)}, u32[]{:S(2)}, u32[]{:S(2)}) collective-permute-start(f32[2,16,16,128]{3,2,1,0:T(8,128)S(1)} %get-tuple-element.54._), channel_id=1, source_target_pairs={{0,1},{1,0},{2,3},{3,2},{4,5},{5,4},{6,7},{7,6},{8,9},{9,8},{10,11... | collective-permute-start | bytes 786440 | tf_op jit(solution)/shard_map/ppermute | solution.py:879
  7.9 0.0 copy-done
  7.9 0.3 turn_again.1
  8.3 0.1 collective-permute-start.2
  8.4 0.7 collective-permute-start.3
  9.0 0.7 collective-permute-done.2._.ya
  9.7 0.0 collective-permute-done.3.__.yb
  9.7 0.0 collective-permute-done.1.zb
  9.7 0.0 collective-permute-done.za
  9.7 0.8 %coefficients.1 = (f32[448,128]{1,0:T(8,128)S(1)}, f32[448,128]{1,0:T(8,128)S(1)}, f32[16,176,128]{2,1,0:T(8,128)S(1)}, f32[8,64,128]{2,1,0:T(8,128)S(1)}) custom-call(f32[16,128,128]{2,1,0:T(8,128)S(1)} %get-tuple-element.56.c_in, f32[2,16,16,128]{3,2,1,0:T(8,128)S(1)} %collective-permute-done.za, f32[2,16,16,128]{3,2,1,0:T(8,128)S(1)} %collective-permute-done.1.zb, ...), custom_call_target="tpu_custom_call" | custom-call | bytes 3000000 | tf_op jit(solution)/shard_map/coefficients/pallas_call | solution.py:132
  10.5 1.6 %collective-permute-start.4 = (f32[448,128]{1,0:T(8,128)S(1)}, f32[448,128]{1,0:T(8,128)S(1)}, u32[]{:S(2)}, u32[]{:S(2)}) collective-permute-start(f32[448,128]{1,0:T(8,128)S(1)} %get-tuple-element.68), channel_id=1, source_target_pairs={{0,4},{4,0},{8,12},{12,8},{16,20},{20,16},{24,28},{28,24},{1,5},{5... | collective-permute-start | bytes 688136 | tf_op jit(solution)/shard_map/ppermute | solution.py:890
  12.1 0.7 collective-permute-start.5
  12.7 3.3 %inner.1 = (f32[16,176,128]{2,1,0:T(8,128)S(1)}, f32[16,176,128]{2,1,0:T(8,128)S(1)}, f32[4,176,128]{2,1,0:T(8,128)S(1)}, f32[6,48,128]{2,1,0:T(8,128)S(1)}, f32...) custom-call(f32[16,128,128]{2,1,0:T(8,128)S(1)} %get-tuple-element.5, ...), custom_call_target="tpu_custom_call" | custom-call | bytes 3000000 | tf_op jit(solution)/shard_map/inner/pallas_call | solution.py:132
  16.1 0.5 collective-permute-done.4.xa
  16.6 0.0 collective-permute-done.5.xb
  16.6 4.4 %outer.1 = (f32[16,2,8,128]{3,2,1,0:T(8,128)S(1)}, f32[312,128]{1,0:T(8,128)S(1)}, f32[312,128]{1,0:T(8,128)S(1)}, f32[336,128]{1,0:T(8,128)S(1)}, f32[336,128]{...) custom-call(f32[16,176,128]{2,1,0:T(8,128)S(1)} %get-tuple-element.6, ...), custom_call_target="tpu_custom_call" | custom-call | bytes 3000000 | tf_op jit(solution)/shard_map/outer/pallas_call | solution.py:132
  21.1 5.0 %collective-permute-start.7 = (f32[312,128]{1,0:T(8,128)S(1)}, f32[312,128]{1,0:T(8,128)S(1)}, u32[]{:S(2)}, u32[]{:S(2)}) collective-permute-start(f32[312,128]{1,0:T(8,128)S(1)} %get-tuple-element.73), channel_id=1, source_target_pairs={{0,4},{4,0},{8,12},{12,8},{16,20},{20,16},{24,28},{28,24},{1,5},{5... | collective-permute-start | bytes 479240 | tf_op jit(solution)/shard_map/ppermute | solution.py:921
  26.0 0.7 collective-permute-start.8
  26.7 19.9 %conditional.2 = (f32[16,2,8,128]{3,2,1,0:T(8,128)S(1)}) conditional(s32[]{:T(128)} %convert_element_type.2, f32[16,2,8,128]{3,2,1,0:T(8,128)S(1)} %get-tuple-element.70, f32[16,2,8,128]{3,2,1,0:T(8,128)S(1)} %get-tuple-element.70), branch_computations={%region_0.0_spmd, %region_1.0_spmd} | conditional | bytes 524296 | solution.py:859
  26.7 19.9 %all_to_all.13 = f32[16,2,8,128]{3,2,1,0:T(8,128)S(1)} all-to-all(f32[16,2,8,128]{3,2,1,0:T(8,128)S(1)} %copy.10), channel_id=1, replica_groups=mesh['gx'=8,'gy'=2,'gc'=2] {'gx','gy'}, dimensions={0} | all-to-all | bytes 262144 | tf_op jit(solution)/shard_map/cond/branch_1_fun/all_to_all | solution.py:859
  46.6 0.0 collective-permute-done.7.xa
  46.6 0.0 collective-permute-done.8.xb
  46.6 0.1 meet.1
  46.6 0.8 %collective-permute-start.13 = (f32[744,128]{1,0:T(8,128)S(1)}, f32[744,128]{1,0:T(8,128)S(1)}, u32[]{:S(2)}, u32[]{:S(2)}) collective-permute-start(f32[744,128]{1,0:T(8,128)S(1)} %get-tuple-element.92), channel_id=1, source_target_pairs={{0,4},{4,0},{8,12},{12,8},{16,20},{20,16},{24,28},{28,24},{1,5},{5... | collective-permute-start | bytes 1142792 | tf_op jit(solution)/shard_map/ppermute | solution.py:928
  47.5 0.7 collective-permute-start.14
  48.1 0.1 collective-permute-start.6
  48.2 0.7 collective-permute-start.10
  48.9 2.0 %collective-permute-start.9 = (f32[8,8,128]{2,1,0:T(8,128)S(1)}, f32[8,8,128]{2,1,0:T(8,128)S(1)}, u32[]{:S(2)}, u32[]{:S(2)}) collective-permute-start(f32[8,8,128]{2,1,0:T(8,128)S(1)} %get-tuple-element.79.own.own2), channel_id=1, source_target_pairs={{0,1},{1,0},{2,3},{3,2},{4,5},{5,4},{6,7},{7,6},{8,9},{9,8},{10,11... | collective-permute-start | bytes 98312 | tf_op jit(solution)/shard_map/ppermute | solution.py:931
  50.9 0.0 collective-permute-done.6.other
  50.9 3.4 %coarse.1 = (f32[3,10,3,8,128]{4,3,2,1,0:T(8,128)S(1)}, f32[32,128]{1,0:T(8,128)S(1)}) custom-call(f32[16,2,8,128]{3,2,1,0:T(8,128)S(1)} %get-tuple-element.94.own._, f32[16,2,8,128]{3,2,1,0:T(8,128)S(1)} %collective-permute-done.6.other, f32[128,4096]{1,0:T(8,128)} %inverse_far.1), custom_call_target="tpu_custom_call" | custom-call | bytes 3000000 | tf_op jit(solution)/shard_map/coarse/pallas_call | solution.py:132
  54.2 0.0 collective-permute-done.10.zb
  54.2 0.0 collective-permute-done.9.za
  54.3 0.7 collective-permute-start.12
  55.0 7.3 %collective-permute-start.11 = (f32[14,8,128]{2,1,0:T(8,128)S(1)}, f32[14,8,128]{2,1,0:T(8,128)S(1)}, u32[]{:S(2)}, u32[]{:S(2)}) collective-permute-start(f32[14,8,128]{2,1,0:T(8,128)S(1)} %get-tuple-element.80._), channel_id=1, source_target_pairs={{0,4},{4,0},{8,12},{12,8},{16,20},{20,16},{24,28},{28,24},{1,5},{5... | collective-permute-start | bytes 172040 | tf_op jit(solution)/shard_map/ppermute | solution.py:944
  62.2 9.1 %conditional.3 = (f32[32,128]{1,0:T(8,128)S(1)}) conditional(s32[]{:T(128)} %convert_element_type.2, f32[32,128]{1,0:T(8,128)S(1)} %follow.1, f32[32,128]{1,0:T(8,128)S(1)} %follow.1), branch_computations={%region_2.0_spmd, %region_3.0_spmd} | conditional | bytes 65544 | solution.py:859
  62.2 9.1 %all_to_all.14 = f32[32,1,128]{2,1,0:T(1,128)S(1)} all-to-all(f32[32,1,128]{2,1,0:T(1,128)S(1)} %copy.11), channel_id=1, replica_groups=mesh['gx'=8,'gy'=2,'gc'=2] {'gx','gy','gc'}, dimensions={0} | all-to-all | bytes 32768 | tf_op jit(solution)/shard_map/cond/branch_1_fun/all_to_all | solution.py:859
  71.4 0.0 collective-permute-done.12.sides_b
  71.4 0.0 collective-permute-done.11.sides_a
  71.4 0.0 collective-permute-done.13.later_a
  71.4 0.0 collective-permute-done.14.later_b
  71.4 7.4 %up.1 = (f32[16,128,128]{2,1,0:T(8,128)}, f32[16,128,128]{2,1,0:T(8,128)}) custom-call(f32[32,128]{1,0:T(8,128)S(1)} %get-tuple-element.95.e, f32[3,10,3,8,128]{4,3,2,1,0:T(8,128)S(1)} %get-tuple-element.81.window3, f32[8,8,128]{2,1,0:T(8,128)S(1)} %get-tuple-element.79.own.own2, f32[8,8,128]{2,1,0:T(8,128)S(1)} %collective-permute-done.9.za, ...), custom_call_target="tpu_custom_call" | custom-call | bytes 3000000 | tf_op jit(solution)/shard_map/up/pallas_call | solution.py:132
  (4 shorter events, 0.0 us)
Async XLA Ops:
  0.6 7.3 %copy-start = (f32[16,128,128]{2,1,0:T(8,128)S(1)}, f32[16,128,128]{2,1,0:T(8,128)}, u32[]{:S(2)}) copy-start(f32[16,128,128]{2,1,0:T(8,128)} %v_in.1) | copy-start | bytes 3145732
  2.9 6.8 %collective-permute-start.1 = (f32[2,16,16,128]{3,2,1,0:T(8,128)S(1)}, f32[2,16,16,128]{3,2,1,0:T(8,128)S(1)}, u32[]{:S(2)}, u32[]{:S(2)}) collective-permute-start(f32[2,16,16,128]{3,2,1,0:T(8,128)S(1)} %get-tuple-element.57), channel_id=1, source_target_pairs={{1,2},{2,1},{5,6},{6,5},{9,10},{10,9},{13,14},{14,13},{17,18},{18,... | collective-permute-start | bytes 786440 | tf_op jit(solution)/shard_map/ppermute | solution.py:880
  3.5 6.2 %collective-permute-start = (f32[2,16,16,128]{3,2,1,0:T(8,128)S(1)}, f32[2,16,16,128]{3,2,1,0:T(8,128)S(1)}, u32[]{:S(2)}, u32[]{:S(2)}) collective-permute-start(f32[2,16,16,128]{3,2,1,0:T(8,128)S(1)} %get-tuple-element.54._), channel_id=1, source_target_pairs={{0,1},{1,0},{2,3},{3,2},{4,5},{5,4},{6,7},{7,6},{8,9},{9,8},{10,11... | collective-permute-start | bytes 786440 | tf_op jit(solution)/shard_map/ppermute | solution.py:879
  8.3 1.4 %collective-permute-start.2 = (f32[16,16,128]{2,1,0:T(8,128)S(1)}, f32[16,16,128]{2,1,0:T(8,128)S(1)}, u32[]{:S(2)}, u32[]{:S(2)}) collective-permute-start(f32[16,16,128]{2,1,0:T(8,128)S(1)} %get-tuple-element.58), channel_id=1, source_target_pairs={{0,1},{1,0},{2,3},{3,2},{4,5},{5,4},{6,7},{7,6},{8,9},{9,8},{10,11... | collective-permute-start | bytes 393224 | tf_op jit(solution)/shard_map/ppermute | solution.py:882
  8.4 1.3 %collective-permute-start.3 = (f32[16,16,128]{2,1,0:T(8,128)S(1)}, f32[16,16,128]{2,1,0:T(8,128)S(1)}, u32[]{:S(2)}, u32[]{:S(2)}) collective-permute-start(f32[16,16,128]{2,1,0:T(8,128)S(1)} %get-tuple-element.59), channel_id=1, source_target_pairs={{1,2},{2,1},{5,6},{6,5},{9,10},{10,9},{13,14},{14,13},{17,18},{18,... | collective-permute-start | bytes 393224 | tf_op jit(solution)/shard_map/ppermute | solution.py:883
  10.5 6.1 %collective-permute-start.4 = (f32[448,128]{1,0:T(8,128)S(1)}, f32[448,128]{1,0:T(8,128)S(1)}, u32[]{:S(2)}, u32[]{:S(2)}) collective-permute-start(f32[448,128]{1,0:T(8,128)S(1)} %get-tuple-element.68), channel_id=1, source_target_pairs={{0,4},{4,0},{8,12},{12,8},{16,20},{20,16},{24,28},{28,24},{1,5},{5... | collective-permute-start | bytes 688136 | tf_op jit(solution)/shard_map/ppermute | solution.py:890
  12.1 4.5 %collective-permute-start.5 = (f32[448,128]{1,0:T(8,128)S(1)}, f32[448,128]{1,0:T(8,128)S(1)}, u32[]{:S(2)}, u32[]{:S(2)}) collective-permute-start(f32[448,128]{1,0:T(8,128)S(1)} %get-tuple-element.69), channel_id=1, source_target_pairs={{4,8},{8,4},{12,16},{16,12},{20,24},{24,20},{5,9},{9,5},{13,17},{1... | collective-permute-start | bytes 688136 | tf_op jit(solution)/shard_map/ppermute | solution.py:891
  21.1 25.5 %collective-permute-start.7 = (f32[312,128]{1,0:T(8,128)S(1)}, f32[312,128]{1,0:T(8,128)S(1)}, u32[]{:S(2)}, u32[]{:S(2)}) collective-permute-start(f32[312,128]{1,0:T(8,128)S(1)} %get-tuple-element.73), channel_id=1, source_target_pairs={{0,4},{4,0},{8,12},{12,8},{16,20},{20,16},{24,28},{28,24},{1,5},{5... | collective-permute-start | bytes 479240 | tf_op jit(solution)/shard_map/ppermute | solution.py:921
  26.0 20.6 %collective-permute-start.8 = (f32[312,128]{1,0:T(8,128)S(1)}, f32[312,128]{1,0:T(8,128)S(1)}, u32[]{:S(2)}, u32[]{:S(2)}) collective-permute-start(f32[312,128]{1,0:T(8,128)S(1)} %get-tuple-element.74), channel_id=1, source_target_pairs={{4,8},{8,4},{12,16},{16,12},{20,24},{24,20},{5,9},{9,5},{13,17},{1... | collective-permute-start | bytes 479240 | tf_op jit(solution)/shard_map/ppermute | solution.py:922
  46.6 24.7 %collective-permute-start.13 = (f32[744,128]{1,0:T(8,128)S(1)}, f32[744,128]{1,0:T(8,128)S(1)}, u32[]{:S(2)}, u32[]{:S(2)}) collective-permute-start(f32[744,128]{1,0:T(8,128)S(1)} %get-tuple-element.92), channel_id=1, source_target_pairs={{0,4},{4,0},{8,12},{12,8},{16,20},{20,16},{24,28},{28,24},{1,5},{5... | collective-permute-start | bytes 1142792 | tf_op jit(solution)/shard_map/ppermute | solution.py:928
  47.5 23.9 %collective-permute-start.14 = (f32[744,128]{1,0:T(8,128)S(1)}, f32[744,128]{1,0:T(8,128)S(1)}, u32[]{:S(2)}, u32[]{:S(2)}) collective-permute-start(f32[744,128]{1,0:T(8,128)S(1)} %get-tuple-element.93), channel_id=1, source_target_pairs={{4,8},{8,4},{12,16},{16,12},{20,24},{24,20},{5,9},{9,5},{13,17},{1... | collective-permute-start | bytes 1142792 | tf_op jit(solution)/shard_map/ppermute | solution.py:929
  48.1 2.7 %collective-permute-start.6 = (f32[16,2,8,128]{3,2,1,0:T(8,128)S(1)}, f32[16,2,8,128]{3,2,1,0:T(8,128)S(1)}, u32[]{:S(2)}, u32[]{:S(2)}) collective-permute-start(f32[16,2,8,128]{3,2,1,0:T(8,128)S(1)} %get-tuple-element.94.own._), channel_id=1, source_target_pairs={{0,1},{1,0},{2,3},{3,2},{4,5},{5,4},{6,7},{7,6},{8,9},{9,8},{10,11... | collective-permute-start | bytes 393224 | tf_op jit(solution)/shard_map/ppermute | solution.py:930
  48.2 6.0 %collective-permute-start.10 = (f32[8,8,128]{2,1,0:T(8,128)S(1)}, f32[8,8,128]{2,1,0:T(8,128)S(1)}, u32[]{:S(2)}, u32[]{:S(2)}) collective-permute-start(f32[8,8,128]{2,1,0:T(8,128)S(1)} %get-tuple-element.79.own.own2), channel_id=1, source_target_pairs={{1,2},{2,1},{5,6},{6,5},{9,10},{10,9},{13,14},{14,13},{17,18},{18,... | collective-permute-start | bytes 98312 | tf_op jit(solution)/shard_map/ppermute | solution.py:932
  48.9 5.4 %collective-permute-start.9 = (f32[8,8,128]{2,1,0:T(8,128)S(1)}, f32[8,8,128]{2,1,0:T(8,128)S(1)}, u32[]{:S(2)}, u32[]{:S(2)}) collective-permute-start(f32[8,8,128]{2,1,0:T(8,128)S(1)} %get-tuple-element.79.own.own2), channel_id=1, source_target_pairs={{0,1},{1,0},{2,3},{3,2},{4,5},{5,4},{6,7},{7,6},{8,9},{9,8},{10,11... | collective-permute-start | bytes 98312 | tf_op jit(solution)/shard_map/ppermute | solution.py:931
  54.3 17.1 %collective-permute-start.12 = (f32[14,8,128]{2,1,0:T(8,128)S(1)}, f32[14,8,128]{2,1,0:T(8,128)S(1)}, u32[]{:S(2)}, u32[]{:S(2)}) collective-permute-start(f32[14,8,128]{2,1,0:T(8,128)S(1)} %get-tuple-element.82), channel_id=1, source_target_pairs={{4,8},{8,4},{12,16},{16,12},{20,24},{24,20},{5,9},{9,5},{13,17},{1... | collective-permute-start | bytes 172040 | tf_op jit(solution)/shard_map/ppermute | solution.py:945
  55.0 16.4 %collective-permute-start.11 = (f32[14,8,128]{2,1,0:T(8,128)S(1)}, f32[14,8,128]{2,1,0:T(8,128)S(1)}, u32[]{:S(2)}, u32[]{:S(2)}) collective-permute-start(f32[14,8,128]{2,1,0:T(8,128)S(1)} %get-tuple-element.80._), channel_id=1, source_target_pairs={{0,4},{4,0},{8,12},{12,8},{16,20},{20,16},{24,28},{28,24},{1,5},{5... | collective-permute-start | bytes 172040 | tf_op jit(solution)/shard_map/ppermute | solution.py:944
